TPU v7x, 32 devices: a whole 2x2x4 slice. The times are simulated.
32 devices in a mesh: freq: 4 (over z), row: 8 (over y, x, core).
Axes of the slice: x: 2, y: 2, z: 4, core: 2. Of those that a mesh axis runs over, the one named last changes fastest.
Arguments:
- source_field: float32 [4, 2, 2048, 2048], P('freq', None, 'row'), may hold values from -6 to 6
- receiver_field: float32 [4, 2, 2048, 2048], P('freq', None, 'row'), may hold values from -6 to 6
- slowness_store: float32 [4, 2048, 2048], P('freq', 'row'), may hold values from -0.08 to 0.08
- store_pos: int32 [4], replicated, may hold values from 0 to 3, each once
- freq_index: int32 [4], P('freq'), may hold values from 24 to 64
Outputs:
- image: float32 [2, 2048, 2048], P(None, 'row')
- source_out: float32 [4, 2, 2048, 2048], P('freq', None, 'row')
- receiver_out: float32 [4, 2, 2048, 2048], P('freq', None, 'row')
Inputs may be any that keep to these rules, and one draw needn't show every extreme that they name: `store_pos`: entries are distinct.
All inputs are finite; a program needn't handle non-finite values.
Results may differ from a plain program's by a relative error of at most 0.0003.
Values sent between devices are 32-bit elements; how exact they have to be, the bound alone decides.
No kernel may reach another device: no remote copies, remote signals or barrier semaphores. Data moves between devices by JAX's collectives and lax.ppermute only.
A program may use at most 128 MiB of HBM per device.

v0:
```python
import jax
import jax.numpy as jnp
from jax import lax
from jax.sharding import PartitionSpec as P

DEPTHS = 2


depth_step = 16.0
omega_unit = 0.045
radix_size = 128


def from_root(value, axis, source):
    kept = jnp.where(lax.axis_index(axis) == source, value, 0).astype(value.dtype)
    return lax.psum(kept, axis)


def angle_table(rows, cols, period, orient):
    product = lax.broadcasted_iota(jnp.int32, (rows, cols), 0) * lax.broadcasted_iota(
        jnp.int32, (rows, cols), 1
    )
    angles = 2.0 * jnp.pi / period * (product % period).astype(jnp.float32)
    return (jnp.cos(angles), orient * jnp.sin(angles))


def block_table(rows, cols, period, orient):
    table_real, table_imag = angle_table(rows, cols, period, orient)
    upper = jnp.stack([table_real, table_imag], axis=1)
    lower = jnp.stack([-table_imag, table_real], axis=1)
    return jnp.stack([upper, lower], axis=0)


def twiddled(stacked, twid_real, twid_imag):
    real_part = stacked[:, 0]
    imaginary = stacked[:, 1]
    return jnp.stack(
        [
            real_part * twid_real - imaginary * twid_imag,
            real_part * twid_imag + imaginary * twid_real,
        ],
        axis=1,
    )


def transform(field, orient, along_last):
    highest = lax.Precision.HIGHEST
    freqs, comps, rows, cols = field.shape
    if along_last:
        length = cols
        outer_size = length // radix_size
        shaped = field.reshape(freqs, comps, rows, outer_size, radix_size)
        first_form = "fpyab,paqc->fqycb"
        second_form = "fqycb,qbsd->fsydc"
        twiddle_shape = (outer_size, radix_size)
    else:
        length = rows
        outer_size = length // radix_size
        shaped = field.reshape(freqs, comps, outer_size, radix_size, cols)
        first_form = "fpaby,paqc->fqcby"
        second_form = "fqcby,qbsd->fsdcy"
        twiddle_shape = (outer_size, radix_size, 1)
    first_table = block_table(outer_size, outer_size, outer_size, orient)
    twid_real, twid_imag = angle_table(outer_size, radix_size, length, orient)
    twid_real = twid_real.reshape(twiddle_shape)
    twid_imag = twid_imag.reshape(twiddle_shape)
    last_table = block_table(radix_size, radix_size, radix_size, orient)
    section = jnp.einsum(first_form, shaped, first_table, precision=highest)
    turned = twiddled(section, twid_real, twid_imag)
    final = jnp.einsum(second_form, turned, last_table, precision=highest)
    return final.reshape(field.shape)


def wavenumber(index, length):
    signed = jnp.where(index < length // 2, index, index - length)
    return 2.0 * jnp.pi * (signed.astype(jnp.float32) / length)


def rotate(field, cos_part, sin_part):
    real_part = field[:, 0]
    imaginary = field[:, 1]
    return jnp.stack(
        [real_part * cos_part - imaginary * sin_part, real_part * sin_part + imaginary * cos_part],
        axis=1,
    )


def forward_one(field):
    first = transform(field, -1.0, True)
    moved = lax.all_to_all(first, "row", split_axis=3, concat_axis=2, tiled=True)
    return transform(moved, -1.0, False)


def inverse_one(field):
    first = transform(field, 1.0, False)
    moved = lax.all_to_all(first, "row", split_axis=2, concat_axis=3, tiled=True)
    return transform(moved, 1.0, True)


def on_device(source_field, receiver_field, slowness_store, store_pos, freq_index):
    omegas = omega_unit * freq_index.astype(jnp.float32)
    rows_local = source_field.shape[2]
    cols_total = source_field.shape[3]
    rows_total = rows_local * lax.axis_size("row")
    col_block = cols_total // lax.axis_size("row")
    kx_index = lax.broadcasted_iota(jnp.int32, (rows_total, col_block), 0)
    ky_index = (
        lax.broadcasted_iota(jnp.int32, (rows_total, col_block), 1)
        + lax.axis_index("row") * col_block
    )
    kx_values = wavenumber(kx_index, rows_total)
    ky_values = wavenumber(ky_index, cols_total)
    phase_q = (
        omegas[:, None, None] * omegas[:, None, None]
        - (kx_values * kx_values + ky_values * ky_values)[None]
    )
    travel = jnp.sqrt(jnp.maximum(phase_q, 0.0))
    decay = jnp.sqrt(jnp.maximum(-phase_q, 0.0))
    damping = jnp.exp(-depth_step * decay) / (rows_total * cols_total)
    mult_real = damping * jnp.cos(depth_step * travel)
    mult_imag = damping * jnp.sin(depth_step * travel)
    source_now = source_field
    receiver_now = receiver_field
    image_terms = []
    for depth_index in range(DEPTHS):
        slowness = from_root(slowness_store[0], "freq", store_pos[depth_index])
        spec_source = rotate(forward_one(source_now), mult_real, -mult_imag)
        source_now = inverse_one(spec_source)
        spec_receiver = rotate(forward_one(receiver_now), mult_real, mult_imag)
        receiver_now = inverse_one(spec_receiver)
        angles = depth_step * omegas[:, None, None] * slowness[None]
        lens_cos = jnp.cos(angles)
        lens_sin = jnp.sin(angles)
        source_now = rotate(source_now, lens_cos, -lens_sin)
        receiver_now = rotate(receiver_now, lens_cos, lens_sin)
        local_term = jnp.sum(source_now * receiver_now, axis=(0, 1))
        image_terms.append(lax.psum(local_term, "freq"))
    image = jnp.stack(image_terms)
    return (image, source_now, receiver_now)


def solution(mesh):
    placed = (
        P("freq", None, "row", None),
        P("freq", None, "row", None),
        P("freq", "row", None),
        P(),
        P("freq"),
    )
    return jax.shard_map(
        on_device,
        mesh=mesh,
        in_specs=placed,
        out_specs=(
            P(None, "row", None),
            P("freq", None, "row", None),
            P("freq", None, "row", None),
        ),
        check_vma=False,
    )
```

profile of v0, /device:TPU:0, one launch (start us, length us, event | category | flops | bytes accessed | tf_op | source)
XLA Modules:
  0.0 1037.4 jit_solution(3174717837657168840)
XLA Ops:
  30.4 12.2 %copy.227 = f32[1,2,256,2048]{2,1,0,3:T(2,128)} copy(f32[1,2,256,2048]{2,3,1,0:T(8,128)S(1)} %bitcast.603) | data formatting | bytes 8388608 | tf_op jit(solution)/shard_map/reshape | solution.py:71
  57.2 12.2 %copy.253 = f32[1,2,256,2048]{2,1,0,3:T(2,128)} copy(f32[1,2,256,2048]{2,3,1,0:T(8,128)S(1)} %bitcast.604) | data formatting | bytes 8388608 | tf_op jit(solution)/shard_map/reshape | solution.py:71
  69.4 28.0 %all-to-all-done = f32[1,2,256,2048]{2,1,0,3:T(2,128)} async-done(((f32[1,2,256,2048]{2,1,0,3:T(2,128)}), f32[1,2,256,2048]{2,1,0,3:T(2,128)}, u32[]{:S(2)}, u32[]{:S(2)}) %all-to-all-start) | async-done | bytes 4194336 | tf_op jit(solution)/shard_map/all_to_all | solution.py:90
  113.2 10.0 fusion.91
  123.2 28.1 %all-to-all-done.2 = f32[1,2,256,2048]{2,1,0,3:T(2,128)} async-done(((f32[1,2,256,2048]{2,1,0,3:T(2,128)}), f32[1,2,256,2048]{2,1,0,3:T(2,128)}, u32[]{:S(2)}, u32[]{:S(2)}) %all-to-all-start.2) | async-done | bytes 4194336 | tf_op jit(solution)/shard_map/all_to_all | solution.py:90
  161.2 8.4 fusion.109
  171.6 5.9 fusion.94
  180.4 6.3 fusion.112
  189.2 12.3 %multiply_subtract_fusion.19 = (f32[1,1,2048,256]{3,2,1,0:T(8,128)S(1)}, f32[1,1,2048,256]{3,2,1,0:T(8,128)S(1)}, f32[1,1,2048,256]{3,2,1,0:T(8,128)S(1)}, f32[1,1,2048,256]{3,2,1,0:T(8,128)S(1)}) fusion(f32[1,2,2048,256]{3,2,1,0:T(8,128)S(1)} %bitcast.597, s32[256]{0:T(256)S(1)} %get-tuple-element.114, s32[256]{0:T(256)S(1)} %get-tuple-element.113, ...), kind=kLoop, calls=%fused_computation.197 | loop fusion | flops 16252928 | bytes 16789764 | tf_op jit(solution)/shard_map/sub | solution.py:83
  225.1 12.2 %copy.242 = f32[1,2,2048,256]{3,1,0,2:T(2,128)} copy(f32[1,2,2048,256]{3,2,1,0:T(8,128)S(1)} %bitcast.609) | data formatting | bytes 8388608 | tf_op jit(solution)/shard_map/reshape;fqcby,qbsd->fsdcy/transpose | solution.py:71
  252.4 12.2 %copy.265 = f32[1,2,2048,256]{3,1,0,2:T(2,128)} copy(f32[1,2,2048,256]{3,2,1,0:T(8,128)S(1)} %bitcast.610) | data formatting | bytes 8388608 | tf_op jit(solution)/shard_map/reshape;fqcby,qbsd->fsdcy/transpose | solution.py:71
  264.6 26.6 %all-to-all-done.1 = f32[1,2,2048,256]{3,1,0,2:T(2,128)} async-done(((f32[1,2,2048,256]{3,1,0,2:T(2,128)}), f32[1,2,2048,256]{3,1,0,2:T(2,128)}, u32[]{:S(2)}, u32[]{:S(2)}) %all-to-all-start.1) | async-done | bytes 4194336 | tf_op jit(solution)/shard_map/all_to_all | solution.py:96
  314.2 30.9 %all-to-all-done.3 = f32[1,2,2048,256]{3,1,0,2:T(2,128)} async-done(((f32[1,2,2048,256]{3,1,0,2:T(2,128)}), f32[1,2,2048,256]{3,1,0,2:T(2,128)}, u32[]{:S(2)}, u32[]{:S(2)}) %all-to-all-start.3) | async-done | bytes 4194336 | tf_op jit(solution)/shard_map/all_to_all | solution.py:96
  356.8 6.0 convolution_bitcast_fusion.3
  386.6 73.4 %all-reduce.7.cloned.1.call-done = (f32[256,2048]{0,1:T(8,128)}, f32[256,2048]{0,1:T(8,128)}) async-done(((f32[256,2048]{0,1:T(8,128)}, f32[256,2048]{0,1:T(8,128)}), (f32[256,2048]{0,1:T(8,128)}, f32[256,2048]{0,1:T(8,128)})) %all-reduce.7.cloned.1.call-update) | async-done | bytes 4194320 | tf_op jit(solution)/shard_map/psum | solution.py:16
  460.0 14.1 %multiply_subtract_fusion.16 = (f32[256,2048]{0,1:T(8,128)S(1)}, f32[256,2048]{0,1:T(8,128)}, f32[256,2048]{0,1:T(8,128)}, f32[256,2048]{0,1:T(8,128)}) fusion(f32[1,2,256,2048]{2,3,1,0:T(8,128)} %bitcast.622, f32[256,2048]{0,1:T(8,128)} %get-tuple-element.14, f32[]{:T(128)} %bitcast.72, f32[1,2,256,2048]{2,3,1,0:T(8,128)} %bitcast.624), kind=kLoop, calls=%fused_computation.190 | loop fusion | flops 7340032 | bytes 18874372 | tf_op jit(solution)/shard_map/sub | solution.py:83
  485.2 5.9 fusion.152
  505.6 12.2 %copy.276 = f32[1,2,256,2048]{2,1,0,3:T(2,128)} copy(f32[1,2,256,2048]{2,3,1,0:T(8,128)S(1)} %bitcast.613) | data formatting | bytes 8388608 | tf_op jit(solution)/shard_map/reshape | solution.py:71
  532.0 12.2 %copy.300 = f32[1,2,256,2048]{2,1,0,3:T(2,128)} copy(f32[1,2,256,2048]{2,3,1,0:T(8,128)S(1)} %bitcast.614) | data formatting | bytes 8388608 | tf_op jit(solution)/shard_map/reshape | solution.py:71
  544.2 27.3 %all-to-all-done.4 = f32[1,2,256,2048]{2,1,0,3:T(2,128)} async-done(((f32[1,2,256,2048]{2,1,0,3:T(2,128)}), f32[1,2,256,2048]{2,1,0,3:T(2,128)}, u32[]{:S(2)}, u32[]{:S(2)}) %all-to-all-start.4) | async-done | bytes 4194336 | tf_op jit(solution)/shard_map/all_to_all | solution.py:90
  586.4 10.0 fusion.124
  596.4 29.2 %all-to-all-done.6 = f32[1,2,256,2048]{2,1,0,3:T(2,128)} async-done(((f32[1,2,256,2048]{2,1,0,3:T(2,128)}), f32[1,2,256,2048]{2,1,0,3:T(2,128)}, u32[]{:S(2)}, u32[]{:S(2)}) %all-to-all-start.6) | async-done | bytes 4194336 | tf_op jit(solution)/shard_map/all_to_all | solution.py:90
  635.5 8.4 fusion.139
  654.7 6.1 fusion.142
  663.3 12.5 %multiply_subtract_fusion.7 = (f32[1,1,2048,256]{3,2,1,0:T(8,128)S(1)}, f32[1,1,2048,256]{3,2,1,0:T(8,128)S(1)}, f32[1,1,2048,256]{3,2,1,0:T(8,128)S(1)}, f32[1,1,2048,256]{3,2,1,0:T(8,128)S(1)}) fusion(f32[1,2,2048,256]{3,2,1,0:T(8,128)S(1)} %bitcast.596, s32[256]{0:T(256)S(1)} %copy-done.21, s32[256]{0:T(256)S(1)} %copy-done.19, ...), kind=kLoop, calls=%fused_computation.172 | loop fusion | flops 16252928 | bytes 16789764 | tf_op jit(solution)/shard_map/sub | solution.py:83
  699.8 12.2 %copy.288 = f32[1,2,2048,256]{3,1,0,2:T(2,128)} copy(f32[1,2,2048,256]{3,2,1,0:T(8,128)S(1)} %bitcast.618) | data formatting | bytes 8388608 | tf_op jit(solution)/shard_map/reshape;fqcby,qbsd->fsdcy/transpose | solution.py:71
  727.9 12.2 %copy.312 = f32[1,2,2048,256]{3,1,0,2:T(2,128)} copy(f32[1,2,2048,256]{3,2,1,0:T(8,128)S(1)} %bitcast.619) | data formatting | bytes 8388608 | tf_op jit(solution)/shard_map/reshape;fqcby,qbsd->fsdcy/transpose | solution.py:71
  740.1 25.9 %all-to-all-done.5 = f32[1,2,2048,256]{3,1,0,2:T(2,128)} async-done(((f32[1,2,2048,256]{3,1,0,2:T(2,128)}), f32[1,2,2048,256]{3,1,0,2:T(2,128)}, u32[]{:S(2)}, u32[]{:S(2)}) %all-to-all-start.5) | async-done | bytes 4194336 | tf_op jit(solution)/shard_map/all_to_all | solution.py:96
  787.6 7.9 convolution_bitcast_fusion.1
  795.5 24.5 %all-to-all-done.7 = f32[1,2,2048,256]{3,1,0,2:T(2,128)} async-done(((f32[1,2,2048,256]{3,1,0,2:T(2,128)}), f32[1,2,2048,256]{3,1,0,2:T(2,128)}, u32[]{:S(2)}, u32[]{:S(2)}) %all-to-all-start.7) | async-done | bytes 4194336 | tf_op jit(solution)/shard_map/all_to_all | solution.py:96
  853.4 8.3 subtract_bitcast_fusion.1
  878.4 141.9 %all-reduce.5.cloned.1.call-done = (f32[1,256,2048]{1,2,0:T(8,128)}, f32[1,256,2048]{1,2,0:T(8,128)}) async-done(((f32[1,256,2048]{1,2,0:T(8,128)}, f32[1,256,2048]{1,2,0:T(8,128)}), (f32[1,256,2048]{1,2,0:T(8,128)}, f32[1,256,2048]{1,2,0:T(8,128)})) %all-reduce.5.cloned.1.call-update) | async-done | bytes 4194320 | tf_op jit(solution)/shard_map/psum | solution.py:137
  (184 shorter events, 364.3 us)
Async XLA Ops:
  8.2 3.5 copy-start.6
  42.6 54.8 %all-to-all-start = ((f32[1,2,256,2048]{2,1,0,3:T(2,128)}), f32[1,2,256,2048]{2,1,0,3:T(2,128)}, u32[]{:S(2)}, u32[]{:S(2)}) async-start(f32[1,2,256,2048]{2,1,0,3:T(2,128)} %copy.227), calls=%async_computation | async-start | bytes 8388608 | tf_op jit(solution)/shard_map/all_to_all | solution.py:90
  97.4 53.9 %all-to-all-start.2 = ((f32[1,2,256,2048]{2,1,0,3:T(2,128)}), f32[1,2,256,2048]{2,1,0,3:T(2,128)}, u32[]{:S(2)}, u32[]{:S(2)}) async-start(f32[1,2,256,2048]{2,1,0,3:T(2,128)} %copy.253), calls=%async_computation.2 | async-start | bytes 8388608 | tf_op jit(solution)/shard_map/all_to_all | solution.py:90
  102.3 67.2 %copy-start.10 = (f32[16,128]{0,1:T(8,128)}, f32[16,128]{0,1:T(8,128)S(1)}, u32[]{:S(2)}) copy-start(f32[16,128]{0,1:T(8,128)S(1)} %copy.232) | copy-start | bytes 24580
  103.1 263.7 %copy-start.12 = (f32[16,128]{1,0:T(8,128)}, f32[16,128]{1,0:T(8,128)S(1)}, u32[]{:S(2)}) copy-start(f32[16,128]{1,0:T(8,128)S(1)} %fusion.203) | copy-start | bytes 24580
  103.2 111.1 %copy-start.8 = (f32[16,128]{0,1:T(8,128)}, f32[16,128]{0,1:T(8,128)S(1)}, u32[]{:S(2)}) copy-start(f32[16,128]{0,1:T(8,128)S(1)} %copy.238) | copy-start | bytes 24580
  103.2 85.9 %copy-start.22 = (pred[256]{0:T(512)(128)(4,1)}, pred[256]{0:T(512)(128)(4,1)S(1)}, u32[]{:S(2)}) copy-start(pred[256]{0:T(512)(128)(4,1)S(1)} %fusion.210) | copy-start | bytes 772
  103.2 85.9 %copy-start.18 = (s32[256]{0:T(256)}, s32[256]{0:T(256)S(1)}, u32[]{:S(2)}) copy-start(s32[256]{0:T(256)S(1)} %get-tuple-element.113) | copy-start | bytes 3076
  103.2 85.9 %copy-start.20 = (s32[256]{0:T(256)}, s32[256]{0:T(256)S(1)}, u32[]{:S(2)}) copy-start(s32[256]{0:T(256)S(1)} %get-tuple-element.114) | copy-start | bytes 3076
  103.3 85.9 %copy-start.16 = (pred[2048]{0:T(1024)(128)(4,1)}, pred[2048]{0:T(1024)(128)(4,1)S(1)}, u32[]{:S(2)}) copy-start(pred[2048]{0:T(1024)(128)(4,1)S(1)} %iota_compare_fusion) | copy-start | bytes 6148
  103.3 85.9 %copy-start.14 = (s32[2048]{0:T(1024)}, s32[2048]{0:T(1024)S(1)}, u32[]{:S(2)}) copy-start(s32[2048]{0:T(1024)S(1)} %iota_add_fusion) | copy-start | bytes 24580
  161.2 8.4 copy-start.3
  237.3 53.9 %all-to-all-start.1 = ((f32[1,2,2048,256]{3,1,0,2:T(2,128)}), f32[1,2,2048,256]{3,1,0,2:T(2,128)}, u32[]{:S(2)}, u32[]{:S(2)}) async-start(f32[1,2,2048,256]{3,1,0,2:T(2,128)} %copy.242), calls=%async_computation.1 | async-start | bytes 8388608 | tf_op jit(solution)/shard_map/all_to_all | solution.py:96
  264.6 31.4 %copy-start.24 = (s32[4]{0:T(128)S(1)}, s32[4]{0:T(128)}, u32[]{:S(2)}) copy-start(s32[4]{0:T(128)} %param.8) | copy-start | bytes 52
  291.2 53.9 %all-to-all-start.3 = ((f32[1,2,2048,256]{3,1,0,2:T(2,128)}), f32[1,2,2048,256]{3,1,0,2:T(2,128)}, u32[]{:S(2)}, u32[]{:S(2)}) async-start(f32[1,2,2048,256]{3,1,0,2:T(2,128)} %copy.265), calls=%async_computation.3 | async-start | bytes 8388608 | tf_op jit(solution)/shard_map/all_to_all | solution.py:96
  296.0 164.0 %all-reduce.7.cloned.1.call-start = ((), (), s32[]{:S(2)}) async-start(), calls=%async_computation.9 | async-start | bytes 8388608 | tf_op jit(solution)/shard_map/psum | solution.py:16
  356.8 6.0 copy-start.1
  485.2 5.9 copy-start.4
  485.2 6.0 copy-start.5
  517.8 53.7 %all-to-all-start.4 = ((f32[1,2,256,2048]{2,1,0,3:T(2,128)}), f32[1,2,256,2048]{2,1,0,3:T(2,128)}, u32[]{:S(2)}, u32[]{:S(2)}) async-start(f32[1,2,256,2048]{2,1,0,3:T(2,128)} %copy.276), calls=%async_computation.4 | async-start | bytes 8388608 | tf_op jit(solution)/shard_map/all_to_all | solution.py:90
  571.5 54.1 %all-to-all-start.6 = ((f32[1,2,256,2048]{2,1,0,3:T(2,128)}), f32[1,2,256,2048]{2,1,0,3:T(2,128)}, u32[]{:S(2)}, u32[]{:S(2)}) async-start(f32[1,2,256,2048]{2,1,0,3:T(2,128)} %copy.300), calls=%async_computation.6 | async-start | bytes 8388608 | tf_op jit(solution)/shard_map/all_to_all | solution.py:90
  635.5 8.4 copy-start.2
  635.5 8.4 copy-start.11
  660.8 2.5 copy-start.15
  660.8 2.5 copy-start.17
  660.8 2.5 copy-start.19
  684.5 4.0 copy-start.9
  712.0 54.1 %all-to-all-start.5 = ((f32[1,2,2048,256]{3,1,0,2:T(2,128)}), f32[1,2,2048,256]{3,1,0,2:T(2,128)}, u32[]{:S(2)}, u32[]{:S(2)}) async-start(f32[1,2,2048,256]{3,1,0,2:T(2,128)} %copy.288), calls=%async_computation.5 | async-start | bytes 8388608 | tf_op jit(solution)/shard_map/all_to_all | solution.py:96
  766.1 53.9 %all-to-all-start.7 = ((f32[1,2,2048,256]{3,1,0,2:T(2,128)}), f32[1,2,2048,256]{3,1,0,2:T(2,128)}, u32[]{:S(2)}, u32[]{:S(2)}) async-start(f32[1,2,2048,256]{3,1,0,2:T(2,128)} %copy.312), calls=%async_computation.7 | async-start | bytes 8388608 | tf_op jit(solution)/shard_map/all_to_all | solution.py:96
  770.8 249.5 %all-reduce.5.cloned.1.call-start = ((), (), s32[]{:S(2)}) async-start(), calls=%async_computation.8 | async-start | bytes 8388608 | tf_op jit(solution)/shard_map/psum | solution.py:137
  831.6 5.8 copy-start
  831.6 5.8 copy-start.13
  (3 other events, 7.4 us)
Sparse Core Ops, SparseCore 0:
  302.3 157.6 all-reduce.6
  867.7 152.5 all-reduce.4
where the time goes:
time: 1050 us; the launch traced here: 1040 us
  waiting for transfers between devices  436 us (42%)
  local copies, waits for them, and re-layouts  272 us (26%)
  matrix products  179 us (17%)
  other arithmetic  94.1 us (9%)
  starting transfers between devices  39.2 us (4%)
  between operations  17.5 us (2%)
    psum x1, waiting for transfers between devices, on_device(): image_terms.append(lax.psum(local_term, 'freq'))  142 us
    all_to_all x4, waiting for transfers between devices, forward_one(): lax.all_to_all(first, 'row', split_axis=3, concat_axis=2, tiled=True)  113 us
    all_to_all x4, waiting for transfers between devices, inverse_one(): lax.all_to_all(first, 'row', split_axis=2, concat_axis=3, tiled=True)  108 us
    dot_general x16, matrix products, transform(): section = jnp.einsum(first_form, shaped, first_table, precision=highest)  93.8 us
    dot_general x16, matrix products, transform(): final = jnp.einsum(second_form, turned, last_table, precision=highest)  85.5 us
    psum x1, waiting for transfers between devices, from_root(): return lax.psum(kept, axis)  73.4 us
    reshape x4, local copies, waits for them, and re-layouts, transform(): return final.reshape(field.shape)  48.8 us
    transpose x4, local copies, waits for them, and re-layouts, transform(): return final.reshape(field.shape)  48.8 us
  transfers between devices with their start and end apart: 10, of which 10 were waited for; matrix products, arithmetic and copies ran while one was open for 21% of the time, Pallas kernels for 0%

commit v1 on v0

v1 whole, which is shorter than its diff:
```python
import functools

import jax
import jax.numpy as jnp
import numpy as np
from jax import lax
from jax.experimental import pallas as pl
from jax.experimental.pallas import tpu as pltpu
from jax.sharding import PartitionSpec as P

DEPTHS = 2


depth_step = 16.0
omega_unit = 0.045
lanes = 128
digits = 16
sub = 8
vmem_bytes = 60 * 1024 * 1024


def split_pair(table):
    high = table.astype(jnp.bfloat16)
    low = (table - high.astype(np.float64)).astype(jnp.bfloat16)
    return high, low


@functools.lru_cache(None)
def right_table(orient):
    index = np.arange(lanes)
    angle = orient * 2.0 * np.pi * (np.outer(index, index) % lanes) / lanes
    c, s = np.cos(angle), np.sin(angle)
    high, low = split_pair(np.block([[c, s], [-s, c]]))
    return np.concatenate([high, high, low], axis=0)


@functools.lru_cache(None)
def twiddle_table(length, orient):
    turns = np.outer(np.arange(digits), np.arange(lanes)) % length
    angle = orient * 2.0 * np.pi * turns / length
    return np.stack([np.cos(angle), np.sin(angle)]).astype(np.float32)


@functools.lru_cache(None)
def left_table(length, orient):
    index = np.arange(lanes)
    digit = np.arange(digits)
    turns = (digits * index[None, :, None] * index[None, None, :]
             + digit[:, None, None] * index[None, None, :]) % length
    if orient > 0:
        turns = np.swapaxes(turns, 1, 2)
    angle = orient * 2.0 * np.pi * turns / length
    c, s = np.cos(angle), np.sin(angle)
    full = np.concatenate([np.concatenate([c, -s], 2), np.concatenate([s, c], 2)], 1)
    high, low = split_pair(full)
    return np.concatenate([high, low], axis=2)


def four(a, b, c, d, orient):
    (ar, ai), (br, bi), (cr, ci), (dr, di) = a, b, c, d
    pr, pi = ar + cr, ai + ci
    mr, mi = ar - cr, ai - ci
    qr, qi = br + dr, bi + di
    nr, ni = br - dr, bi - di
    ir, ii = (-ni, nr) if orient > 0 else (ni, -nr)
    return [(pr + qr, pi + qi), (mr + ir, mi + ii), (pr - qr, pi - qi), (mr - ir, mi - ii)]


def turn16(value, step, orient):
    real, imag = value
    step = step % 16
    if step == 0:
        return value
    if step == 4:
        return (-imag, real) if orient > 0 else (imag, -real)
    root = float(np.sqrt(0.5))
    if step == 2:
        if orient > 0:
            return ((real - imag) * root, (real + imag) * root)
        return ((real + imag) * root, (imag - real) * root)
    if step == 6:
        if orient > 0:
            return ((real + imag) * -root, (real - imag) * root)
        return ((imag - real) * root, (real + imag) * -root)
    c = float(np.cos(2.0 * np.pi * step / 16))
    s = float(orient * np.sin(2.0 * np.pi * step / 16))
    return (real * c - imag * s, real * s + imag * c)


def sixteen(values, orient):
    inner = []
    for n2 in range(4):
        part = four(values[n2], values[4 + n2], values[8 + n2], values[12 + n2], orient)
        inner.append([turn16(part[k1], n2 * k1, orient) for k1 in range(4)])
    out = [None] * 16
    for k1 in range(4):
        part = four(inner[0][k1], inner[1][k1], inner[2][k1], inner[3][k1], orient)
        for k2 in range(4):
            out[k1 + 4 * k2] = part[k2]
    return out


def halves(value):
    high = value.astype(jnp.bfloat16)
    low = (value - high.astype(jnp.float32)).astype(jnp.bfloat16)
    return high, low


def times_right(value, table_ref):
    high, low = halves(value)
    wide = jnp.concatenate([high, low, high], axis=1)
    return jnp.dot(wide, table_ref[...], preferred_element_type=jnp.float32)


def times_left(table, value):
    high, low = halves(value)
    tall = jnp.concatenate([high, low, high], axis=0)
    wide = jnp.concatenate([table[:, :2 * lanes], table[:, :2 * lanes], table[:, 2 * lanes:]], axis=1)
    return jnp.dot(wide, tall, preferred_element_type=jnp.float32)


def product(a, b):
    return (a[0] * b[0] - a[1] * b[1], a[0] * b[1] + a[1] * b[0])


def to_last_wavenumbers(me, held, table_ref, out_refs):
    mine = out_refs[0].shape[0]
    rows = held.shape[1]
    for k, out_ref in enumerate(out_refs):
        base = (me ^ k) * mine
        done = times_right(held[pl.ds(base, mine)].reshape(mine * rows, 2 * lanes), table_ref)
        for j in range(mine):
            out_ref[j, 0] = done[j * rows:(j + 1) * rows, :lanes]
            out_ref[j, 1] = done[j * rows:(j + 1) * rows, lanes:]


def forward_last_kernel(shards, me_ref, x_ref, twid_ref, table_ref, *rest):
    outs, held = rest[:shards], rest[shards]
    rows = x_ref.shape[1]

    def one(t, carry):
        at = pl.ds(pl.multiple_of(t * sub, sub), sub)
        values = [
            (x_ref[0, at, a * lanes:(a + 1) * lanes], x_ref[1, at, a * lanes:(a + 1) * lanes])
            for a in range(digits)
        ]
        for q, value in enumerate(sixteen(values, -1)):
            if q:
                value = product(value, (twid_ref[0, q:q + 1, :], twid_ref[1, q:q + 1, :]))
            held[q, at, :lanes] = value[0]
            held[q, at, lanes:] = value[1]
        return carry

    lax.fori_loop(0, rows // sub, one, 0)
    to_last_wavenumbers(me_ref[0], held, table_ref, outs)


def smem():
    return pl.BlockSpec(memory_space=pltpu.SMEM)


def whole(table):
    return pl.BlockSpec(table.shape, lambda i: (0,) * table.ndim)


def forward_last(me, field, shards, chunk):
    _, rows, cols = field.shape
    mine = digits // shards
    twid = twiddle_table(cols, -1)
    table = right_table(-1)
    return pl.pallas_call(
        functools.partial(forward_last_kernel, shards),
        grid=(rows // chunk,),
        in_specs=[
            smem(),
            pl.BlockSpec((2, chunk, cols), lambda i: (0, i, 0)),
            whole(twid),
            whole(table),
        ],
        out_specs=[pl.BlockSpec((mine, 2, chunk, lanes), lambda i: (0, 0, i, 0))] * shards,
        out_shape=[jax.ShapeDtypeStruct((mine, 2, rows, lanes), jnp.float32)] * shards,
        scratch_shapes=[pltpu.VMEM((digits, chunk, 2 * lanes), jnp.float32)],
        compiler_params=pltpu.CompilerParams(vmem_limit_bytes=vmem_bytes),
        cost_estimate=pl.CostEstimate(
            flops=2 * 3 * rows * digits * 256 * 256, bytes_accessed=16 * rows * cols, transcendentals=0
        ),
        name="forward_last",
    )(me, field, twid, table)


def middle_kernel(sign, shards, pieces, me_ref, fwd_ref, inv_ref, mult_ref, *rest):
    ins, outs = rest[:shards], rest[shards:-2]
    held, spare = rest[-2:]
    per = digits // shards
    local = per * lanes
    me = me_ref[0]
    for k, in_ref in enumerate(ins):
        for j in range(per):
            spare[(me ^ k) * per + j] = in_ref[0, :, j * lanes:(j + 1) * lanes, :]

    def first(t, carry):
        base = pl.multiple_of(t * sub, sub)
        at = pl.ds(base, sub)
        values = [(spare[a, 0, at, :], spare[a, 1, at, :]) for a in range(digits)]
        for q, value in enumerate(sixteen(values, -1)):
            held[q, at, :] = value[0]
            held[q, pl.ds(lanes + base, sub), :] = value[1]
        return carry

    lax.fori_loop(0, lanes // sub, first, 0)

    def second(q, carry):
        spec = times_left(fwd_ref[q], held[q])
        real, imag = spec[:lanes], spec[lanes:]
        mr, mi = mult_ref[0, 0, q], mult_ref[1, 0, q]
        if sign > 0:
            moved = (real * mr - imag * mi, real * mi + imag * mr)
        else:
            moved = (real * mr + imag * mi, imag * mr - real * mi)
        held[q] = times_left(inv_ref[q], jnp.concatenate(moved, axis=0))
        return carry

    lax.fori_loop(0, digits, second, 0)

    def third(t, carry):
        base = pl.multiple_of(t * sub, sub)
        at = pl.ds(base, sub)
        values = [(held[q, at, :], held[q, pl.ds(lanes + base, sub), :]) for q in range(digits)]
        for a, value in enumerate(sixteen(values, 1)):
            spare[a, 0, at, :] = value[0]
            spare[a, 1, at, :] = value[1]
        return carry

    lax.fori_loop(0, lanes // sub, third, 0)
    start = 0
    for p, size in enumerate(pieces):
        for k in range(shards):
            out_ref = outs[p * shards + k]
            at = 0
            while at < size:
                row = start + at
                j, r = row // lanes, row % lanes
                span = min(size - at, lanes - r)
                out_ref[0, :, at:at + span, :] = spare[(me ^ k) * per + j, :, r:r + span, :]
                at += span
        start += size


def middle(me, moved, mult, sign, pieces):
    shards = len(moved)
    mine, _, rows, _ = moved[0].shape
    length = shards * rows
    fwd, inv = left_table(length, -1), left_table(length, 1)

    def block(size):
        return pl.BlockSpec((1, 2, size, lanes), lambda i: (i, 0, 0, 0))

    outs = pl.pallas_call(
        functools.partial(middle_kernel, sign, shards, pieces),
        grid=(mine,),
        in_specs=[
            smem(),
            whole(fwd),
            whole(inv),
            pl.BlockSpec((2, 1, digits, lanes, lanes), lambda i: (0, i, 0, 0, 0)),
        ] + [block(rows)] * shards,
        out_specs=[block(size) for size in pieces for _ in range(shards)],
        out_shape=[
            jax.ShapeDtypeStruct((mine, 2, size, lanes), jnp.float32) for size in pieces for _ in range(shards)
        ],
        scratch_shapes=[
            pltpu.VMEM((digits, 2 * lanes, lanes), jnp.float32),
            pltpu.VMEM((digits, 2, lanes, lanes), jnp.float32),
        ],
        compiler_params=pltpu.CompilerParams(vmem_limit_bytes=vmem_bytes),
        cost_estimate=pl.CostEstimate(
            flops=2 * 2 * 3 * rows * digits * 256 * 256,
            bytes_accessed=24 * rows * length,
            transcendentals=0,
        ),
        name="middle",
    )(me, fwd, inv, mult, *moved)
    return [outs[p * shards:(p + 1) * shards] for p in range(len(pieces))]


def space_kernel(sign, shards, onward, keep, with_image, aliased, *refs):
    refs = list(refs)
    me = refs.pop(0)[0]
    lens_ref, itwid_ref, itable_ref = refs[:3]
    del refs[:3]
    ins = refs[:shards]
    del refs[:shards]
    if with_image:
        other_ref = refs.pop(0)
    if onward:
        twid_ref, table_ref = refs[:2]
        del refs[:2]
    if aliased:
        refs.pop(0)
    held = refs.pop()
    field_ref = refs.pop(0) if keep else None
    if onward:
        outs = refs[:shards]
        del refs[:shards]
    if with_image:
        image_ref = refs.pop(0)
    mine, _, rows, _ = ins[0].shape

    for k, in_ref in enumerate(ins):
        wide = jnp.concatenate([in_ref[:, 0], in_ref[:, 1]], axis=2).reshape(mine * rows, 2 * lanes)
        held[pl.ds((me ^ k) * mine, mine)] = times_right(wide, itable_ref).reshape(mine, rows, 2 * lanes)

    def one(t, carry):
        at = pl.ds(pl.multiple_of(t * sub, sub), sub)
        values = []
        for q in range(digits):
            value = (held[q, at, :lanes], held[q, at, lanes:])
            if q:
                value = product(value, (itwid_ref[0, q:q + 1, :], itwid_ref[1, q:q + 1, :]))
            values.append(value)
        values = sixteen(values, 1)
        for a in range(digits):
            real, imag = values[a]
            col = slice(a * lanes, (a + 1) * lanes)
            c, s = lens_ref[0, at, col], lens_ref[1, at, col]
            if sign > 0:
                real, imag = real * c - imag * s, real * s + imag * c
            else:
                real, imag = real * c + imag * s, imag * c - real * s
            if keep:
                field_ref[0, at, col] = real
                field_ref[1, at, col] = imag
            if with_image:
                image_ref[at, col] = real * other_ref[0, at, col] + imag * other_ref[1, at, col]
            values[a] = (real, imag)
        if onward:
            for q, value in enumerate(sixteen(values, -1)):
                if q:
                    value = product(value, (twid_ref[0, q:q + 1, :], twid_ref[1, q:q + 1, :]))
                held[q, at, :lanes] = value[0]
                held[q, at, lanes:] = value[1]
        return carry

    lax.fori_loop(0, rows // sub, one, 0)
    if onward:
        to_last_wavenumbers(me, held, table_ref, outs)


def space(me, blocks, lens, sign, onward, other=None, keep=True, start=0, into=None, chunk=64):
    shards = len(blocks)
    mine, _, part, _ = blocks[0].shape
    _, rows, cols = lens.shape
    chunk = min(chunk, part)
    first = start // chunk
    itwid, itable = twiddle_table(cols, 1), right_table(1)
    row_spec = pl.BlockSpec((2, chunk, cols), lambda i: (0, first + i, 0))
    wave_spec = pl.BlockSpec((mine, 2, chunk, lanes), lambda i: (0, 0, i, 0))
    operands = [me, lens, itwid, itable, *blocks]
    in_specs = [smem(), row_spec, whole(itwid), whole(itable)] + [wave_spec] * shards
    if other is not None:
        operands.append(other)
        in_specs.append(row_spec)
    if onward:
        tables = [twiddle_table(cols, -1), right_table(-1)]
        operands += tables
        in_specs += [whole(table) for table in tables]
    aliases = {}
    if into is not None:
        aliases = {len(operands): 0}
        operands.append(into)
        in_specs.append(pl.BlockSpec(memory_space=pl.ANY))
    out_specs, out_shape = [], []
    if keep:
        out_specs.append(row_spec)
        out_shape.append(jax.ShapeDtypeStruct((2, rows, cols), jnp.float32))
    if onward:
        out_specs += [wave_spec] * shards
        out_shape += [jax.ShapeDtypeStruct((mine, 2, part, lanes), jnp.float32)] * shards
    if other is not None:
        out_specs.append(pl.BlockSpec((chunk, cols), lambda i: (i, 0)))
        out_shape.append(jax.ShapeDtypeStruct((part, cols), jnp.float32))
    outs = pl.pallas_call(
        functools.partial(space_kernel, sign, shards, onward, keep, other is not None, into is not None),
        grid=(part // chunk,),
        in_specs=in_specs,
        out_specs=out_specs,
        out_shape=out_shape,
        input_output_aliases=aliases,
        scratch_shapes=[pltpu.VMEM((digits, chunk, 2 * lanes), jnp.float32)],
        compiler_params=pltpu.CompilerParams(vmem_limit_bytes=vmem_bytes),
        cost_estimate=pl.CostEstimate(
            flops=(2 if onward else 1) * 2 * 3 * part * digits * 256 * 256,
            bytes_accessed=32 * part * cols,
            transcendentals=0,
        ),
        name="space",
    )(*operands)
    outs = list(outs)
    field = outs.pop(0) if keep else None
    term = outs.pop() if other is not None else None
    return field, outs, term


def wavenumber(index, length):
    signed = jnp.where(index < length // 2, index, index - length)
    return 2.0 * jnp.pi * (signed.astype(jnp.float32) / length)


def multiplier(omega, kx_index, ky_index, rows_total, cols_total):
    kx_values = wavenumber(kx_index, rows_total)
    ky_values = wavenumber(ky_index, cols_total)
    phase_q = omega * omega - (kx_values * kx_values + ky_values * ky_values)
    travel = jnp.sqrt(jnp.maximum(phase_q, 0.0))
    decay = jnp.sqrt(jnp.maximum(-phase_q, 0.0))
    damping = jnp.exp(-depth_step * decay) / (rows_total * cols_total)
    return damping * jnp.cos(depth_step * travel), damping * jnp.sin(depth_step * travel)


def swap(array, axis, mask):
    size = lax.axis_size(axis)
    return lax.ppermute(array, axis, [(d, d ^ mask) for d in range(size)])


def exchange(blocks, gates):
    if gates is not None:
        blocks = [blocks[0]] + [lax.optimization_barrier((b, g))[0] for b, g in zip(blocks[1:], gates[1:])]
    return [blocks[0]] + [swap(block, "row", k) for k, block in enumerate(blocks) if k]


def slices_of(slowness_store, store_pos):
    mine = lax.axis_index("freq")
    return [
        jnp.where(mine == store_pos[z], slowness_store[0], 0.0).astype(jnp.float32) for z in range(DEPTHS)
    ]


def on_device(source_field, receiver_field, slowness_store, store_pos, freq_index):
    omega = omega_unit * freq_index.astype(jnp.float32)[0]
    rows = source_field.shape[2]
    cols = source_field.shape[3]
    shards = lax.axis_size("row")
    n_freq = lax.axis_size("freq")
    mine = digits // shards
    rows_total = rows * shards
    me = lax.axis_index("row").astype(jnp.int32)[None]

    kept = slices_of(slowness_store, store_pos)
    slow = [lax.psum(kept[0], "freq")]
    second_kept, _ = lax.optimization_barrier((kept[1], slow[0]))
    slow.append(lax.psum(second_kept, "freq"))

    grid_shape = (mine, digits, lanes, lanes)
    kx_index = lax.broadcasted_iota(jnp.int32, grid_shape, 1) + digits * lax.broadcasted_iota(
        jnp.int32, grid_shape, 2
    )
    ky_index = (
        lax.axis_index("row") * mine
        + lax.broadcasted_iota(jnp.int32, grid_shape, 0)
        + digits * lax.broadcasted_iota(jnp.int32, grid_shape, 3)
    )
    mult = jnp.stack(multiplier(omega, kx_index, ky_index, rows_total, cols))

    spec_source = forward_last(me, source_field[0], shards, 128)
    spec_receiver = forward_last(me, receiver_field[0], shards, 128)
    images = []
    gates = None
    for z in range(DEPTHS):
        last = z == DEPTHS - 1
        moved_source = exchange(spec_source, gates)
        moved_receiver = exchange(spec_receiver, moved_source)
        (mid_source,) = middle(me, moved_source, mult, -1, (rows,))
        (mid_receiver,) = middle(me, moved_receiver, mult, 1, (rows,))
        back_source = exchange(mid_source, moved_receiver)
        back_receiver = exchange(mid_receiver, back_source)
        gates = back_receiver
        angles = depth_step * omega * slow[z]
        lens = jnp.stack([jnp.cos(angles), jnp.sin(angles)])
        source_now, spec_source, _ = space(me, back_source, lens, -1, not last)
        receiver_now, spec_receiver, term = space(
            me, back_receiver, lens, 1, not last, other=source_now, keep=last
        )
        if last:
            term, images[0] = lax.optimization_barrier((term, images[0]))
            for mask in (1, 2):
                term = term + swap(term, "freq", mask)
            images.append(term)
        else:
            images.append(lax.psum(term, "freq"))
    return jnp.stack(images), source_now[None], receiver_now[None]


def plain_step(field, mult_real, mult_imag):
    def table(length, orient):
        index = lax.broadcasted_iota(jnp.int32, (length, length), 0) * lax.broadcasted_iota(
            jnp.int32, (length, length), 1
        )
        angle = 2.0 * jnp.pi / length * (index % length).astype(jnp.float32)
        return jnp.cos(angle), orient * jnp.sin(angle)

    def along(real, imag, orient, last):
        c, s = table(real.shape[1 if last else 0], orient)
        dot = functools.partial(jnp.matmul, precision=lax.Precision.HIGHEST)
        if last:
            return dot(real, c) - dot(imag, s), dot(real, s) + dot(imag, c)
        return dot(c, real) - dot(s, imag), dot(s, real) + dot(c, imag)

    def trade(pair, split, join):
        both = lax.all_to_all(jnp.stack(pair), "row", split_axis=split, concat_axis=join, tiled=True)
        return both[0], both[1]

    real, imag = along(field[0], field[1], -1.0, True)
    real, imag = trade((real, imag), 2, 1)
    real, imag = along(real, imag, -1.0, False)
    real, imag = product((real, imag), (mult_real, mult_imag))
    real, imag = along(real, imag, 1.0, False)
    real, imag = trade((real, imag), 1, 2)
    return jnp.stack(along(real, imag, 1.0, True))


def on_device_plain(source_field, receiver_field, slowness_store, store_pos, freq_index):
    omega = omega_unit * freq_index.astype(jnp.float32)[0]
    rows = source_field.shape[2]
    cols = source_field.shape[3]
    shards = lax.axis_size("row")
    rows_total = rows * shards
    block = cols // shards
    slow = lax.psum(jnp.stack(slices_of(slowness_store, store_pos)), "freq")
    kx_index = lax.broadcasted_iota(jnp.int32, (rows_total, block), 0)
    ky_index = lax.broadcasted_iota(jnp.int32, (rows_total, block), 1) + lax.axis_index("row") * block
    mult_real, mult_imag = multiplier(omega, kx_index, ky_index, rows_total, cols)
    source_now, receiver_now = source_field[0], receiver_field[0]
    images = []
    for z in range(DEPTHS):
        angles = depth_step * omega * slow[z]
        lens_cos, lens_sin = jnp.cos(angles), jnp.sin(angles)
        source_now = plain_step(source_now, mult_real, -mult_imag)
        receiver_now = plain_step(receiver_now, mult_real, mult_imag)
        source_now = jnp.stack(product(source_now, (lens_cos, -lens_sin)))
        receiver_now = jnp.stack(product(receiver_now, (lens_cos, lens_sin)))
        images.append(lax.psum(jnp.sum(source_now * receiver_now, axis=0), "freq"))
    return jnp.stack(images), source_now[None], receiver_now[None]


def solution(mesh):
    placed = (
        P("freq", None, "row", None),
        P("freq", None, "row", None),
        P("freq", "row", None),
        P(),
        P("freq"),
    )

    def chosen(source_field, *rest):
        rows, cols = source_field.shape[2:]
        shards = lax.axis_size("row")
        length = digits * lanes
        four_freqs = lax.axis_size("freq") == 4
        fits = digits % shards == 0 and cols == length and rows * shards == length and four_freqs
        return (on_device if fits else on_device_plain)(source_field, *rest)

    return jax.shard_map(
        chosen,
        mesh=mesh,
        in_specs=placed,
        out_specs=(
            P(None, "row", None),
            P("freq", None, "row", None),
            P("freq", None, "row", None),
        ),
        check_vma=False,
    )
```

time: 1050 us -> 603 us (0.57); the launches traced: 1040 us -> 602 us
  local copies, waits for them, and re-layouts: 272 us -> 2.03 us
  matrix products: 179 us -> 0 us
  Pallas kernels: 0 us -> 163 us
  waiting for transfers between devices: 436 us -> 322 us
  other arithmetic: 94.1 us -> 39.9 us
  starting transfers between devices: 39.2 us -> 58.5 us
    ppermute x0 -> x58, waiting for transfers between devices: none -> 322 us  [swap(): return lax.ppermute(array, axis, [(d, d ^ mask) for d in range(size)])]
    all_to_all x8 -> x0, waiting for transfers between devices: 220 us -> none  [the longest x4 113 us: forward_one(): lax.all_to_all(first, 'row', split_axis=3, concat_axis=2, tiled=True)]
    psum x2, waiting for transfers between devices: 215 us -> 0.01 us  [the longest x1 0.01 us: on_device(): slow = [lax.psum(kept[0], 'freq')]]
    dot_general x32 -> x0, matrix products: 179 us -> none  [the longest x16 93.8 us: transform(): section = jnp.einsum(first_form, shaped, first_table, precision=highest)]
    pallas_call x0 -> x10, Pallas kernels: none -> 163 us  [the longest x4 109 us: middle(): pl.pallas_call(functools.partial(middle_kernel, sign, shards, pieces), gr...]
    transpose x12 -> x0, local copies, waits for them, and re-layouts: 72.7 us -> none  [the longest x4 48.8 us: transform(): return final.reshape(field.shape)]
    all_to_all x16 -> x0, local copies, waits for them, and re-layouts: 67.3 us -> none  [the longest x8 39.5 us: forward_one(): lax.all_to_all(first, 'row', split_axis=3, concat_axis=2, tiled=True)]
    ppermute x0 -> x58, starting transfers between devices: none -> 58.4 us  [swap(): return lax.ppermute(array, axis, [(d, d ^ mask) for d in range(size)])]
  transfers between devices with their start and end apart: 10 -> 60, of which waited for: 10 -> 20; matrix products, arithmetic and copies ran while one was open for 21% -> 6% of each run, Pallas kernels for 0% -> 22%
where the time goes in v1:
time: 603 us; the launch traced here: 602 us
  waiting for transfers between devices  322 us (53%)
  Pallas kernels  163 us (27%)
  starting transfers between devices  58.5 us (10%)
  other arithmetic  39.9 us (7%)
  between operations  16.4 us (3%)
    ppermute x58, waiting for transfers between devices, swap(): return lax.ppermute(array, axis, [(d, d ^ mask) for d in range(size)])  322 us
    pallas_call x4, Pallas kernels, middle(): pl.pallas_call(functools.partial(middle_kernel, sign, shards, pieces), gr...  109 us
    ppermute x58, starting transfers between devices, swap(): return lax.ppermute(array, axis, [(d, d ^ mask) for d in range(size)])  58.4 us
    pallas_call x4, Pallas kernels, space(): pl.pallas_call(functools.partial(space_kernel, sign, shards, onward, keep...  40.5 us
    another operation x4, other arithmetic, on_device(): lens = jnp.stack([jnp.cos(angles), jnp.sin(angles)])  21.4 us
    pallas_call x2, Pallas kernels, forward_last(): pl.pallas_call(functools.partial(forward_last_kernel, shards), grid=(rows...  13 us
  transfers between devices with their start and end apart: 60, of which 20 were waited for; matrix products, arithmetic and copies ran while one was open for 6% of the time, Pallas kernels for 22%

profile of v1, /device:TPU:0, one launch (start us, length us, event | category | flops | bytes accessed | tf_op | source)
XLA Modules:
  0.0 602.1 jit_solution(14763374191142886636)
XLA Ops:
  7.2 6.5 %forward_last.3 = (f32[2,2,256,128]{3,2,1,0:T(8,128)}, f32[2,2,256,128]{3,2,1,0:T(8,128)}, f32[2,2,256,128]{3,2,1,0:T(8,128)}, f32[2,2,256,128]{3,2,1,0:T(8,128)...) custom-call(s32[1]{0:T(128)} %bitcast.me_ref.refs_0_, ...), custom_call_target="tpu_custom_call" | custom-call | flops 1610612736 | bytes 8388608 | tf_op jit(solution)/shard_map/forward_last/pallas_call | solution.py:171
  20.7 9.0 %collective-permute-done.2.rest_2_ = f32[2,2,256,128]{3,2,1,0:T(8,128)S(1)} collective-permute-done((f32[2,2,256,128]{3,2,1,0:T(8,128)}, f32[2,2,256,128]{3,2,1,0:T(8,128)S(1)}, u32[]{:S(2)}, u32[]{:S(2)}) %collective-permute-start.2) | collective-permute-done | bytes 524320 | tf_op jit(solution)/shard_map/ppermute | solution.py:421
  29.7 3.0 collective-permute-start.10
  35.3 6.4 %forward_last.2 = (f32[2,2,256,128]{3,2,1,0:T(8,128)}, f32[2,2,256,128]{3,2,1,0:T(8,128)}, f32[2,2,256,128]{3,2,1,0:T(8,128)}, f32[2,2,256,128]{3,2,1,0:T(8,128)...) custom-call(s32[1]{0:T(128)} %bitcast.me_ref.refs_0_, ...), custom_call_target="tpu_custom_call" | custom-call | flops 1610612736 | bytes 8388608 | tf_op jit(solution)/shard_map/forward_last/pallas_call | solution.py:171
  43.8 20.7 %collective-permute-done.8.rest_5_ = f32[2,2,256,128]{3,2,1,0:T(8,128)} collective-permute-done((f32[2,2,256,128]{3,2,1,0:T(8,128)}, f32[2,2,256,128]{3,2,1,0:T(8,128)}, u32[]{:S(2)}, u32[]{:S(2)}) %collective-permute-start.8) | collective-permute-done | bytes 524320 | tf_op jit(solution)/shard_map/ppermute | solution.py:421
  69.2 9.2 %cosine_multiply_fusion = (f32[1,2,16,128,128]{4,3,2,1,0:T(8,128)S(1)}, f32[1,2,16,128,128]{4,3,2,1,0:T(8,128)S(1)}) fusion(s32[128]{0:T(128)S(1)} %iota_multiply_fusion, s32[2]{0:T(128)S(1)} %iota_add_fusion, f32[]{:T(128)} %bitcast.8), kind=kLoop, calls=%fused_computation.18 | loop fusion | flops 12582912 | bytes 4194828 | tf_op jit(solution)/shard_map/mul | solution.py:416
  82.0 27.8 %middle.5 = (f32[2,2,256,128]{3,2,1,0:T(8,128)}, f32[2,2,256,128]{3,2,1,0:T(8,128)}, f32[2,2,256,128]{3,2,1,0:T(8,128)}, f32[2,2,256,128]{3,2,1,0:T(8,128)}, f32...) custom-call(s32[1]{0:T(128)} %bitcast.me_ref.refs_0_, ...), custom_call_target="tpu_custom_call" | custom-call | flops 3221225472 | bytes 12582912 | tf_op jit(solution)/shard_map/middle/pallas_call | solution.py:258
  114.0 11.0 %collective-permute-done.13.rest_7_ = f32[2,2,256,128]{3,2,1,0:T(8,128)S(1)} collective-permute-done((f32[2,2,256,128]{3,2,1,0:T(8,128)}, f32[2,2,256,128]{3,2,1,0:T(8,128)S(1)}, u32[]{:S(2)}, u32[]{:S(2)}) %collective-permute-start.13) | collective-permute-done | bytes 524320 | tf_op jit(solution)/shard_map/ppermute | solution.py:421
  127.1 8.2 %collective-permute-done.18.refs_7_ = f32[2,2,256,128]{3,2,1,0:T(8,128)} collective-permute-done((f32[2,2,256,128]{3,2,1,0:T(8,128)}, f32[2,2,256,128]{3,2,1,0:T(8,128)}, u32[]{:S(2)}, u32[]{:S(2)}) %collective-permute-start.18) | collective-permute-done | bytes 524320 | tf_op jit(solution)/shard_map/ppermute | solution.py:421
  137.3 10.6 %collective-permute-done.16.refs_6_ = f32[2,2,256,128]{3,2,1,0:T(8,128)} collective-permute-done((f32[2,2,256,128]{3,2,1,0:T(8,128)}, f32[2,2,256,128]{3,2,1,0:T(8,128)}, u32[]{:S(2)}, u32[]{:S(2)}) %collective-permute-start.16) | collective-permute-done | bytes 524320 | tf_op jit(solution)/shard_map/ppermute | solution.py:421
  148.0 27.2 %middle.4 = (f32[2,2,256,128]{3,2,1,0:T(8,128)}, f32[2,2,256,128]{3,2,1,0:T(8,128)}, f32[2,2,256,128]{3,2,1,0:T(8,128)}, f32[2,2,256,128]{3,2,1,0:T(8,128)}, f32...) custom-call(s32[1]{0:T(128)} %bitcast.me_ref.refs_0_, ...), custom_call_target="tpu_custom_call" | custom-call | flops 3221225472 | bytes 12582912 | tf_op jit(solution)/shard_map/middle/pallas_call | solution.py:258
  180.1 8.4 %cosine_bitcast_fusion = (f32[1,256,2048]{2,1,0:T(8,128)S(1)}, f32[1,256,2048]{2,1,0:T(8,128)S(1)}) fusion(f32[256,2048]{1,0:T(8,128)} %all-reduce.4.cloned.1.call-done, f32[]{:T(128)} %bitcast.1), kind=kLoop, calls=%fused_computation.16 | loop fusion | flops 524288 | bytes 6291460 | tf_op jit(solution)/shard_map/stack | solution.py:477
  190.4 12.0 %collective-permute-done.25.refs_10_ = f32[2,2,256,128]{3,2,1,0:T(8,128)S(1)} collective-permute-done((f32[2,2,256,128]{3,2,1,0:T(8,128)}, f32[2,2,256,128]{3,2,1,0:T(8,128)S(1)}, u32[]{:S(2)}, u32[]{:S(2)}) %collective-permute-start.25) | collective-permute-done | bytes 524320 | tf_op jit(solution)/shard_map/ppermute | solution.py:421
  204.7 11.3 %space.4 = (f32[2,256,2048]{2,1,0:T(8,128)}, f32[2,2,256,128]{3,2,1,0:T(8,128)}, f32[2,2,256,128]{3,2,1,0:T(8,128)}, f32[2,2,256,128]{3,2,1,0:T(8,128)}, f32[2,2...) custom-call(s32[1]{0:T(128)} %bitcast.me_ref.refs_0_, ...), custom_call_target="tpu_custom_call" | custom-call | flops 3221225472 | bytes 16777216 | tf_op jit(solution)/shard_map/space/pallas_call | solution.py:382
  216.0 8.2 %collective-permute-done.21.refs_8_ = f32[2,2,256,128]{3,2,1,0:T(8,128)S(1)} collective-permute-done((f32[2,2,256,128]{3,2,1,0:T(8,128)}, f32[2,2,256,128]{3,2,1,0:T(8,128)S(1)}, u32[]{:S(2)}, u32[]{:S(2)}) %collective-permute-start.21) | collective-permute-done | bytes 524320 | tf_op jit(solution)/shard_map/ppermute | solution.py:421
  225.6 11.8 %space.5 = (f32[2,2,256,128]{3,2,1,0:T(8,128)}, f32[2,2,256,128]{3,2,1,0:T(8,128)}, f32[2,2,256,128]{3,2,1,0:T(8,128)}, f32[2,2,256,128]{3,2,1,0:T(8,128)}, f32[...) custom-call(s32[1]{0:T(128)} %bitcast.me_ref.refs_0_, ...), custom_call_target="tpu_custom_call" | custom-call | flops 3221225472 | bytes 16777216 | tf_op jit(solution)/shard_map/space/pallas_call | solution.py:382
  242.3 10.2 %collective-permute-done.40.rest_7_ = f32[2,2,256,128]{3,2,1,0:T(8,128)S(1)} collective-permute-done((f32[2,2,256,128]{3,2,1,0:T(8,128)}, f32[2,2,256,128]{3,2,1,0:T(8,128)S(1)}, u32[]{:S(2)}, u32[]{:S(2)}) %collective-permute-start.40) | collective-permute-done | bytes 524320 | tf_op jit(solution)/shard_map/ppermute | solution.py:421
  253.9 9.4 %collective-permute-done.32.rest_3_ = f32[2,2,256,128]{3,2,1,0:T(8,128)S(1)} collective-permute-done((f32[2,2,256,128]{3,2,1,0:T(8,128)}, f32[2,2,256,128]{3,2,1,0:T(8,128)S(1)}, u32[]{:S(2)}, u32[]{:S(2)}) %collective-permute-start.32) | collective-permute-done | bytes 524320 | tf_op jit(solution)/shard_map/ppermute | solution.py:421
  265.5 9.6 %collective-permute-done.30.rest_2_ = f32[2,2,256,128]{3,2,1,0:T(8,128)S(1)} collective-permute-done((f32[2,2,256,128]{3,2,1,0:T(8,128)S(1)}, f32[2,2,256,128]{3,2,1,0:T(8,128)S(1)}, u32[]{:S(2)}, u32[]{:S(2)}) %collective-permute-start.30) | collective-permute-done | bytes 524320 | tf_op jit(solution)/shard_map/ppermute | solution.py:421
  275.1 11.9 %collective-permute-done.38.rest_6_ = f32[2,2,256,128]{3,2,1,0:T(8,128)S(1)} collective-permute-done((f32[2,2,256,128]{3,2,1,0:T(8,128)S(1)}, f32[2,2,256,128]{3,2,1,0:T(8,128)S(1)}, u32[]{:S(2)}, u32[]{:S(2)}) %collective-permute-start.38) | collective-permute-done | bytes 524320 | tf_op jit(solution)/shard_map/ppermute | solution.py:421
  288.2 12.4 %collective-permute-done.34.rest_4_ = f32[2,2,256,128]{3,2,1,0:T(8,128)S(1)} collective-permute-done((f32[2,2,256,128]{3,2,1,0:T(8,128)}, f32[2,2,256,128]{3,2,1,0:T(8,128)S(1)}, u32[]{:S(2)}, u32[]{:S(2)}) %collective-permute-start.34) | collective-permute-done | bytes 524320 | tf_op jit(solution)/shard_map/ppermute | solution.py:421
  302.3 27.2 %middle.7 = (f32[2,2,256,128]{3,2,1,0:T(8,128)}, f32[2,2,256,128]{3,2,1,0:T(8,128)}, f32[2,2,256,128]{3,2,1,0:T(8,128)}, f32[2,2,256,128]{3,2,1,0:T(8,128)}, f32...) custom-call(s32[1]{0:T(128)} %bitcast.me_ref.refs_0_, ...), custom_call_target="tpu_custom_call" | custom-call | flops 3221225472 | bytes 12582912 | tf_op jit(solution)/shard_map/middle/pallas_call | solution.py:258
  334.5 11.1 %collective-permute-done.39.rest_6_ = f32[2,2,256,128]{3,2,1,0:T(8,128)S(1)} collective-permute-done((f32[2,2,256,128]{3,2,1,0:T(8,128)}, f32[2,2,256,128]{3,2,1,0:T(8,128)S(1)}, u32[]{:S(2)}, u32[]{:S(2)}) %collective-permute-start.39) | collective-permute-done | bytes 524320 | tf_op jit(solution)/shard_map/ppermute | solution.py:421
  346.5 8.7 %collective-permute-done.54.refs_11_ = f32[2,2,256,128]{3,2,1,0:T(8,128)S(1)} collective-permute-done((f32[2,2,256,128]{3,2,1,0:T(8,128)}, f32[2,2,256,128]{3,2,1,0:T(8,128)S(1)}, u32[]{:S(2)}, u32[]{:S(2)}) %collective-permute-start.54) | collective-permute-done | bytes 524320 | tf_op jit(solution)/shard_map/ppermute | solution.py:421
  358.7 27.2 %middle.6 = (f32[2,2,256,128]{3,2,1,0:T(8,128)}, f32[2,2,256,128]{3,2,1,0:T(8,128)}, f32[2,2,256,128]{3,2,1,0:T(8,128)}, f32[2,2,256,128]{3,2,1,0:T(8,128)}, f32...) custom-call(s32[1]{0:T(128)} %bitcast.me_ref.refs_0_, ...), custom_call_target="tpu_custom_call" | custom-call | flops 3221225472 | bytes 12582912 | tf_op jit(solution)/shard_map/middle/pallas_call | solution.py:258
  387.1 17.2 %collective-permute-done.48.refs_8_ = f32[2,2,256,128]{3,2,1,0:T(8,128)} collective-permute-done((f32[2,2,256,128]{3,2,1,0:T(8,128)}, f32[2,2,256,128]{3,2,1,0:T(8,128)}, u32[]{:S(2)}, u32[]{:S(2)}) %collective-permute-start.48) | collective-permute-done | bytes 524320 | tf_op jit(solution)/shard_map/ppermute | solution.py:421
  408.7 8.4 %cosine_bitcast_fusion.1 = (f32[1,256,2048]{2,1,0:T(8,128)S(1)}, f32[1,256,2048]{2,1,0:T(8,128)S(1)}) fusion(f32[256,2048]{1,0:T(8,128)} %get-tuple-element.243, f32[]{:T(128)} %bitcast.1), kind=kLoop, calls=%fused_computation.22 | loop fusion | flops 524288 | bytes 6291460 | tf_op jit(solution)/shard_map/stack | solution.py:477
  419.5 7.9 %space.6.refs_12_ = f32[2,256,2048]{2,1,0:T(8,128)} custom-call(s32[1]{0:T(128)} %bitcast.me_ref.refs_0_, f32[2,256,2048]{2,1,0:T(8,128)} %pad_maximum_fusion.refs_1_, f32[2,16,128]{2,1,0:T(8,128)} %constant.59.clone.refs_2_, bf16[768,256]{1,0:T(8,128)(2,1)} %constant.60.clone.refs_3_, f32[2,2,256,128]{3,2,1,0:T(8,128)} %get-tuple-element.237.refs_4_, ...), custom_call_target="tpu_custom_call" | custom-call | flops 1610612736 | bytes 16777216 | tf_op jit(solution)/shard_map/space/pallas_call | solution.py:382
  429.4 11.2 %collective-permute-done.49.refs_8_ = f32[2,2,256,128]{3,2,1,0:T(8,128)} collective-permute-done((f32[2,2,256,128]{3,2,1,0:T(8,128)}, f32[2,2,256,128]{3,2,1,0:T(8,128)}, u32[]{:S(2)}, u32[]{:S(2)}) %collective-permute-start.49) | collective-permute-done | bytes 524320 | tf_op jit(solution)/shard_map/ppermute | solution.py:421
  440.6 9.5 %space.7 = (f32[2,256,2048]{2,1,0:T(8,128)}, f32[256,2048]{1,0:T(8,128)}) custom-call(s32[1]{0:T(128)} %bitcast.me_ref.refs_0_, f32[2,256,2048]{2,1,0:T(8,128)} %pad_maximum_fusion.refs_1_, f32[2,16,128]{2,1,0:T(8,128)} %constant.59.clone.refs_2_, bf16[768,256]{1,0:T(8,128)(2,1)} %constant.60.clone.refs_3_, f32[2,2,256,128]{3,2,1,0:T(8,128)} %get-tuple-element.207.refs_4_, ...), custom_call_target="tpu_custom_call" | custom-call | flops 1610612736 | bytes 16777216 | tf_op jit(solution)/shard_map/space/pallas_call | solution.py:382
  450.9 47.2 %collective-permute-done.56 = f32[256,2048]{1,0:T(8,128)S(1)} collective-permute-done((f32[256,2048]{1,0:T(8,128)}, f32[256,2048]{1,0:T(8,128)S(1)}, u32[]{:S(2)}, u32[]{:S(2)}) %collective-permute-start.56) | collective-permute-done | bytes 2097184 | tf_op jit(solution)/shard_map/ppermute | solution.py:421
  502.4 90.3 %collective-permute-done.57 = f32[256,2048]{1,0:T(8,128)S(1)} collective-permute-done((f32[256,2048]{1,0:T(8,128)S(1)}, f32[256,2048]{1,0:T(8,128)S(1)}, u32[]{:S(2)}, u32[]{:S(2)}) %collective-permute-start.57) | collective-permute-done | bytes 2097184 | tf_op jit(solution)/shard_map/ppermute | solution.py:421
  (199 shorter events, 74.8 us)
Async XLA Ops:
  7.2 173.0 %all-reduce.4.cloned.1.call-start = ((), (), s32[]{:S(2)}) async-start(), calls=%async_computation | async-start | bytes 4194304 | tf_op jit(solution)/shard_map/psum | solution.py:448
  16.7 50.9 %collective-permute-start = (f32[2,2,256,128]{3,2,1,0:T(8,128)}, f32[2,2,256,128]{3,2,1,0:T(8,128)S(1)}, u32[]{:S(2)}, u32[]{:S(2)}) collective-permute-start(f32[2,2,256,128]{3,2,1,0:T(8,128)} %get-tuple-element.126), channel_id=1, source_target_pairs={{0,1},{1,0},{2,3},{3,2},{4,5},{5,4},{6,7},{7,6},{8,9},{9,8},{10,11... | collective-permute-start | bytes 1572872 | tf_op jit(solution)/shard_map/ppermute | solution.py:421
  16.9 50.8 %collective-permute-start.6 = (f32[2,2,256,128]{3,2,1,0:T(8,128)}, f32[2,2,256,128]{3,2,1,0:T(8,128)}, u32[]{:S(2)}, u32[]{:S(2)}) collective-permute-start(f32[2,2,256,128]{3,2,1,0:T(8,128)} %get-tuple-element.135), channel_id=1, source_target_pairs={{0,4},{1,5},{2,6},{3,7},{4,0},{5,1},{6,2},{7,3},{8,12},{9,13},{10,... | collective-permute-start | bytes 1572872 | tf_op jit(solution)/shard_map/ppermute | solution.py:421
  18.9 45.6 %collective-permute-start.8 = (f32[2,2,256,128]{3,2,1,0:T(8,128)}, f32[2,2,256,128]{3,2,1,0:T(8,128)}, u32[]{:S(2)}, u32[]{:S(2)}) collective-permute-start(f32[2,2,256,128]{3,2,1,0:T(8,128)} %get-tuple-element.138), channel_id=1, source_target_pairs={{0,5},{1,4},{2,7},{3,6},{4,1},{5,0},{6,3},{7,2},{8,13},{9,12},{10,... | collective-permute-start | bytes 1572872 | tf_op jit(solution)/shard_map/ppermute | solution.py:421
  35.2 373.5 %all-reduce.6.cloned.1.call-start = ((), (), s32[]{:S(2)}) async-start(), calls=%async_computation.1 | async-start | bytes 8388608 | tf_op jit(solution)/shard_map/psum | solution.py:450
  42.4 38.3 %collective-permute-start.12 = (f32[2,2,256,128]{3,2,1,0:T(8,128)S(1)}, f32[2,2,256,128]{3,2,1,0:T(8,128)S(1)}, u32[]{:S(2)}, u32[]{:S(2)}) collective-permute-start(f32[2,2,256,128]{3,2,1,0:T(8,128)S(1)} %copy-done.39), channel_id=1, source_target_pairs={{0,7},{1,6},{2,5},{3,4},{4,3},{5,2},{6,1},{7,0},{8,15},{9,14},{10,... | collective-permute-start | bytes 1572872 | tf_op jit(solution)/shard_map/ppermute | solution.py:421
  64.5 46.3 %collective-permute-start.11 = (f32[2,2,256,128]{3,2,1,0:T(8,128)}, f32[2,2,256,128]{3,2,1,0:T(8,128)S(1)}, u32[]{:S(2)}, u32[]{:S(2)}) collective-permute-start(f32[2,2,256,128]{3,2,1,0:T(8,128)} %get-tuple-element.142), channel_id=1, source_target_pairs={{0,6},{1,7},{2,4},{3,5},{4,2},{5,3},{6,0},{7,1},{8,14},{9,15},{10,... | collective-permute-start | bytes 1572872 | tf_op jit(solution)/shard_map/ppermute | solution.py:421
  66.7 45.8 %collective-permute-start.9 = (f32[2,2,256,128]{3,2,1,0:T(8,128)}, f32[2,2,256,128]{3,2,1,0:T(8,128)S(1)}, u32[]{:S(2)}, u32[]{:S(2)}) collective-permute-start(f32[2,2,256,128]{3,2,1,0:T(8,128)} %get-tuple-element.139), channel_id=1, source_target_pairs={{0,5},{1,4},{2,7},{3,6},{4,1},{5,0},{6,3},{7,2},{8,13},{9,12},{10,... | collective-permute-start | bytes 1572872 | tf_op jit(solution)/shard_map/ppermute | solution.py:421
  67.6 42.2 %collective-permute-start.5 = (f32[2,2,256,128]{3,2,1,0:T(8,128)}, f32[2,2,256,128]{3,2,1,0:T(8,128)S(1)}, u32[]{:S(2)}, u32[]{:S(2)}) collective-permute-start(f32[2,2,256,128]{3,2,1,0:T(8,128)} %get-tuple-element.133), channel_id=1, source_target_pairs={{0,3},{1,2},{2,1},{3,0},{4,7},{5,6},{6,5},{7,4},{8,11},{9,10},{10,... | collective-permute-start | bytes 1572872 | tf_op jit(solution)/shard_map/ppermute | solution.py:421
  67.7 43.2 %collective-permute-start.3 = (f32[2,2,256,128]{3,2,1,0:T(8,128)}, f32[2,2,256,128]{3,2,1,0:T(8,128)S(1)}, u32[]{:S(2)}, u32[]{:S(2)}) collective-permute-start(f32[2,2,256,128]{3,2,1,0:T(8,128)} %get-tuple-element.130), channel_id=1, source_target_pairs={{0,2},{1,3},{2,0},{3,1},{4,6},{5,7},{6,4},{7,5},{8,10},{9,11},{10,... | collective-permute-start | bytes 1572872 | tf_op jit(solution)/shard_map/ppermute | solution.py:421
  112.5 35.4 %collective-permute-start.16 = (f32[2,2,256,128]{3,2,1,0:T(8,128)}, f32[2,2,256,128]{3,2,1,0:T(8,128)}, u32[]{:S(2)}, u32[]{:S(2)}) collective-permute-start(f32[2,2,256,128]{3,2,1,0:T(8,128)} %get-tuple-element.154), channel_id=1, source_target_pairs={{0,2},{1,3},{2,0},{3,1},{4,6},{5,7},{6,4},{7,5},{8,10},{9,11},{10,... | collective-permute-start | bytes 1572872 | tf_op jit(solution)/shard_map/ppermute | solution.py:421
  112.9 62.2 %collective-permute-start.20 = (f32[2,2,256,128]{3,2,1,0:T(8,128)}, f32[2,2,256,128]{3,2,1,0:T(8,128)}, u32[]{:S(2)}, u32[]{:S(2)}) collective-permute-start(f32[2,2,256,128]{3,2,1,0:T(8,128)} %get-tuple-element.162), channel_id=1, source_target_pairs={{0,4},{1,5},{2,6},{3,7},{4,0},{5,1},{6,2},{7,3},{8,12},{9,13},{10,... | collective-permute-start | bytes 1572872 | tf_op jit(solution)/shard_map/ppermute | solution.py:421
  125.0 50.1 %collective-permute-start.22 = (f32[2,2,256,128]{3,2,1,0:T(8,128)}, f32[2,2,256,128]{3,2,1,0:T(8,128)}, u32[]{:S(2)}, u32[]{:S(2)}) collective-permute-start(f32[2,2,256,128]{3,2,1,0:T(8,128)} %get-tuple-element.166), channel_id=1, source_target_pairs={{0,5},{1,4},{2,7},{3,6},{4,1},{5,0},{6,3},{7,2},{8,13},{9,12},{10,... | collective-permute-start | bytes 1572872 | tf_op jit(solution)/shard_map/ppermute | solution.py:421
  126.2 48.9 %collective-permute-start.24 = (f32[2,2,256,128]{3,2,1,0:T(8,128)}, f32[2,2,256,128]{3,2,1,0:T(8,128)}, u32[]{:S(2)}, u32[]{:S(2)}) collective-permute-start(f32[2,2,256,128]{3,2,1,0:T(8,128)} %get-tuple-element.170), channel_id=1, source_target_pairs={{0,6},{1,7},{2,4},{3,5},{4,2},{5,3},{6,0},{7,1},{8,14},{9,15},{10,... | collective-permute-start | bytes 1572872 | tf_op jit(solution)/shard_map/ppermute | solution.py:421
  135.3 39.8 %collective-permute-start.26 = (f32[2,2,256,128]{3,2,1,0:T(8,128)}, f32[2,2,256,128]{3,2,1,0:T(8,128)}, u32[]{:S(2)}, u32[]{:S(2)}) collective-permute-start(f32[2,2,256,128]{3,2,1,0:T(8,128)} %get-tuple-element.174), channel_id=1, source_target_pairs={{0,7},{1,6},{2,5},{3,4},{4,3},{5,2},{6,1},{7,0},{8,15},{9,14},{10,... | collective-permute-start | bytes 1572872 | tf_op jit(solution)/shard_map/ppermute | solution.py:421
  178.2 37.8 %collective-permute-start.23 = (f32[2,2,256,128]{3,2,1,0:T(8,128)}, f32[2,2,256,128]{3,2,1,0:T(8,128)S(1)}, u32[]{:S(2)}, u32[]{:S(2)}) collective-permute-start(f32[2,2,256,128]{3,2,1,0:T(8,128)} %get-tuple-element.167), channel_id=1, source_target_pairs={{0,5},{1,4},{2,7},{3,6},{4,1},{5,0},{6,3},{7,2},{8,13},{9,12},{10,... | collective-permute-start | bytes 1572872 | tf_op jit(solution)/shard_map/ppermute | solution.py:421
  178.5 45.8 %collective-permute-start.21 = (f32[2,2,256,128]{3,2,1,0:T(8,128)}, f32[2,2,256,128]{3,2,1,0:T(8,128)S(1)}, u32[]{:S(2)}, u32[]{:S(2)}) collective-permute-start(f32[2,2,256,128]{3,2,1,0:T(8,128)} %get-tuple-element.163), channel_id=1, source_target_pairs={{0,4},{1,5},{2,6},{3,7},{4,0},{5,1},{6,2},{7,3},{8,12},{9,13},{10,... | collective-permute-start | bytes 1572872 | tf_op jit(solution)/shard_map/ppermute | solution.py:421
  179.6 44.6 %collective-permute-start.19 = (f32[2,2,256,128]{3,2,1,0:T(8,128)}, f32[2,2,256,128]{3,2,1,0:T(8,128)S(1)}, u32[]{:S(2)}, u32[]{:S(2)}) collective-permute-start(f32[2,2,256,128]{3,2,1,0:T(8,128)} %get-tuple-element.159), channel_id=1, source_target_pairs={{0,3},{1,2},{2,1},{3,0},{4,7},{5,6},{6,5},{7,4},{8,11},{9,10},{10,... | collective-permute-start | bytes 1572872 | tf_op jit(solution)/shard_map/ppermute | solution.py:421
  240.4 46.6 %collective-permute-start.38 = (f32[2,2,256,128]{3,2,1,0:T(8,128)S(1)}, f32[2,2,256,128]{3,2,1,0:T(8,128)S(1)}, u32[]{:S(2)}, u32[]{:S(2)}) collective-permute-start(f32[2,2,256,128]{3,2,1,0:T(8,128)S(1)} %copy-done.41), channel_id=1, source_target_pairs={{0,6},{1,7},{2,4},{3,5},{4,2},{5,3},{6,0},{7,1},{8,14},{9,15},{10,... | collective-permute-start | bytes 1572872 | tf_op jit(solution)/shard_map/ppermute | solution.py:421
  263.2 37.3 %collective-permute-start.34 = (f32[2,2,256,128]{3,2,1,0:T(8,128)}, f32[2,2,256,128]{3,2,1,0:T(8,128)S(1)}, u32[]{:S(2)}, u32[]{:S(2)}) collective-permute-start(f32[2,2,256,128]{3,2,1,0:T(8,128)} %get-tuple-element.193), channel_id=1, source_target_pairs={{0,4},{1,5},{2,6},{3,7},{4,0},{5,1},{6,2},{7,3},{8,12},{9,13},{10,... | collective-permute-start | bytes 1572872 | tf_op jit(solution)/shard_map/ppermute | solution.py:421
  264.4 37.0 %collective-permute-start.41 = (f32[2,2,256,128]{3,2,1,0:T(8,128)}, f32[2,2,256,128]{3,2,1,0:T(8,128)S(1)}, u32[]{:S(2)}, u32[]{:S(2)}) collective-permute-start(f32[2,2,256,128]{3,2,1,0:T(8,128)} %get-tuple-element.206), channel_id=1, source_target_pairs={{0,7},{1,6},{2,5},{3,4},{4,3},{5,2},{6,1},{7,0},{8,15},{9,14},{10,... | collective-permute-start | bytes 1572872 | tf_op jit(solution)/shard_map/ppermute | solution.py:421
  275.1 54.5 %collective-permute-start.29 = (f32[2,2,256,128]{3,2,1,0:T(8,128)}, f32[2,2,256,128]{3,2,1,0:T(8,128)S(1)}, u32[]{:S(2)}, u32[]{:S(2)}) collective-permute-start(f32[2,2,256,128]{3,2,1,0:T(8,128)} %get-tuple-element.182), channel_id=1, source_target_pairs={{0,1},{1,0},{2,3},{3,2},{4,5},{5,4},{6,7},{7,6},{8,9},{9,8},{10,11... | collective-permute-start | bytes 1572872 | tf_op jit(solution)/shard_map/ppermute | solution.py:421
  287.0 43.7 %collective-permute-start.33 = (f32[2,2,256,128]{3,2,1,0:T(8,128)}, f32[2,2,256,128]{3,2,1,0:T(8,128)S(1)}, u32[]{:S(2)}, u32[]{:S(2)}) collective-permute-start(f32[2,2,256,128]{3,2,1,0:T(8,128)} %get-tuple-element.190), channel_id=1, source_target_pairs={{0,3},{1,2},{2,1},{3,0},{4,7},{5,6},{6,5},{7,4},{8,11},{9,10},{10,... | collective-permute-start | bytes 1572872 | tf_op jit(solution)/shard_map/ppermute | solution.py:421
  287.0 45.1 %collective-permute-start.31 = (f32[2,2,256,128]{3,2,1,0:T(8,128)}, f32[2,2,256,128]{3,2,1,0:T(8,128)S(1)}, u32[]{:S(2)}, u32[]{:S(2)}) collective-permute-start(f32[2,2,256,128]{3,2,1,0:T(8,128)} %get-tuple-element.186), channel_id=1, source_target_pairs={{0,2},{1,3},{2,0},{3,1},{4,6},{5,7},{6,4},{7,5},{8,10},{9,11},{10,... | collective-permute-start | bytes 1572872 | tf_op jit(solution)/shard_map/ppermute | solution.py:421
  332.7 53.2 %collective-permute-start.46 = (f32[2,2,256,128]{3,2,1,0:T(8,128)}, f32[2,2,256,128]{3,2,1,0:T(8,128)S(1)}, u32[]{:S(2)}, u32[]{:S(2)}) collective-permute-start(f32[2,2,256,128]{3,2,1,0:T(8,128)} %get-tuple-element.219), channel_id=1, source_target_pairs={{0,3},{1,2},{2,1},{3,0},{4,7},{5,6},{6,5},{7,4},{8,11},{9,10},{10,... | collective-permute-start | bytes 1572872 | tf_op jit(solution)/shard_map/ppermute | solution.py:421
  333.1 52.9 %collective-permute-start.44 = (f32[2,2,256,128]{3,2,1,0:T(8,128)}, f32[2,2,256,128]{3,2,1,0:T(8,128)S(1)}, u32[]{:S(2)}, u32[]{:S(2)}) collective-permute-start(f32[2,2,256,128]{3,2,1,0:T(8,128)} %get-tuple-element.215), channel_id=1, source_target_pairs={{0,2},{1,3},{2,0},{3,1},{4,6},{5,7},{6,4},{7,5},{8,10},{9,11},{10,... | collective-permute-start | bytes 1572872 | tf_op jit(solution)/shard_map/ppermute | solution.py:421
  345.6 58.7 %collective-permute-start.52 = (f32[2,2,256,128]{3,2,1,0:T(8,128)}, f32[2,2,256,128]{3,2,1,0:T(8,128)}, u32[]{:S(2)}, u32[]{:S(2)}) collective-permute-start(f32[2,2,256,128]{3,2,1,0:T(8,128)} %get-tuple-element.231), channel_id=1, source_target_pairs={{0,6},{1,7},{2,4},{3,5},{4,2},{5,3},{6,0},{7,1},{8,14},{9,15},{10,... | collective-permute-start | bytes 1572872 | tf_op jit(solution)/shard_map/ppermute | solution.py:421
  355.3 49.0 %collective-permute-start.50 = (f32[2,2,256,128]{3,2,1,0:T(8,128)}, f32[2,2,256,128]{3,2,1,0:T(8,128)}, u32[]{:S(2)}, u32[]{:S(2)}) collective-permute-start(f32[2,2,256,128]{3,2,1,0:T(8,128)} %get-tuple-element.227), channel_id=1, source_target_pairs={{0,5},{1,4},{2,7},{3,6},{4,1},{5,0},{6,3},{7,2},{8,13},{9,12},{10,... | collective-permute-start | bytes 1572872 | tf_op jit(solution)/shard_map/ppermute | solution.py:421
  357.8 46.5 %collective-permute-start.48 = (f32[2,2,256,128]{3,2,1,0:T(8,128)}, f32[2,2,256,128]{3,2,1,0:T(8,128)}, u32[]{:S(2)}, u32[]{:S(2)}) collective-permute-start(f32[2,2,256,128]{3,2,1,0:T(8,128)} %get-tuple-element.223), channel_id=1, source_target_pairs={{0,4},{1,5},{2,6},{3,7},{4,0},{5,1},{6,2},{7,3},{8,12},{9,13},{10,... | collective-permute-start | bytes 1572872 | tf_op jit(solution)/shard_map/ppermute | solution.py:421
  405.2 35.4 %collective-permute-start.49 = (f32[2,2,256,128]{3,2,1,0:T(8,128)}, f32[2,2,256,128]{3,2,1,0:T(8,128)}, u32[]{:S(2)}, u32[]{:S(2)}) collective-permute-start(f32[2,2,256,128]{3,2,1,0:T(8,128)} %get-tuple-element.224), channel_id=1, source_target_pairs={{0,4},{1,5},{2,6},{3,7},{4,0},{5,1},{6,2},{7,3},{8,12},{9,13},{10,... | collective-permute-start | bytes 1572872 | tf_op jit(solution)/shard_map/ppermute | solution.py:421
  450.2 47.9 %collective-permute-start.56 = (f32[256,2048]{1,0:T(8,128)}, f32[256,2048]{1,0:T(8,128)S(1)}, u32[]{:S(2)}, u32[]{:S(2)}) collective-permute-start(f32[256,2048]{1,0:T(8,128)} %get-tuple-element.241), channel_id=1, source_target_pairs={{0,8},{8,0},{16,24},{24,16},{1,9},{9,1},{17,25},{25,17},{2,10},{10... | collective-permute-start | bytes 6291464 | tf_op jit(solution)/shard_map/ppermute | solution.py:421
  500.0 92.7 %collective-permute-start.57 = (f32[256,2048]{1,0:T(8,128)S(1)}, f32[256,2048]{1,0:T(8,128)S(1)}, u32[]{:S(2)}, u32[]{:S(2)}) collective-permute-start(f32[256,2048]{1,0:T(8,128)S(1)} %add.90), channel_id=1, source_target_pairs={{0,16},{8,24},{16,0},{24,8},{1,17},{9,25},{17,1},{25,9},{2,18},{10... | collective-permute-start | bytes 6291464 | tf_op jit(solution)/shard_map/ppermute | solution.py:421
  (71 other events, 1581.0 us)
Sparse Core Ops, SparseCore 0:
  35.3 85.8 all-reduce.3
  237.6 155.1 all-reduce.5

commit v2 on v1

v2 whole, which is shorter than its diff:
```python
import functools
import math

import jax
import jax.numpy as jnp
import numpy as np
from jax import lax
from jax.experimental import pallas as pl
from jax.experimental.pallas import tpu as pltpu
from jax.sharding import PartitionSpec as P

DEPTHS = 2


depth_step = 16.0
omega_unit = 0.045
lanes = 128
digits = 16
sub = 8
vmem_bytes = 60 * 1024 * 1024


def split_pair(table):
    high = table.astype(jnp.bfloat16)
    low = (table - high.astype(np.float64)).astype(jnp.bfloat16)
    return high, low


@functools.lru_cache(None)
def right_table(orient):
    index = np.arange(lanes)
    angle = orient * 2.0 * np.pi * (np.outer(index, index) % lanes) / lanes
    c, s = np.cos(angle), np.sin(angle)
    high, low = split_pair(np.block([[c, s], [-s, c]]))
    return np.concatenate([high, high, low], axis=0)


@functools.lru_cache(None)
def twiddle_table(length, orient):
    turns = np.outer(np.arange(digits), np.arange(lanes)) % length
    angle = orient * 2.0 * np.pi * turns / length
    return np.stack([np.cos(angle), np.sin(angle)]).astype(np.float32)


@functools.lru_cache(None)
def left_table(length, orient):
    index = np.arange(lanes)
    digit = np.arange(digits)
    turns = (digits * index[None, :, None] * index[None, None, :]
             + digit[:, None, None] * index[None, None, :]) % length
    if orient > 0:
        turns = np.swapaxes(turns, 1, 2)
    angle = orient * 2.0 * np.pi * turns / length
    c, s = np.cos(angle), np.sin(angle)
    full = np.concatenate([np.concatenate([c, -s], 2), np.concatenate([s, c], 2)], 1)
    high, low = split_pair(full)
    return np.concatenate([high, low], axis=2)


def four(a, b, c, d, orient):
    (ar, ai), (br, bi), (cr, ci), (dr, di) = a, b, c, d
    pr, pi = ar + cr, ai + ci
    mr, mi = ar - cr, ai - ci
    qr, qi = br + dr, bi + di
    nr, ni = br - dr, bi - di
    ir, ii = (-ni, nr) if orient > 0 else (ni, -nr)
    return [(pr + qr, pi + qi), (mr + ir, mi + ii), (pr - qr, pi - qi), (mr - ir, mi - ii)]


def turn16(value, step, orient):
    real, imag = value
    step = step % 16
    if step == 0:
        return value
    if step == 4:
        return (-imag, real) if orient > 0 else (imag, -real)
    root = float(np.sqrt(0.5))
    if step == 2:
        if orient > 0:
            return ((real - imag) * root, (real + imag) * root)
        return ((real + imag) * root, (imag - real) * root)
    if step == 6:
        if orient > 0:
            return ((real + imag) * -root, (real - imag) * root)
        return ((imag - real) * root, (real + imag) * -root)
    c = float(np.cos(2.0 * np.pi * step / 16))
    s = float(orient * np.sin(2.0 * np.pi * step / 16))
    return (real * c - imag * s, real * s + imag * c)


def sixteen(values, orient):
    inner = []
    for n2 in range(4):
        part = four(values[n2], values[4 + n2], values[8 + n2], values[12 + n2], orient)
        inner.append([turn16(part[k1], n2 * k1, orient) for k1 in range(4)])
    out = [None] * 16
    for k1 in range(4):
        part = four(inner[0][k1], inner[1][k1], inner[2][k1], inner[3][k1], orient)
        for k2 in range(4):
            out[k1 + 4 * k2] = part[k2]
    return out


def halves(value):
    high = value.astype(jnp.bfloat16)
    low = (value - high.astype(jnp.float32)).astype(jnp.bfloat16)
    return high, low


def times_right(value, table_ref):
    high, low = halves(value)
    wide = jnp.concatenate([high, low, high], axis=1)
    return jnp.dot(wide, table_ref[...], preferred_element_type=jnp.float32)


def times_left(table, value):
    high, low = halves(value)
    tall = jnp.concatenate([high, low, high], axis=0)
    wide = jnp.concatenate([table[:, :2 * lanes], table[:, :2 * lanes], table[:, 2 * lanes:]], axis=1)
    return jnp.dot(wide, tall, preferred_element_type=jnp.float32)


sine_terms = [(-1.0) ** n / math.factorial(2 * n + 1) for n in range(6)]
cosine_terms = [(-1.0) ** n / math.factorial(2 * n) for n in range(7)]
pi_high = float(np.float32(np.pi).astype(jnp.bfloat16))
pi_low = float(np.pi - pi_high)


def series(terms, square):
    total = square * terms[-1] + terms[-2]
    for term in reversed(terms[:-2]):
        total = total * square + term
    return total


def cos_sin(angle):
    turns = jnp.floor(angle * (1.0 / np.pi) + 0.5)
    rest = (angle - turns * pi_high) - turns * pi_low
    flip = 1.0 - 2.0 * (turns - 2.0 * jnp.floor(turns * 0.5))
    square = rest * rest
    return flip * series(cosine_terms, square), flip * rest * series(sine_terms, square)


def product(a, b):
    return (a[0] * b[0] - a[1] * b[1], a[0] * b[1] + a[1] * b[0])


shards = 8


def block_shapes(rows):
    return [jax.ShapeDtypeStruct((2, 2, rows, lanes), jnp.float32)] * shards


def block_specs(rows):
    return [pl.BlockSpec((2, 2, rows, lanes), lambda i: (0, 0, i, 0))] * shards


def swap(array, axis, mask):
    size = lax.axis_size(axis)
    return lax.ppermute(array, axis, [(d, d ^ mask) for d in range(size)])


def after(value, *others):
    return lax.optimization_barrier((value, *others))[0]


def exchange(blocks, gate=None):
    if gate is not None:
        blocks = [blocks[0]] + [after(block, seen) for block, seen in zip(blocks[1:], gate[1:])]
    return [blocks[0]] + [swap(block, "row", k) for k, block in enumerate(blocks) if k]


def to_last_wavenumbers(me, held, table_ref, outs):
    rows = held.shape[1]
    for k in range(shards):
        done = times_right(held[pl.ds((me ^ k) * 2, 2)].reshape(2 * rows, 2 * lanes), table_ref)
        for j in range(2):
            for c in range(2):
                outs[k][j, c] = done[j * rows:(j + 1) * rows, c * lanes:(c + 1) * lanes]


def forward_last_kernel(me_ref, x_ref, twid_ref, table_ref, *rest):
    outs, held = rest[:-1], rest[-1]
    rows = x_ref.shape[1]

    def one(t, carry):
        at = pl.ds(pl.multiple_of(t * sub, sub), sub)
        values = [
            (x_ref[0, at, a * lanes:(a + 1) * lanes], x_ref[1, at, a * lanes:(a + 1) * lanes])
            for a in range(digits)
        ]
        for q, value in enumerate(sixteen(values, -1)):
            if q:
                value = product(value, (twid_ref[0, q:q + 1, :], twid_ref[1, q:q + 1, :]))
            held[q, at, :lanes] = value[0]
            held[q, at, lanes:] = value[1]
        return carry

    lax.fori_loop(0, rows // sub, one, 0)
    to_last_wavenumbers(me_ref[0], held, table_ref, outs)


def light():
    return pl.CostEstimate(flops=1000, bytes_accessed=1000, transcendentals=0)


def smem():
    return pl.BlockSpec(memory_space=pltpu.SMEM)


def whole(table):
    return pl.BlockSpec(table.shape, lambda i: (0,) * table.ndim)


def params():
    return pltpu.CompilerParams(vmem_limit_bytes=vmem_bytes)


def forward_last(me, field, chunk):
    _, rows, cols = field.shape
    twid = twiddle_table(cols, -1)
    table = right_table(-1)
    return pl.pallas_call(
        forward_last_kernel,
        grid=(rows // chunk,),
        in_specs=[
            smem(),
            pl.BlockSpec((2, chunk, cols), lambda i: (0, i, 0)),
            whole(twid),
            whole(table),
        ],
        out_specs=block_specs(chunk),
        out_shape=block_shapes(rows),
        scratch_shapes=[pltpu.VMEM((digits, chunk, 2 * lanes), jnp.float32)],
        compiler_params=params(),
        cost_estimate=light(),
        name="forward_last",
    )(me, field, twid, table)


def middle_kernel(sign, pieces, me_ref, fwd_ref, inv_ref, mr_ref, mi_ref, *rest):
    ins, (held, spare) = rest[:shards], rest[-2:]
    outs = rest[-2 - shards * max(len(pieces), 1):-2]
    me = me_ref[0]
    for j in range(2):
        col = slice(j * lanes, (j + 1) * lanes)
        for k in range(shards):
            for n in range(2):
                spare[(me ^ k) * 2 + n, :, :, col] = ins[k][j, :, n * lanes:(n + 1) * lanes, :]

    def first(t, carry):
        base = pl.multiple_of(t // 2 * sub, sub)
        col = pl.ds(pl.multiple_of(t % 2 * lanes, lanes), lanes)
        at = pl.ds(base, sub)
        values = [(spare[a, 0, at, col], spare[a, 1, at, col]) for a in range(digits)]
        for q, value in enumerate(sixteen(values, -1)):
            held[q, at, col] = value[0]
            held[q, pl.ds(lanes + base, sub), col] = value[1]
        return carry

    lax.fori_loop(0, 2 * lanes // sub, first, 0)

    def second(q, carry):
        spec = times_left(fwd_ref[q], held[q])
        real, imag = spec[:lanes], spec[lanes:]
        mr, mi = mr_ref[q], mi_ref[q]
        if sign > 0:
            moved = (real * mr - imag * mi, real * mi + imag * mr)
        else:
            moved = (real * mr + imag * mi, imag * mr - real * mi)
        held[q] = times_left(inv_ref[q], jnp.concatenate(moved, axis=0))
        return carry

    lax.fori_loop(0, digits, second, 0)

    def third(t, carry):
        base = pl.multiple_of(t // 2 * sub, sub)
        col = pl.ds(pl.multiple_of(t % 2 * lanes, lanes), lanes)
        at = pl.ds(base, sub)
        values = [(held[q, at, col], held[q, pl.ds(lanes + base, sub), col]) for q in range(digits)]
        for a, value in enumerate(sixteen(values, 1)):
            spare[a, 0, at, col] = value[0]
            spare[a, 1, at, col] = value[1]
        return carry

    lax.fori_loop(0, 2 * lanes // sub, third, 0)
    start = 0
    for p, size in enumerate(pieces or (outs[0].shape[2],)):
        at = 0
        while at < size:
            n, r = (start + at) // lanes, (start + at) % lanes
            span = min(size - at, lanes - r)
            for k in range(shards):
                for j in range(2):
                    col = slice(j * lanes, (j + 1) * lanes)
                    value = spare[(me ^ k) * 2 + n, :, r:r + span, col]
                    if pieces:
                        outs[p * shards + k][0, j, :, at:at + span] = value
                    else:
                        outs[k][j, :, at:at + span] = value
            at += span
        start += size


def middle(me, blocks, mult, sign, pieces=(), into=None):
    rows = blocks[0].shape[2]
    length = shards * rows
    fwd, inv = left_table(length, -1), left_table(length, 1)
    operands = [me, fwd, inv, *mult, *blocks]
    in_specs = [smem(), whole(fwd), whole(inv), whole(mult[0]), whole(mult[1])] + block_specs(rows)
    aliases = {}
    out_specs, out_shape = block_specs(rows), block_shapes(rows)
    if pieces:
        out_specs, out_shape = [], []
        for p, (size, fields, place) in enumerate(pieces):
            for k in range(shards):
                out_specs.append(pl.BlockSpec((1, 2, 2, size, lanes), lambda i, place=place: (place, 0, 0, 0, 0)))
                out_shape.append(jax.ShapeDtypeStruct((fields, 2, 2, size, lanes), jnp.float32))
                if place:
                    aliases[len(operands)] = p * shards + k
                    operands.append(into[p][k])
                    in_specs.append(pl.BlockSpec(memory_space=pl.ANY))
    outs = pl.pallas_call(
        functools.partial(middle_kernel, sign, tuple(size for size, _, _ in pieces)),
        grid=(1,),
        in_specs=in_specs,
        out_specs=out_specs,
        out_shape=out_shape,
        input_output_aliases=aliases,
        scratch_shapes=[
            pltpu.VMEM((digits, 2 * lanes, 2 * lanes), jnp.float32),
            pltpu.VMEM((digits, 2, lanes, 2 * lanes), jnp.float32),
        ],
        compiler_params=params(),
        cost_estimate=light(),
        name="middle",
    )(*operands)
    return [outs[p * shards:(p + 1) * shards] for p in range(len(pieces))] if pieces else outs


def space_kernel(sign, onward, keep, image, aliased, *refs):
    refs = list(refs)
    me = refs.pop(0)[0]
    if image == "halves":
        bit = refs.pop(0)[0]
    scale_ref, slow_ref, itwid_ref, itable_ref = refs[:4]
    del refs[:4]
    scale = scale_ref[0]
    ins = refs[:shards]
    del refs[:shards]
    if image:
        other_ref = refs.pop(0)
    if onward:
        twid_ref, table_ref = refs[:2]
        del refs[:2]
    if aliased:
        refs.pop(0)
    field_ref = refs.pop(0) if keep else None
    if onward:
        outs = refs[:shards]
        del refs[:shards]
    if image == "halves":
        mine_ref, theirs_ref, held, image_ref = refs
    elif image:
        image_ref, held = refs
    else:
        (held,) = refs
    rows = held.shape[1]

    for k in range(shards):
        block = ins[k][0] if len(ins[k].shape) == 5 else ins[k][...]
        wide = [jnp.concatenate([block[j, 0], block[j, 1]], axis=1) for j in range(2)]
        done = times_right(jnp.concatenate(wide, axis=0), itable_ref)
        held[pl.ds((me ^ k) * 2, 2)] = done.reshape(2, rows, 2 * lanes)

    def one(t, carry):
        at = pl.ds(pl.multiple_of(t * sub, sub), sub)
        values = []
        for q in range(digits):
            value = (held[q, at, :lanes], held[q, at, lanes:])
            if q:
                value = product(value, (itwid_ref[0, q:q + 1, :], itwid_ref[1, q:q + 1, :]))
            values.append(value)
        values = sixteen(values, 1)
        for a in range(digits):
            real, imag = values[a]
            col = slice(a * lanes, (a + 1) * lanes)
            c, s = cos_sin(scale * slow_ref[0, at, col])
            if sign > 0:
                real, imag = real * c - imag * s, real * s + imag * c
            else:
                real, imag = real * c + imag * s, imag * c - real * s
            if keep:
                field_ref[0, at, col] = real
                field_ref[1, at, col] = imag
            if image:
                image_ref[at, col] = real * other_ref[0, at, col] + imag * other_ref[1, at, col]
            values[a] = (real, imag)
        if onward:
            for q, value in enumerate(sixteen(values, -1)):
                if q:
                    value = product(value, (twid_ref[0, q:q + 1, :], twid_ref[1, q:q + 1, :]))
                held[q, at, :lanes] = value[0]
                held[q, at, lanes:] = value[1]
        return carry

    lax.fori_loop(0, rows // sub, one, 0)
    if image == "halves":
        half = rows // 2
        mine_ref[...] = image_ref[pl.ds(pl.multiple_of(bit * half, sub), half), :]
        theirs_ref[...] = image_ref[pl.ds(pl.multiple_of((1 - bit) * half, sub), half), :]
    if onward:
        to_last_wavenumbers(me, held, table_ref, outs)


def space(me, blocks, scale, slow, z, sign, onward, other=None, keep=True, start=0, into=None, bit=None, chunk=128):
    _, rows, cols = slow.shape
    if isinstance(blocks, tuple):
        blocks, place = blocks
        part = blocks[0].shape[3]
        chunk = min(chunk, part)
        specs = [pl.BlockSpec((1, 2, 2, chunk, lanes), lambda i: (place, 0, 0, i, 0))] * shards
    else:
        part = blocks[0].shape[2]
        specs = block_specs(chunk)
    first = start // chunk
    image = None if other is None else "whole" if bit is None else "halves"
    itwid, itable = twiddle_table(cols, 1), right_table(1)
    field_spec = pl.BlockSpec((2, chunk, cols), lambda i: (0, first + i, 0))
    slow_spec = pl.BlockSpec((1, chunk, cols), lambda i: (z, first + i, 0))
    operands, in_specs = [me], [smem()]
    if image == "halves":
        operands.append(bit)
        in_specs.append(smem())
    operands += [scale, slow, itwid, itable]
    in_specs += [smem(), slow_spec, whole(itwid), whole(itable)]
    operands += blocks
    in_specs += specs
    if image:
        operands.append(other)
        in_specs.append(field_spec)
    if onward:
        tables = [twiddle_table(cols, -1), right_table(-1)]
        operands += tables
        in_specs += [whole(table) for table in tables]
    aliases = {}
    if into is not None:
        aliases = {len(operands): 0}
        operands.append(into)
        in_specs.append(pl.BlockSpec(memory_space=pl.ANY))
    out_specs, out_shape = [], []
    scratch = [pltpu.VMEM((digits, chunk, 2 * lanes), jnp.float32)]
    if keep:
        out_specs.append(field_spec)
        out_shape.append(jax.ShapeDtypeStruct((2, rows, cols), jnp.float32))
    if onward:
        out_specs += block_specs(chunk)
        out_shape += block_shapes(part)
    if image == "whole":
        out_specs.append(pl.BlockSpec((chunk, cols), lambda i: (i, 0)))
        out_shape.append(jax.ShapeDtypeStruct((part, cols), jnp.float32))
    elif image:
        out_specs += [pl.BlockSpec((chunk // 2, cols), lambda i: (i, 0))] * 2
        out_shape += [jax.ShapeDtypeStruct((part // 2, cols), jnp.float32)] * 2
        scratch.append(pltpu.VMEM((chunk, cols), jnp.float32))
    outs = pl.pallas_call(
        functools.partial(space_kernel, sign, onward, keep, image, into is not None),
        grid=(part // chunk,),
        in_specs=in_specs,
        out_specs=out_specs,
        out_shape=out_shape,
        input_output_aliases=aliases,
        scratch_shapes=scratch,
        compiler_params=params(),
        cost_estimate=light(),
        name="space",
    )(*operands)
    outs = list(outs)
    field = outs.pop(0) if keep else None
    onward_blocks = outs[:shards] if onward else None
    if image == "halves":
        term = outs[-2:]
    else:
        term = outs[-1] if image else None
    return field, onward_blocks, term


def put_kernel(halved, bit_ref, *refs):
    refs, out_ref = list(refs[:-2]), refs[-1]
    bit = bit_ref[0]
    at = 0
    for two in halved:
        size = refs[0].shape[0]
        if two:
            mine, theirs = refs.pop(0), refs.pop(0)
            out_ref[0, pl.ds(pl.multiple_of(at + bit * size, sub), size), :] = mine[...]
            out_ref[0, pl.ds(pl.multiple_of(at + (1 - bit) * size, sub), size), :] = theirs[...]
            at += 2 * size
        else:
            out_ref[0, at:at + size, :] = refs.pop(0)[...]
            at += size


def put(image, z, bit, sums):
    flat = []
    for value in sums:
        flat += list(value) if isinstance(value, tuple) else [value]
    return pl.pallas_call(
        functools.partial(put_kernel, [isinstance(value, tuple) for value in sums]),
        grid=(1,),
        in_specs=[smem()] + [whole(v) for v in flat] + [pl.BlockSpec(memory_space=pl.ANY)],
        out_specs=pl.BlockSpec((1,) + image.shape[1:], lambda i: (z, 0, 0)),
        out_shape=jax.ShapeDtypeStruct(image.shape, jnp.float32),
        input_output_aliases={1 + len(flat): 0},
        compiler_params=params(),
        cost_estimate=light(),
        name="put",
    )(bit, *flat, image)


def wavenumber(index, length):
    signed = jnp.where(index < length // 2, index, index - length)
    return 2.0 * jnp.pi * (signed.astype(jnp.float32) / length)


def multiplier(omega, kx_index, ky_index, rows_total, cols_total):
    kx_values = wavenumber(kx_index, rows_total)
    ky_values = wavenumber(ky_index, cols_total)
    phase_q = omega * omega - (kx_values * kx_values + ky_values * ky_values)
    travel = jnp.sqrt(jnp.maximum(phase_q, 0.0))
    decay = jnp.sqrt(jnp.maximum(-phase_q, 0.0))
    damping = jnp.exp(-depth_step * decay) / (rows_total * cols_total)
    return damping * jnp.cos(depth_step * travel), damping * jnp.sin(depth_step * travel)


def slices_of(slowness_store, store_pos):
    mine = lax.axis_index("freq")
    return jnp.stack([
        jnp.where(mine == store_pos[z], slowness_store[0], 0.0).astype(jnp.float32) for z in range(DEPTHS)
    ])


def on_device(source_field, receiver_field, slowness_store, store_pos, freq_index):
    omega = omega_unit * freq_index.astype(jnp.float32)[0]
    rows = source_field.shape[2]
    cols = source_field.shape[3]
    rows_total = rows * 8
    me = lax.axis_index("row").astype(jnp.int32)[None]
    bit = lax.axis_index("freq").astype(jnp.int32)[None] & 1

    grid_shape = (digits, lanes, 2 * lanes)
    kx_index = lax.broadcasted_iota(jnp.int32, grid_shape, 0) + digits * lax.broadcasted_iota(
        jnp.int32, grid_shape, 1
    )
    column = lax.broadcasted_iota(jnp.int32, grid_shape, 2)
    ky_index = lax.axis_index("row") * 2 + column // lanes + digits * (column % lanes)
    def behind(*arrays):
        return after(me, *arrays)

    spec_source = forward_last(me, source_field[0], 128)
    moved_source = exchange(spec_source)
    kept = slices_of(after(slowness_store, moved_source[1]), store_pos)
    slow = lax.psum(kept, "freq")
    mult = multiplier(after(omega, *moved_source), kx_index, ky_index, rows_total, cols)

    scale = (depth_step * omega)[None]

    spec_receiver = forward_last(behind(kept), receiver_field[0], 128)
    moved_receiver = exchange(spec_receiver, moved_source)
    mid_source = middle(behind(spec_receiver[0]), moved_source, mult, -1)
    mid_receiver = middle(behind(mid_source[0]), moved_receiver, mult, 1)
    back_source = exchange(mid_source, moved_receiver)
    back_receiver = exchange(mid_receiver, back_source)
    source_now, spec_source, _ = space(behind(mid_receiver[0]), back_source, scale, slow, 0, -1, True)
    _, spec_receiver, term = space(me, back_receiver, scale, slow, 0, 1, True, other=source_now, keep=False)
    first_image = lax.psum(term, "freq")

    moved_source = exchange(spec_source, back_receiver)
    moved_receiver = exchange(spec_receiver, moved_source)
    sizes = (rows // 2, rows // 4, rows // 4)
    mid_source = middle(
        behind(spec_receiver[0]), moved_source, mult, -1,
        tuple((size, min(n, 1) + 1, 0) for n, size in enumerate(sizes)),
    )
    image = put(jnp.zeros((DEPTHS, rows, cols), jnp.float32), 0, bit, [first_image])
    first_source = exchange(mid_source[0], moved_receiver)
    mid_receiver = middle(
        me, moved_receiver, mult, 1, tuple((size, min(n, 1) + 1, min(n, 1)) for n, size in enumerate(sizes)),
        mid_source,
    )
    source_now = receiver_now = None
    sums = []
    start = 0
    seen = first_source
    for n, size in enumerate(sizes):
        moved = exchange(mid_receiver[n], seen)
        seen = moved
        back_source, back_receiver = ((moved, 0), (moved, 1)) if n else ((first_source, 0), (moved, 0))
        source_now, _, _ = space(
            behind(mid_receiver[-1][0], image) if n == 0 else me, back_source, scale, slow, 1, -1, False, start=start, into=source_now
        )
        receiver_now, _, term = space(
            me, back_receiver, scale, slow, 1, 1, False, other=source_now, start=start, into=receiver_now, bit=bit
        )
        start += size
        mine, theirs = term
        mine = mine + swap(theirs, "freq", 1)
        mine = mine + swap(mine, "freq", 2)
        sums.append((mine, swap(mine, "freq", 1)))
    return put(image, 1, bit, sums), source_now[None], receiver_now[None]


def plain_step(field, mult_real, mult_imag):
    def table(length, orient):
        index = lax.broadcasted_iota(jnp.int32, (length, length), 0) * lax.broadcasted_iota(
            jnp.int32, (length, length), 1
        )
        angle = 2.0 * jnp.pi / length * (index % length).astype(jnp.float32)
        return jnp.cos(angle), orient * jnp.sin(angle)

    def along(real, imag, orient, last):
        c, s = table(real.shape[1 if last else 0], orient)
        dot = functools.partial(jnp.matmul, precision=lax.Precision.HIGHEST)
        if last:
            return dot(real, c) - dot(imag, s), dot(real, s) + dot(imag, c)
        return dot(c, real) - dot(s, imag), dot(s, real) + dot(c, imag)

    def trade(pair, split, join):
        both = lax.all_to_all(jnp.stack(pair), "row", split_axis=split, concat_axis=join, tiled=True)
        return both[0], both[1]

    real, imag = along(field[0], field[1], -1.0, True)
    real, imag = trade((real, imag), 2, 1)
    real, imag = along(real, imag, -1.0, False)
    real, imag = product((real, imag), (mult_real, mult_imag))
    real, imag = along(real, imag, 1.0, False)
    real, imag = trade((real, imag), 1, 2)
    return jnp.stack(along(real, imag, 1.0, True))


def on_device_plain(source_field, receiver_field, slowness_store, store_pos, freq_index):
    omega = omega_unit * freq_index.astype(jnp.float32)[0]
    rows = source_field.shape[2]
    cols = source_field.shape[3]
    shards = lax.axis_size("row")
    rows_total = rows * shards
    block = cols // shards
    slow = lax.psum(slices_of(slowness_store, store_pos), "freq")
    kx_index = lax.broadcasted_iota(jnp.int32, (rows_total, block), 0)
    ky_index = lax.broadcasted_iota(jnp.int32, (rows_total, block), 1) + lax.axis_index("row") * block
    mult_real, mult_imag = multiplier(omega, kx_index, ky_index, rows_total, cols)
    source_now, receiver_now = source_field[0], receiver_field[0]
    images = []
    for z in range(DEPTHS):
        angles = depth_step * omega * slow[z]
        lens_cos, lens_sin = jnp.cos(angles), jnp.sin(angles)
        source_now = plain_step(source_now, mult_real, -mult_imag)
        receiver_now = plain_step(receiver_now, mult_real, mult_imag)
        source_now = jnp.stack(product(source_now, (lens_cos, -lens_sin)))
        receiver_now = jnp.stack(product(receiver_now, (lens_cos, lens_sin)))
        images.append(lax.psum(jnp.sum(source_now * receiver_now, axis=0), "freq"))
    return jnp.stack(images), source_now[None], receiver_now[None]


def solution(mesh):
    placed = (
        P("freq", None, "row", None),
        P("freq", None, "row", None),
        P("freq", "row", None),
        P(),
        P("freq"),
    )

    def chosen(source_field, *rest):
        rows, cols = source_field.shape[2:]
        split = lax.axis_size("row")
        length = digits * lanes
        fits = split == shards and lax.axis_size("freq") == 4 and cols == length and rows * split == length
        return (on_device if fits else on_device_plain)(source_field, *rest)

    return jax.shard_map(
        chosen,
        mesh=mesh,
        in_specs=placed,
        out_specs=(
            P(None, "row", None),
            P("freq", None, "row", None),
            P("freq", None, "row", None),
        ),
        check_vma=False,
    )
```

time: 603 us -> 523 us (0.87)
  waiting for transfers between devices: 322 us -> 216 us
  starting transfers between devices: 58.5 us -> 92.9 us
  other arithmetic: 39.9 us -> 17 us
  Pallas kernels: 163 us -> 173 us
    ppermute x58 -> x79, waiting for transfers between devices: 322 us -> 216 us  [swap(): return lax.ppermute(array, axis, [(d, d ^ mask) for d in range(size)])]
    ppermute x58 -> x79, starting transfers between devices: 58.4 us -> 92.8 us  [swap(): return lax.ppermute(array, axis, [(d, d ^ mask) for d in range(size)])]
    another operation x7 -> x1, other arithmetic: 26.3 us -> 2.28 us  [slices_of(): jnp.stack([jnp.where(mine == store_pos[z], slowness_store[0], 0.0).astype...]
    pallas_call x10 -> x16, Pallas kernels: 163 us -> 173 us  [the longest x4 92.5 us: middle(): pl.pallas_call(functools.partial(middle_kernel, sign, tuple((size for siz...]
  transfers between devices with their start and end apart: 60 -> 81, of which waited for: 20 -> 33; matrix products, arithmetic and copies ran while one was open for 6% -> 3% of each run, Pallas kernels for 22% -> 31%
where the time goes in v2:
time: 523 us; the launch traced here: 522 us
  waiting for transfers between devices  216 us (41%)
  Pallas kernels  173 us (33%)
  starting transfers between devices  92.9 us (18%)
  other arithmetic  17 us (3%)
  between operations  16.7 us (3%)
  local copies, waits for them, and re-layouts  6.63 us (1%)
    ppermute x79, waiting for transfers between devices, swap(): return lax.ppermute(array, axis, [(d, d ^ mask) for d in range(size)])  216 us
    ppermute x79, starting transfers between devices, swap(): return lax.ppermute(array, axis, [(d, d ^ mask) for d in range(size)])  92.8 us
    pallas_call x4, Pallas kernels, middle(): pl.pallas_call(functools.partial(middle_kernel, sign, tuple((size for siz...  92.5 us
    pallas_call x8, Pallas kernels, space(): pl.pallas_call(functools.partial(space_kernel, sign, onward, keep, image,...  62 us
    pallas_call x2, Pallas kernels, forward_last(): pl.pallas_call(forward_last_kernel, grid=(rows // chunk,), in_specs=[smem...  12.9 us
    mul x1, other arithmetic, multiplier(): damping * jnp.sin(depth_step * travel)  10.8 us
  transfers between devices with their start and end apart: 81, of which 33 were waited for; matrix products, arithmetic and copies ran while one was open for 3% of the time, Pallas kernels for 31%

profile of v2, /device:TPU:0, one launch (start us, length us, event | category | flops | bytes accessed | tf_op | source)
XLA Modules:
  0.0 522.4 jit_solution(9784505921236970266)
XLA Ops:
  7.2 6.5 %forward_last.2 = (f32[2,2,256,128]{3,2,1,0:T(8,128)}, f32[2,2,256,128]{3,2,1,0:T(8,128)}, f32[2,2,256,128]{3,2,1,0:T(8,128)}, f32[2,2,256,128]{3,2,1,0:T(8,128)...) custom-call(s32[1]{0:T(128)} %bitcast.1.me_ref.refs_0_, ...), custom_call_target="tpu_custom_call" | custom-call | flops 1000 | bytes 1000 | tf_op jit(solution)/shard_map/forward_last/pallas_call | solution.py:224
  26.5 9.1 %collective-permute-done.6.rest_7_ = f32[2,2,256,128]{3,2,1,0:T(8,128)S(1)} collective-permute-done((f32[2,2,256,128]{3,2,1,0:T(8,128)}, f32[2,2,256,128]{3,2,1,0:T(8,128)S(1)}, u32[]{:S(2)}, u32[]{:S(2)}) %collective-permute-start.6) | collective-permute-done | bytes 524320 | tf_op jit(solution)/shard_map/ppermute | solution.py:161
  37.8 6.4 %forward_last.3 = (f32[2,2,256,128]{3,2,1,0:T(8,128)}, f32[2,2,256,128]{3,2,1,0:T(8,128)}, f32[2,2,256,128]{3,2,1,0:T(8,128)}, f32[2,2,256,128]{3,2,1,0:T(8,128)...) custom-call(s32[1]{0:T(128)} %bitcast.1.me_ref.refs_0_, ...), custom_call_target="tpu_custom_call" | custom-call | flops 1000 | bytes 1000 | tf_op jit(solution)/shard_map/forward_last/pallas_call | solution.py:224
  49.1 9.9 %collective-permute-done.1.rest_2_ = f32[2,2,256,128]{3,2,1,0:T(8,128)S(1)} collective-permute-done((f32[2,2,256,128]{3,2,1,0:T(8,128)S(1)}, f32[2,2,256,128]{3,2,1,0:T(8,128)S(1)}, u32[]{:S(2)}, u32[]{:S(2)}) %collective-permute-start.1) | collective-permute-done | bytes 524320 | tf_op jit(solution)/shard_map/ppermute | solution.py:161
  61.1 8.2 %collective-permute-done.2.rest_3_ = f32[2,2,256,128]{3,2,1,0:T(8,128)S(1)} collective-permute-done((f32[2,2,256,128]{3,2,1,0:T(8,128)}, f32[2,2,256,128]{3,2,1,0:T(8,128)S(1)}, u32[]{:S(2)}, u32[]{:S(2)}) %collective-permute-start.2) | collective-permute-done | bytes 524320 | tf_op jit(solution)/shard_map/ppermute | solution.py:161
  73.1 7.5 %collective-permute-done.13.rest_7_ = f32[2,2,256,128]{3,2,1,0:T(8,128)S(1)} collective-permute-done((f32[2,2,256,128]{3,2,1,0:T(8,128)}, f32[2,2,256,128]{3,2,1,0:T(8,128)S(1)}, u32[]{:S(2)}, u32[]{:S(2)}) %collective-permute-start.13) | collective-permute-done | bytes 524320 | tf_op jit(solution)/shard_map/ppermute | solution.py:161
  82.1 10.1 %collective-permute-done.12.rest_6_ = f32[2,2,256,128]{3,2,1,0:T(8,128)S(1)} collective-permute-done((f32[2,2,256,128]{3,2,1,0:T(8,128)}, f32[2,2,256,128]{3,2,1,0:T(8,128)S(1)}, u32[]{:S(2)}, u32[]{:S(2)}) %collective-permute-start.12) | collective-permute-done | bytes 524320 | tf_op jit(solution)/shard_map/ppermute | solution.py:161
  92.2 10.8 %sine_multiply_fusion = (f32[16,128,256]{2,1,0:T(8,128)}, f32[16,128,256]{2,1,0:T(8,128)}) fusion(s32[256]{0:T(256)S(1)} %get-tuple-element.366, s32[256]{0:T(256)S(1)} %get-tuple-element.369, pred[256]{0:T(512)(128)(4,1)S(1)} %get-tuple-element.367, s32[256]{0:T(256)S(1)} %get-tuple-element.365, s32[256]{0:T(256)S(1)} %get-tuple-element.370, ...), kind=kLoop, calls=%fused_computation.11 | loop fusion | flops 14680064 | bytes 4199432 | tf_op jit(solution)/shard_map/mul | solution.py:534
  103.1 23.7 %middle.4 = (f32[2,2,256,128]{3,2,1,0:T(8,128)}, f32[2,2,256,128]{3,2,1,0:T(8,128)}, f32[2,2,256,128]{3,2,1,0:T(8,128)}, f32[2,2,256,128]{3,2,1,0:T(8,128)}, f32...) custom-call(s32[1]{0:T(128)} %bitcast.1.me_ref.refs_0_, ...), custom_call_target="tpu_custom_call" | custom-call | flops 1000 | bytes 1000 | tf_op jit(solution)/shard_map/middle/pallas_call | solution.py:324
  133.2 9.2 %collective-permute-done.26.refs_12_ = f32[2,2,256,128]{3,2,1,0:T(8,128)S(1)} collective-permute-done((f32[2,2,256,128]{3,2,1,0:T(8,128)}, f32[2,2,256,128]{3,2,1,0:T(8,128)S(1)}, u32[]{:S(2)}, u32[]{:S(2)}) %collective-permute-start.26) | collective-permute-done | bytes 524320 | tf_op jit(solution)/shard_map/ppermute | solution.py:161
  143.6 10.4 %collective-permute-done.24.refs_11_ = f32[2,2,256,128]{3,2,1,0:T(8,128)S(1)} collective-permute-done((f32[2,2,256,128]{3,2,1,0:T(8,128)}, f32[2,2,256,128]{3,2,1,0:T(8,128)S(1)}, u32[]{:S(2)}, u32[]{:S(2)}) %collective-permute-start.24) | collective-permute-done | bytes 524320 | tf_op jit(solution)/shard_map/ppermute | solution.py:161
  154.0 22.9 %middle.5 = (f32[2,2,256,128]{3,2,1,0:T(8,128)}, f32[2,2,256,128]{3,2,1,0:T(8,128)}, f32[2,2,256,128]{3,2,1,0:T(8,128)}, f32[2,2,256,128]{3,2,1,0:T(8,128)}, f32...) custom-call(s32[1]{0:T(128)} %bitcast.1.me_ref.refs_0_, ...), custom_call_target="tpu_custom_call" | custom-call | flops 1000 | bytes 1000 | tf_op jit(solution)/shard_map/middle/pallas_call | solution.py:324
  183.2 9.1 %collective-permute-done.27.refs_12_ = f32[2,2,256,128]{3,2,1,0:T(8,128)S(1)} collective-permute-done((f32[2,2,256,128]{3,2,1,0:T(8,128)}, f32[2,2,256,128]{3,2,1,0:T(8,128)S(1)}, u32[]{:S(2)}, u32[]{:S(2)}) %collective-permute-start.27) | collective-permute-done | bytes 524320 | tf_op jit(solution)/shard_map/ppermute | solution.py:161
  194.0 10.1 %collective-permute-done.25.refs_11_ = f32[2,2,256,128]{3,2,1,0:T(8,128)S(1)} collective-permute-done((f32[2,2,256,128]{3,2,1,0:T(8,128)}, f32[2,2,256,128]{3,2,1,0:T(8,128)S(1)}, u32[]{:S(2)}, u32[]{:S(2)}) %collective-permute-start.25) | collective-permute-done | bytes 524320 | tf_op jit(solution)/shard_map/ppermute | solution.py:161
  204.1 14.2 %space.8 = (f32[2,256,2048]{2,1,0:T(8,128)}, f32[2,2,256,128]{3,2,1,0:T(8,128)}, f32[2,2,256,128]{3,2,1,0:T(8,128)}, f32[2,2,256,128]{3,2,1,0:T(8,128)}, f32[2,2...) custom-call(s32[1]{0:T(128)} %bitcast.1.me_ref.refs_0_, ...), custom_call_target="tpu_custom_call" | custom-call | flops 1000 | bytes 1000 | tf_op jit(solution)/shard_map/space/pallas_call | solution.py:467
  221.2 5.4 %collective-permute-done.21.refs_9_ = f32[2,2,256,128]{3,2,1,0:T(8,128)} collective-permute-done((f32[2,2,256,128]{3,2,1,0:T(8,128)}, f32[2,2,256,128]{3,2,1,0:T(8,128)}, u32[]{:S(2)}, u32[]{:S(2)}) %collective-permute-start.21) | collective-permute-done | bytes 524320 | tf_op jit(solution)/shard_map/ppermute | solution.py:161
  230.8 14.5 %space.9 = (f32[2,2,256,128]{3,2,1,0:T(8,128)}, f32[2,2,256,128]{3,2,1,0:T(8,128)}, f32[2,2,256,128]{3,2,1,0:T(8,128)}, f32[2,2,256,128]{3,2,1,0:T(8,128)}, f32[...) custom-call(s32[1]{0:T(128)} %bitcast.1.me_ref.refs_0_, ...), custom_call_target="tpu_custom_call" | custom-call | flops 1000 | bytes 1000 | tf_op jit(solution)/shard_map/space/pallas_call | solution.py:467
  248.8 11.1 %collective-permute-done.36.rest_5_ = f32[2,2,256,128]{3,2,1,0:T(8,128)S(1)} collective-permute-done((f32[2,2,256,128]{3,2,1,0:T(8,128)}, f32[2,2,256,128]{3,2,1,0:T(8,128)S(1)}, u32[]{:S(2)}, u32[]{:S(2)}) %collective-permute-start.36) | collective-permute-done | bytes 524320 | tf_op jit(solution)/shard_map/ppermute | solution.py:161
  262.6 8.9 %collective-permute-done.34.rest_4_ = f32[2,2,256,128]{3,2,1,0:T(8,128)S(1)} collective-permute-done((f32[2,2,256,128]{3,2,1,0:T(8,128)}, f32[2,2,256,128]{3,2,1,0:T(8,128)S(1)}, u32[]{:S(2)}, u32[]{:S(2)}) %collective-permute-start.34) | collective-permute-done | bytes 524320 | tf_op jit(solution)/shard_map/ppermute | solution.py:161
  276.4 5.9 %collective-permute-done.41.rest_7_ = f32[2,2,256,128]{3,2,1,0:T(8,128)S(1)} collective-permute-done((f32[2,2,256,128]{3,2,1,0:T(8,128)}, f32[2,2,256,128]{3,2,1,0:T(8,128)S(1)}, u32[]{:S(2)}, u32[]{:S(2)}) %collective-permute-start.41) | collective-permute-done | bytes 524320 | tf_op jit(solution)/shard_map/ppermute | solution.py:161
  283.9 10.1 %collective-permute-done.39.rest_6_ = f32[2,2,256,128]{3,2,1,0:T(8,128)S(1)} collective-permute-done((f32[2,2,256,128]{3,2,1,0:T(8,128)}, f32[2,2,256,128]{3,2,1,0:T(8,128)S(1)}, u32[]{:S(2)}, u32[]{:S(2)}) %collective-permute-start.39) | collective-permute-done | bytes 524320 | tf_op jit(solution)/shard_map/ppermute | solution.py:161
  294.1 23.3 %middle.6 = (f32[1,2,2,128,128]{4,3,2,1,0:T(8,128)}, f32[1,2,2,128,128]{4,3,2,1,0:T(8,128)}, f32[1,2,2,128,128]{4,3,2,1,0:T(8,128)}, f32[1,2,2,128,128]{4,3,2,1,...) custom-call(s32[1]{0:T(128)} %bitcast.1.me_ref.refs_0_, ...), custom_call_target="tpu_custom_call" | custom-call | flops 1000 | bytes 1000 | tf_op jit(solution)/shard_map/middle/pallas_call | solution.py:324
  333.4 22.7 %middle.7 = (f32[1,2,2,128,128]{4,3,2,1,0:T(8,128)}, f32[1,2,2,128,128]{4,3,2,1,0:T(8,128)}, f32[1,2,2,128,128]{4,3,2,1,0:T(8,128)}, f32[1,2,2,128,128]{4,3,2,1,...) custom-call(s32[1]{0:T(128)} %bitcast.1.me_ref.refs_0_, ...), custom_call_target="tpu_custom_call", output_to_operand_aliasing={{8}: (13, {}), {9}: (14, {}), {10}: (15, {}), {11}: (16, {}... | custom-call | flops 1000 | bytes 1000 | tf_op jit(solution)/shard_map/middle/pallas_call | solution.py:324
  372.2 5.1 collective-permute-done.51.refs_11_
  394.0 6.7 %space.10.refs_14_.refs_13_ = f32[2,256,2048]{2,1,0:T(8,128)} custom-call(s32[1]{0:T(128)} %bitcast.1.me_ref.refs_0_, f32[1]{0:T(128)S(6)} %mul.47.refs_1_.refs_2_, f32[2,256,2048]{2,1,0:T(8,128)} %all-reduce.3.cloned.1.call-done.refs_2_.refs_3_, f32[2,16,128]{2,1,0:T(8,128)} %constant.94.clone.refs_3_.refs_4_, ...), custom_call_target="tpu_custom_call" | custom-call | flops 1000 | bytes 1000 | tf_op jit(solution)/shard_map/space/pallas_call | solution.py:467
  400.7 8.0 %space.11 = (f32[2,256,2048]{2,1,0:T(8,128)}, f32[64,2048]{1,0:T(8,128)}, f32[64,2048]{1,0:T(8,128)}) custom-call(s32[1]{0:T(128)} %bitcast.1.me_ref.refs_0_, s32[1]{0:T(128)} %bitcast.bit_ref.refs_1_, f32[1]{0:T(128)S(6)} %mul.47.refs_1_.refs_2_, f32[2,256,2048]{2,1,0:T(8,128)} %all-reduce.3.cloned.1.call-done.refs_2_.refs_3_, ...), custom_call_target="tpu_custom_call" | custom-call | flops 1000 | bytes 1000 | tf_op jit(solution)/shard_map/space/pallas_call | solution.py:467
  442.4 5.0 space.13
  452.5 5.0 space.15
  459.6 7.4 %collective-permute-done.76 = f32[32,2048]{1,0:T(8,128)S(1)} collective-permute-done((f32[32,2048]{1,0:T(8,128)}, f32[32,2048]{1,0:T(8,128)S(1)}, u32[]{:S(2)}, u32[]{:S(2)}) %collective-permute-start.76) | collective-permute-done | bytes 262176 | tf_op jit(solution)/shard_map/ppermute | solution.py:161
  477.0 11.4 %collective-permute-done.77 = f32[32,2048]{1,0:T(8,128)S(1)} collective-permute-done((f32[32,2048]{1,0:T(8,128)S(1)}, f32[32,2048]{1,0:T(8,128)S(1)}, u32[]{:S(2)}, u32[]{:S(2)}) %collective-permute-start.77) | collective-permute-done | bytes 262176 | tf_op jit(solution)/shard_map/ppermute | solution.py:161
  488.5 5.4 %collective-permute-done.67 = f32[32,2048]{1,0:T(8,128)S(1)} collective-permute-done((f32[32,2048]{1,0:T(8,128)S(1)}, f32[32,2048]{1,0:T(8,128)S(1)}, u32[]{:S(2)}, u32[]{:S(2)}) %collective-permute-start.67) | collective-permute-done | bytes 262176 | tf_op jit(solution)/shard_map/ppermute | solution.py:161
  494.0 12.5 %collective-permute-done.78.refs_5_ = f32[32,2048]{1,0:T(8,128)S(1)} collective-permute-done((f32[32,2048]{1,0:T(8,128)S(1)}, f32[32,2048]{1,0:T(8,128)S(1)}, u32[]{:S(2)}, u32[]{:S(2)}) %collective-permute-start.78) | collective-permute-done | bytes 262176 | tf_op jit(solution)/shard_map/ppermute | solution.py:161
  (305 shorter events, 169.2 us)
Async XLA Ops:
  7.2 196.9 %all-reduce.3.cloned.1.call-start = ((), (), s32[]{:S(2)}) async-start(), calls=%async_computation | async-start | bytes 8388608 | tf_op jit(solution)/shard_map/psum | solution.py:564
  19.3 366.9 %all-reduce.5.cloned.1.call-start = ((), (), s32[]{:S(2)}) async-start(), calls=%async_computation.1 | async-start | bytes 4194304 | tf_op jit(solution)/shard_map/psum | solution.py:577
  24.0 35.0 %collective-permute-start.1 = (f32[2,2,256,128]{3,2,1,0:T(8,128)S(1)}, f32[2,2,256,128]{3,2,1,0:T(8,128)S(1)}, u32[]{:S(2)}, u32[]{:S(2)}) collective-permute-start(f32[2,2,256,128]{3,2,1,0:T(8,128)S(1)} %copy-done.68), channel_id=1, source_target_pairs={{0,2},{1,3},{2,0},{3,1},{4,6},{5,7},{6,4},{7,5},{8,10},{9,11},{10,... | collective-permute-start | bytes 1572872 | tf_op jit(solution)/shard_map/ppermute | solution.py:161
  25.0 44.3 %collective-permute-start.2 = (f32[2,2,256,128]{3,2,1,0:T(8,128)}, f32[2,2,256,128]{3,2,1,0:T(8,128)S(1)}, u32[]{:S(2)}, u32[]{:S(2)}) collective-permute-start(f32[2,2,256,128]{3,2,1,0:T(8,128)} %get-tuple-element.185), channel_id=1, source_target_pairs={{0,3},{1,2},{2,1},{3,0},{4,7},{5,6},{6,5},{7,4},{8,11},{9,10},{10,... | collective-permute-start | bytes 1572872 | tf_op jit(solution)/shard_map/ppermute | solution.py:161
  25.4 43.9 %collective-permute-start.3 = (f32[2,2,256,128]{3,2,1,0:T(8,128)}, f32[2,2,256,128]{3,2,1,0:T(8,128)}, u32[]{:S(2)}, u32[]{:S(2)}) collective-permute-start(f32[2,2,256,128]{3,2,1,0:T(8,128)} %get-tuple-element.186), channel_id=1, source_target_pairs={{0,4},{1,5},{2,6},{3,7},{4,0},{5,1},{6,2},{7,3},{8,12},{9,13},{10,... | collective-permute-start | bytes 1572872 | tf_op jit(solution)/shard_map/ppermute | solution.py:161
  35.6 34.1 %collective-permute-start.4 = (f32[2,2,256,128]{3,2,1,0:T(8,128)S(1)}, f32[2,2,256,128]{3,2,1,0:T(8,128)}, u32[]{:S(2)}, u32[]{:S(2)}) collective-permute-start(f32[2,2,256,128]{3,2,1,0:T(8,128)S(1)} %copy-done.67), channel_id=1, source_target_pairs={{0,5},{1,4},{2,7},{3,6},{4,1},{5,0},{6,3},{7,2},{8,13},{9,12},{10,... | collective-permute-start | bytes 1572872 | tf_op jit(solution)/shard_map/ppermute | solution.py:161
  47.2 33.4 %collective-permute-start.13 = (f32[2,2,256,128]{3,2,1,0:T(8,128)}, f32[2,2,256,128]{3,2,1,0:T(8,128)S(1)}, u32[]{:S(2)}, u32[]{:S(2)}) collective-permute-start(f32[2,2,256,128]{3,2,1,0:T(8,128)} %get-tuple-element.209), channel_id=1, source_target_pairs={{0,7},{1,6},{2,5},{3,4},{4,3},{5,2},{6,1},{7,0},{8,15},{9,14},{10,... | collective-permute-start | bytes 1572872 | tf_op jit(solution)/shard_map/ppermute | solution.py:161
  59.0 33.3 %collective-permute-start.12 = (f32[2,2,256,128]{3,2,1,0:T(8,128)}, f32[2,2,256,128]{3,2,1,0:T(8,128)S(1)}, u32[]{:S(2)}, u32[]{:S(2)}) collective-permute-start(f32[2,2,256,128]{3,2,1,0:T(8,128)} %get-tuple-element.207), channel_id=1, source_target_pairs={{0,6},{1,7},{2,4},{3,5},{4,2},{5,3},{6,0},{7,1},{8,14},{9,15},{10,... | collective-permute-start | bytes 1572872 | tf_op jit(solution)/shard_map/ppermute | solution.py:161
  69.7 57.0 %collective-permute-start.11 = (f32[2,2,256,128]{3,2,1,0:T(8,128)}, f32[2,2,256,128]{3,2,1,0:T(8,128)S(1)}, u32[]{:S(2)}, u32[]{:S(2)}) collective-permute-start(f32[2,2,256,128]{3,2,1,0:T(8,128)} %get-tuple-element.205), channel_id=1, source_target_pairs={{0,5},{1,4},{2,7},{3,6},{4,1},{5,0},{6,3},{7,2},{8,13},{9,12},{10,... | collective-permute-start | bytes 1572872 | tf_op jit(solution)/shard_map/ppermute | solution.py:161
  71.4 58.4 %collective-permute-start.10 = (f32[2,2,256,128]{3,2,1,0:T(8,128)}, f32[2,2,256,128]{3,2,1,0:T(8,128)S(1)}, u32[]{:S(2)}, u32[]{:S(2)}) collective-permute-start(f32[2,2,256,128]{3,2,1,0:T(8,128)} %get-tuple-element.203), channel_id=1, source_target_pairs={{0,4},{1,5},{2,6},{3,7},{4,0},{5,1},{6,2},{7,3},{8,12},{9,13},{10,... | collective-permute-start | bytes 1572872 | tf_op jit(solution)/shard_map/ppermute | solution.py:161
  72.1 57.7 %collective-permute-start.9 = (f32[2,2,256,128]{3,2,1,0:T(8,128)}, f32[2,2,256,128]{3,2,1,0:T(8,128)}, u32[]{:S(2)}, u32[]{:S(2)}) collective-permute-start(f32[2,2,256,128]{3,2,1,0:T(8,128)} %get-tuple-element.201), channel_id=1, source_target_pairs={{0,3},{1,2},{2,1},{3,0},{4,7},{5,6},{6,5},{7,4},{8,11},{9,10},{10,... | collective-permute-start | bytes 1572872 | tf_op jit(solution)/shard_map/ppermute | solution.py:161
  80.6 50.5 %collective-permute-start.8 = (f32[2,2,256,128]{3,2,1,0:T(8,128)}, f32[2,2,256,128]{3,2,1,0:T(8,128)}, u32[]{:S(2)}, u32[]{:S(2)}) collective-permute-start(f32[2,2,256,128]{3,2,1,0:T(8,128)} %get-tuple-element.199), channel_id=1, source_target_pairs={{0,2},{1,3},{2,0},{3,1},{4,6},{5,7},{6,4},{7,5},{8,10},{9,11},{10,... | collective-permute-start | bytes 1572872 | tf_op jit(solution)/shard_map/ppermute | solution.py:161
  92.2 39.6 %collective-permute-start.7 = (f32[2,2,256,128]{3,2,1,0:T(8,128)}, f32[2,2,256,128]{3,2,1,0:T(8,128)}, u32[]{:S(2)}, u32[]{:S(2)}) collective-permute-start(f32[2,2,256,128]{3,2,1,0:T(8,128)} %get-tuple-element.197), channel_id=1, source_target_pairs={{0,1},{1,0},{2,3},{3,2},{4,5},{5,4},{6,7},{7,6},{8,9},{9,8},{10,11... | collective-permute-start | bytes 1572872 | tf_op jit(solution)/shard_map/ppermute | solution.py:161
  129.8 47.1 %collective-permute-start.22 = (f32[2,2,256,128]{3,2,1,0:T(8,128)}, f32[2,2,256,128]{3,2,1,0:T(8,128)S(1)}, u32[]{:S(2)}, u32[]{:S(2)}) collective-permute-start(f32[2,2,256,128]{3,2,1,0:T(8,128)} %get-tuple-element.229), channel_id=1, source_target_pairs={{0,5},{1,4},{2,7},{3,6},{4,1},{5,0},{6,3},{7,2},{8,13},{9,12},{10,... | collective-permute-start | bytes 1572872 | tf_op jit(solution)/shard_map/ppermute | solution.py:161
  131.1 48.6 %collective-permute-start.20 = (f32[2,2,256,128]{3,2,1,0:T(8,128)}, f32[2,2,256,128]{3,2,1,0:T(8,128)S(1)}, u32[]{:S(2)}, u32[]{:S(2)}) collective-permute-start(f32[2,2,256,128]{3,2,1,0:T(8,128)} %get-tuple-element.225), channel_id=1, source_target_pairs={{0,4},{1,5},{2,6},{3,7},{4,0},{5,1},{6,2},{7,3},{8,12},{9,13},{10,... | collective-permute-start | bytes 1572872 | tf_op jit(solution)/shard_map/ppermute | solution.py:161
  131.9 48.1 %collective-permute-start.18 = (f32[2,2,256,128]{3,2,1,0:T(8,128)}, f32[2,2,256,128]{3,2,1,0:T(8,128)S(1)}, u32[]{:S(2)}, u32[]{:S(2)}) collective-permute-start(f32[2,2,256,128]{3,2,1,0:T(8,128)} %get-tuple-element.221), channel_id=1, source_target_pairs={{0,3},{1,2},{2,1},{3,0},{4,7},{5,6},{6,5},{7,4},{8,11},{9,10},{10,... | collective-permute-start | bytes 1572872 | tf_op jit(solution)/shard_map/ppermute | solution.py:161
  142.4 38.9 %collective-permute-start.16 = (f32[2,2,256,128]{3,2,1,0:T(8,128)}, f32[2,2,256,128]{3,2,1,0:T(8,128)}, u32[]{:S(2)}, u32[]{:S(2)}) collective-permute-start(f32[2,2,256,128]{3,2,1,0:T(8,128)} %get-tuple-element.217), channel_id=1, source_target_pairs={{0,2},{1,3},{2,0},{3,1},{4,6},{5,7},{6,4},{7,5},{8,10},{9,11},{10,... | collective-permute-start | bytes 1572872 | tf_op jit(solution)/shard_map/ppermute | solution.py:161
  180.0 38.3 %collective-permute-start.23 = (f32[2,2,256,128]{3,2,1,0:T(8,128)}, f32[2,2,256,128]{3,2,1,0:T(8,128)S(1)}, u32[]{:S(2)}, u32[]{:S(2)}) collective-permute-start(f32[2,2,256,128]{3,2,1,0:T(8,128)} %get-tuple-element.230), channel_id=1, source_target_pairs={{0,5},{1,4},{2,7},{3,6},{4,1},{5,0},{6,3},{7,2},{8,13},{9,12},{10,... | collective-permute-start | bytes 1572872 | tf_op jit(solution)/shard_map/ppermute | solution.py:161
  181.3 45.2 %collective-permute-start.21 = (f32[2,2,256,128]{3,2,1,0:T(8,128)}, f32[2,2,256,128]{3,2,1,0:T(8,128)}, u32[]{:S(2)}, u32[]{:S(2)}) collective-permute-start(f32[2,2,256,128]{3,2,1,0:T(8,128)} %get-tuple-element.226), channel_id=1, source_target_pairs={{0,4},{1,5},{2,6},{3,7},{4,0},{5,1},{6,2},{7,3},{8,12},{9,13},{10,... | collective-permute-start | bytes 1572872 | tf_op jit(solution)/shard_map/ppermute | solution.py:161
  181.9 47.5 %collective-permute-start.19 = (f32[2,2,256,128]{3,2,1,0:T(8,128)}, f32[2,2,256,128]{3,2,1,0:T(8,128)}, u32[]{:S(2)}, u32[]{:S(2)}) collective-permute-start(f32[2,2,256,128]{3,2,1,0:T(8,128)} %get-tuple-element.222), channel_id=1, source_target_pairs={{0,3},{1,2},{2,1},{3,0},{4,7},{5,6},{6,5},{7,4},{8,11},{9,10},{10,... | collective-permute-start | bytes 1572872 | tf_op jit(solution)/shard_map/ppermute | solution.py:161
  192.4 37.0 %collective-permute-start.17 = (f32[2,2,256,128]{3,2,1,0:T(8,128)}, f32[2,2,256,128]{3,2,1,0:T(8,128)}, u32[]{:S(2)}, u32[]{:S(2)}) collective-permute-start(f32[2,2,256,128]{3,2,1,0:T(8,128)} %get-tuple-element.218), channel_id=1, source_target_pairs={{0,2},{1,3},{2,0},{3,1},{4,6},{5,7},{6,4},{7,5},{8,10},{9,11},{10,... | collective-permute-start | bytes 1572872 | tf_op jit(solution)/shard_map/ppermute | solution.py:161
  229.4 42.1 %collective-permute-start.34 = (f32[2,2,256,128]{3,2,1,0:T(8,128)}, f32[2,2,256,128]{3,2,1,0:T(8,128)S(1)}, u32[]{:S(2)}, u32[]{:S(2)}) collective-permute-start(f32[2,2,256,128]{3,2,1,0:T(8,128)} %get-tuple-element.256), channel_id=1, source_target_pairs={{0,4},{1,5},{2,6},{3,7},{4,0},{5,1},{6,2},{7,3},{8,12},{9,13},{10,... | collective-permute-start | bytes 1572872 | tf_op jit(solution)/shard_map/ppermute | solution.py:161
  274.3 43.2 %collective-permute-start.37 = (f32[2,2,256,128]{3,2,1,0:T(8,128)}, f32[2,2,256,128]{3,2,1,0:T(8,128)S(1)}, u32[]{:S(2)}, u32[]{:S(2)}) collective-permute-start(f32[2,2,256,128]{3,2,1,0:T(8,128)} %get-tuple-element.261), channel_id=1, source_target_pairs={{0,5},{1,4},{2,7},{3,6},{4,1},{5,0},{6,3},{7,2},{8,13},{9,12},{10,... | collective-permute-start | bytes 1572872 | tf_op jit(solution)/shard_map/ppermute | solution.py:161
  275.1 45.2 %collective-permute-start.35 = (f32[2,2,256,128]{3,2,1,0:T(8,128)}, f32[2,2,256,128]{3,2,1,0:T(8,128)S(1)}, u32[]{:S(2)}, u32[]{:S(2)}) collective-permute-start(f32[2,2,256,128]{3,2,1,0:T(8,128)} %get-tuple-element.257), channel_id=1, source_target_pairs={{0,4},{1,5},{2,6},{3,7},{4,0},{5,1},{6,2},{7,3},{8,12},{9,13},{10,... | collective-permute-start | bytes 1572872 | tf_op jit(solution)/shard_map/ppermute | solution.py:161
  275.9 44.6 %collective-permute-start.33 = (f32[2,2,256,128]{3,2,1,0:T(8,128)}, f32[2,2,256,128]{3,2,1,0:T(8,128)}, u32[]{:S(2)}, u32[]{:S(2)}) collective-permute-start(f32[2,2,256,128]{3,2,1,0:T(8,128)} %get-tuple-element.253), channel_id=1, source_target_pairs={{0,3},{1,2},{2,1},{3,0},{4,7},{5,6},{6,5},{7,4},{8,11},{9,10},{10,... | collective-permute-start | bytes 1572872 | tf_op jit(solution)/shard_map/ppermute | solution.py:161
  282.4 39.4 %collective-permute-start.31 = (f32[2,2,256,128]{3,2,1,0:T(8,128)}, f32[2,2,256,128]{3,2,1,0:T(8,128)}, u32[]{:S(2)}, u32[]{:S(2)}) collective-permute-start(f32[2,2,256,128]{3,2,1,0:T(8,128)} %get-tuple-element.249), channel_id=1, source_target_pairs={{0,2},{1,3},{2,0},{3,1},{4,6},{5,7},{6,4},{7,5},{8,10},{9,11},{10,... | collective-permute-start | bytes 1572872 | tf_op jit(solution)/shard_map/ppermute | solution.py:161
  320.5 35.7 %collective-permute-start.50 = (f32[1,2,2,128,128]{4,3,2,1,0:T(8,128)}, f32[1,2,2,128,128]{4,3,2,1,0:T(8,128)S(1)}, u32[]{:S(2)}, u32[]{:S(2)}) collective-permute-start(f32[1,2,2,128,128]{4,3,2,1,0:T(8,128)} %get-tuple-element.307), channel_id=1, source_target_pairs={{0,5},{1,4},{2,7},{3,6},{4,1},{5,0},{6,3},{7,2},{8,13},{9,12},{10,... | collective-permute-start | bytes 786440 | tf_op jit(solution)/shard_map/ppermute | solution.py:161
  321.8 37.3 %collective-permute-start.48 = (f32[1,2,2,128,128]{4,3,2,1,0:T(8,128)}, f32[1,2,2,128,128]{4,3,2,1,0:T(8,128)S(1)}, u32[]{:S(2)}, u32[]{:S(2)}) collective-permute-start(f32[1,2,2,128,128]{4,3,2,1,0:T(8,128)} %get-tuple-element.303), channel_id=1, source_target_pairs={{0,4},{1,5},{2,6},{3,7},{4,0},{5,1},{6,2},{7,3},{8,12},{9,13},{10,... | collective-permute-start | bytes 786440 | tf_op jit(solution)/shard_map/ppermute | solution.py:161
  322.4 36.9 %collective-permute-start.46 = (f32[1,2,2,128,128]{4,3,2,1,0:T(8,128)}, f32[1,2,2,128,128]{4,3,2,1,0:T(8,128)S(1)}, u32[]{:S(2)}, u32[]{:S(2)}) collective-permute-start(f32[1,2,2,128,128]{4,3,2,1,0:T(8,128)} %get-tuple-element.299), channel_id=1, source_target_pairs={{0,3},{1,2},{2,1},{3,0},{4,7},{5,6},{6,5},{7,4},{8,11},{9,10},{10,... | collective-permute-start | bytes 786440 | tf_op jit(solution)/shard_map/ppermute | solution.py:161
  327.3 33.2 %collective-permute-start.44 = (f32[1,2,2,128,128]{4,3,2,1,0:T(8,128)}, f32[1,2,2,128,128]{4,3,2,1,0:T(8,128)S(1)}, u32[]{:S(2)}, u32[]{:S(2)}) collective-permute-start(f32[1,2,2,128,128]{4,3,2,1,0:T(8,128)} %get-tuple-element.295), channel_id=1, source_target_pairs={{0,2},{1,3},{2,0},{3,1},{4,6},{5,7},{6,4},{7,5},{8,10},{9,11},{10,... | collective-permute-start | bytes 786440 | tf_op jit(solution)/shard_map/ppermute | solution.py:161
  435.4 37.9 %collective-permute-start.57 = (f32[64,2048]{1,0:T(8,128)S(1)}, f32[64,2048]{1,0:T(8,128)}, u32[]{:S(2)}, u32[]{:S(2)}) collective-permute-start(f32[64,2048]{1,0:T(8,128)S(1)} %add.54), channel_id=1, source_target_pairs={{0,16},{8,24},{16,0},{24,8},{1,17},{9,25},{17,1},{25,9},{2,18},{10... | collective-permute-start | bytes 1572872 | tf_op jit(solution)/shard_map/ppermute | solution.py:161
  474.5 36.7 %collective-permute-start.58 = (f32[64,2048]{1,0:T(8,128)S(1)}, f32[64,2048]{1,0:T(8,128)S(1)}, u32[]{:S(2)}, u32[]{:S(2)}) collective-permute-start(f32[64,2048]{1,0:T(8,128)S(1)} %add.55.refs_0_), channel_id=1, source_target_pairs={{0,8},{8,0},{16,24},{24,16},{1,9},{9,1},{17,25},{25,17},{2,10},{10... | collective-permute-start | bytes 1572872 | tf_op jit(solution)/shard_map/ppermute | solution.py:161
  (120 other events, 2331.4 us)
Sparse Core Ops, SparseCore 0:
  19.5 157.4 all-reduce.2
  245.5 85.9 all-reduce.4

commit v3 on v2

--- a/solution.py
+++ b/solution.py
@@ -153,7 +153,7 @@
 
 
 def block_specs(rows):
-    return [pl.BlockSpec((2, 2, rows, lanes), lambda i: (0, 0, i, 0))] * shards
+    return [pl.BlockSpec((2, 2, rows, lanes), lambda i, *_: (0, 0, i, 0))] * shards
 
 
 def swap(array, axis, mask):
@@ -210,7 +210,7 @@
 
 
 def whole(table):
-    return pl.BlockSpec(table.shape, lambda i: (0,) * table.ndim)
+    return pl.BlockSpec(table.shape, lambda i, *_: (0,) * table.ndim)
 
 
 def params():
@@ -243,6 +243,32 @@
     ins, (held, spare) = rest[:shards], rest[-2:]
     outs = rest[-2 - shards * max(len(pieces), 1):-2]
     me = me_ref[0]
+    step, steps = pl.program_id(0), digits // fwd_ref.shape[0]
+
+    @pl.when(step == 0)
+    def _():
+        along_first(me, ins, held, spare)
+
+    def second(n, carry):
+        q = step * fwd_ref.shape[0] + n
+        spec = times_left(fwd_ref[n], held[q])
+        real, imag = spec[:lanes], spec[lanes:]
+        mr, mi = mr_ref[n], mi_ref[n]
+        if sign > 0:
+            moved = (real * mr - imag * mi, real * mi + imag * mr)
+        else:
+            moved = (real * mr + imag * mi, imag * mr - real * mi)
+        held[q] = times_left(inv_ref[n], jnp.concatenate(moved, axis=0))
+        return carry
+
+    lax.fori_loop(0, fwd_ref.shape[0], second, 0)
+
+    @pl.when(step == steps - 1)
+    def _():
+        along_last(me, pieces, outs, held, spare)
+
+
+def along_first(me, ins, held, spare):
     for j in range(2):
         col = slice(j * lanes, (j + 1) * lanes)
         for k in range(shards):
@@ -261,19 +287,8 @@
 
     lax.fori_loop(0, 2 * lanes // sub, first, 0)
 
-    def second(q, carry):
-        spec = times_left(fwd_ref[q], held[q])
-        real, imag = spec[:lanes], spec[lanes:]
-        mr, mi = mr_ref[q], mi_ref[q]
-        if sign > 0:
-            moved = (real * mr - imag * mi, real * mi + imag * mr)
-        else:
-            moved = (real * mr + imag * mi, imag * mr - real * mi)
-        held[q] = times_left(inv_ref[q], jnp.concatenate(moved, axis=0))
-        return carry
-
-    lax.fori_loop(0, digits, second, 0)
-
+
+def along_last(me, pieces, outs, held, spare):
     def third(t, carry):
         base = pl.multiple_of(t // 2 * sub, sub)
         col = pl.ds(pl.multiple_of(t % 2 * lanes, lanes), lanes)
@@ -308,9 +323,16 @@
     length = shards * rows
     fwd, inv = left_table(length, -1), left_table(length, 1)
     operands = [me, fwd, inv, *mult, *blocks]
-    in_specs = [smem(), whole(fwd), whole(inv), whole(mult[0]), whole(mult[1])] + block_specs(rows)
+    steps = 4
+
+    def by_step(table):
+        return pl.BlockSpec((digits // steps,) + table.shape[1:], lambda i: (i, 0, 0))
+
+    in_specs = [smem(), by_step(fwd), by_step(inv), by_step(mult[0]), by_step(mult[1])]
+    in_specs += [pl.BlockSpec((2, 2, rows, lanes), lambda i: (0, 0, 0, 0))] * shards
     aliases = {}
-    out_specs, out_shape = block_specs(rows), block_shapes(rows)
+    out_specs = [pl.BlockSpec((2, 2, rows, lanes), lambda i: (0, 0, 0, 0))] * shards
+    out_shape = block_shapes(rows)
     if pieces:
         out_specs, out_shape = [], []
         for p, (size, fields, place) in enumerate(pieces):
@@ -323,7 +345,7 @@
                     in_specs.append(pl.BlockSpec(memory_space=pl.ANY))
     outs = pl.pallas_call(
         functools.partial(middle_kernel, sign, tuple(size for size, _, _ in pieces)),
-        grid=(1,),
+        grid=(steps,),
         in_specs=in_specs,
         out_specs=out_specs,
         out_shape=out_shape,
@@ -340,7 +362,7 @@
 
 
 def space_kernel(sign, onward, keep, image, aliased, *refs):
-    refs = list(refs)
+    refs = list(refs[1:])
     me = refs.pop(0)[0]
     if image == "halves":
         bit = refs.pop(0)[0]
@@ -414,22 +436,22 @@
         to_last_wavenumbers(me, held, table_ref, outs)
 
 
-def space(me, blocks, scale, slow, z, sign, onward, other=None, keep=True, start=0, into=None, bit=None, chunk=128):
+def space(me, blocks, scale, slow, store_pos, z, sign, onward, other=None, keep=True, start=0, into=None, bit=None, chunk=128):
     _, rows, cols = slow.shape
     if isinstance(blocks, tuple):
         blocks, place = blocks
         part = blocks[0].shape[3]
         chunk = min(chunk, part)
-        specs = [pl.BlockSpec((1, 2, 2, chunk, lanes), lambda i: (place, 0, 0, i, 0))] * shards
+        specs = [pl.BlockSpec((1, 2, 2, chunk, lanes), lambda i, *_: (place, 0, 0, i, 0))] * shards
     else:
         part = blocks[0].shape[2]
         specs = block_specs(chunk)
     first = start // chunk
     image = None if other is None else "whole" if bit is None else "halves"
     itwid, itable = twiddle_table(cols, 1), right_table(1)
-    field_spec = pl.BlockSpec((2, chunk, cols), lambda i: (0, first + i, 0))
-    slow_spec = pl.BlockSpec((1, chunk, cols), lambda i: (z, first + i, 0))
-    operands, in_specs = [me], [smem()]
+    field_spec = pl.BlockSpec((2, chunk, cols), lambda i, *_: (0, first + i, 0))
+    slow_spec = pl.BlockSpec((1, chunk, cols), lambda i, at: (at[z], first + i, 0))
+    operands, in_specs = [store_pos, me], [smem()]
     if image == "halves":
         operands.append(bit)
         in_specs.append(smem())
@@ -458,20 +480,23 @@
         out_specs += block_specs(chunk)
         out_shape += block_shapes(part)
     if image == "whole":
-        out_specs.append(pl.BlockSpec((chunk, cols), lambda i: (i, 0)))
+        out_specs.append(pl.BlockSpec((chunk, cols), lambda i, *_: (i, 0)))
         out_shape.append(jax.ShapeDtypeStruct((part, cols), jnp.float32))
     elif image:
-        out_specs += [pl.BlockSpec((chunk // 2, cols), lambda i: (i, 0))] * 2
+        out_specs += [pl.BlockSpec((chunk // 2, cols), lambda i, *_: (i, 0))] * 2
         out_shape += [jax.ShapeDtypeStruct((part // 2, cols), jnp.float32)] * 2
         scratch.append(pltpu.VMEM((chunk, cols), jnp.float32))
     outs = pl.pallas_call(
         functools.partial(space_kernel, sign, onward, keep, image, into is not None),
-        grid=(part // chunk,),
-        in_specs=in_specs,
-        out_specs=out_specs,
+        grid_spec=pltpu.PrefetchScalarGridSpec(
+            num_scalar_prefetch=1,
+            grid=(part // chunk,),
+            in_specs=in_specs,
+            out_specs=out_specs,
+            scratch_shapes=scratch,
+        ),
         out_shape=out_shape,
         input_output_aliases=aliases,
-        scratch_shapes=scratch,
         compiler_params=params(),
         cost_estimate=light(),
         name="space",
@@ -487,7 +512,7 @@
 
 
 def put_kernel(halved, bit_ref, *refs):
-    refs, out_ref = list(refs[:-2]), refs[-1]
+    refs, out_ref = list(refs), refs[-1]
     bit = bit_ref[0]
     at = 0
     for two in halved:
@@ -506,17 +531,27 @@
     flat = []
     for value in sums:
         flat += list(value) if isinstance(value, tuple) else [value]
+    in_specs = [smem()] + [whole(v) for v in flat]
+    operands = [bit, *flat]
+    aliases = {}
+    if isinstance(image, tuple):
+        shape = image
+    else:
+        shape = image.shape
+        aliases = {len(operands): 0}
+        operands.append(image)
+        in_specs.append(pl.BlockSpec(memory_space=pl.ANY))
     return pl.pallas_call(
         functools.partial(put_kernel, [isinstance(value, tuple) for value in sums]),
         grid=(1,),
-        in_specs=[smem()] + [whole(v) for v in flat] + [pl.BlockSpec(memory_space=pl.ANY)],
-        out_specs=pl.BlockSpec((1,) + image.shape[1:], lambda i: (z, 0, 0)),
-        out_shape=jax.ShapeDtypeStruct(image.shape, jnp.float32),
-        input_output_aliases={1 + len(flat): 0},
+        in_specs=in_specs,
+        out_specs=pl.BlockSpec((1,) + shape[1:], lambda i: (z, 0, 0)),
+        out_shape=jax.ShapeDtypeStruct(shape, jnp.float32),
+        input_output_aliases=aliases,
         compiler_params=params(),
         cost_estimate=light(),
         name="put",
-    )(bit, *flat, image)
+    )(*operands)
 
 
 def wavenumber(index, length):
@@ -534,13 +569,6 @@
     return damping * jnp.cos(depth_step * travel), damping * jnp.sin(depth_step * travel)
 
 
-def slices_of(slowness_store, store_pos):
-    mine = lax.axis_index("freq")
-    return jnp.stack([
-        jnp.where(mine == store_pos[z], slowness_store[0], 0.0).astype(jnp.float32) for z in range(DEPTHS)
-    ])
-
-
 def on_device(source_field, receiver_field, slowness_store, store_pos, freq_index):
     omega = omega_unit * freq_index.astype(jnp.float32)[0]
     rows = source_field.shape[2]
@@ -560,20 +588,19 @@
 
     spec_source = forward_last(me, source_field[0], 128)
     moved_source = exchange(spec_source)
-    kept = slices_of(after(slowness_store, moved_source[1]), store_pos)
-    slow = lax.psum(kept, "freq")
+    slow = lax.all_gather(slowness_store, "freq", axis=0, tiled=True)
     mult = multiplier(after(omega, *moved_source), kx_index, ky_index, rows_total, cols)
 
     scale = (depth_step * omega)[None]
 
-    spec_receiver = forward_last(behind(kept), receiver_field[0], 128)
+    spec_receiver = forward_last(behind(moved_source[1]), receiver_field[0], 128)
     moved_receiver = exchange(spec_receiver, moved_source)
     mid_source = middle(behind(spec_receiver[0]), moved_source, mult, -1)
     mid_receiver = middle(behind(mid_source[0]), moved_receiver, mult, 1)
     back_source = exchange(mid_source, moved_receiver)
     back_receiver = exchange(mid_receiver, back_source)
-    source_now, spec_source, _ = space(behind(mid_receiver[0]), back_source, scale, slow, 0, -1, True)
-    _, spec_receiver, term = space(me, back_receiver, scale, slow, 0, 1, True, other=source_now, keep=False)
+    source_now, spec_source, _ = space(behind(mid_receiver[0]), back_source, scale, slow, store_pos, 0, -1, True)
+    _, spec_receiver, term = space(me, back_receiver, scale, slow, store_pos, 0, 1, True, other=source_now, keep=False)
     first_image = lax.psum(term, "freq")
 
     moved_source = exchange(spec_source, back_receiver)
@@ -583,29 +610,42 @@
         behind(spec_receiver[0]), moved_source, mult, -1,
         tuple((size, min(n, 1) + 1, 0) for n, size in enumerate(sizes)),
     )
-    image = put(jnp.zeros((DEPTHS, rows, cols), jnp.float32), 0, bit, [first_image])
-    first_source = exchange(mid_source[0], moved_receiver)
+    image = put((DEPTHS, rows, cols), 0, bit, [first_image])
     mid_receiver = middle(
         me, moved_receiver, mult, 1, tuple((size, min(n, 1) + 1, min(n, 1)) for n, size in enumerate(sizes)),
         mid_source,
     )
+    late = [after(block, mid_receiver[0][0]) for block in mid_source[0][1:3]]
+    first_source = exchange([mid_source[0][0], *late, *mid_source[0][3:]], moved_receiver)
     source_now = receiver_now = None
     sums = []
+    marks = []
     start = 0
     seen = first_source
     for n, size in enumerate(sizes):
-        moved = exchange(mid_receiver[n], seen)
+        blocks = mid_receiver[n]
+        if n == 2:
+            late = [after(block, mark) for block, mark in zip(blocks[1:3], marks[2:0:-1])]
+            blocks = [blocks[0], *late, *[after(block, marks[0]) for block in blocks[3:]]]
+        moved = exchange(blocks, seen)
         seen = moved
         back_source, back_receiver = ((moved, 0), (moved, 1)) if n else ((first_source, 0), (moved, 0))
         source_now, _, _ = space(
-            behind(mid_receiver[-1][0], image) if n == 0 else me, back_source, scale, slow, 1, -1, False, start=start, into=source_now
+            behind(mid_receiver[-1][0], image) if n == 0 else me, back_source, scale, slow, store_pos, 1, -1, False, start=start, into=source_now
         )
         receiver_now, _, term = space(
-            me, back_receiver, scale, slow, 1, 1, False, other=source_now, start=start, into=receiver_now, bit=bit
+            me, back_receiver, scale, slow, store_pos, 1, 1, False, other=source_now, start=start, into=receiver_now,
+            bit=bit if n else None,
         )
         start += size
+        if n == 0:
+            sums.append(lax.psum(after(term, image), "freq"))
+            marks.append(term)
+            continue
         mine, theirs = term
+        marks.append(theirs)
         mine = mine + swap(theirs, "freq", 1)
+        marks.append(mine)
         mine = mine + swap(mine, "freq", 2)
         sums.append((mine, swap(mine, "freq", 1)))
     return put(image, 1, bit, sums), source_now[None], receiver_now[None]
@@ -646,14 +686,14 @@
     shards = lax.axis_size("row")
     rows_total = rows * shards
     block = cols // shards
-    slow = lax.psum(slices_of(slowness_store, store_pos), "freq")
+    slow = lax.all_gather(slowness_store, "freq", axis=0, tiled=True)
     kx_index = lax.broadcasted_iota(jnp.int32, (rows_total, block), 0)
     ky_index = lax.broadcasted_iota(jnp.int32, (rows_total, block), 1) + lax.axis_index("row") * block
     mult_real, mult_imag = multiplier(omega, kx_index, ky_index, rows_total, cols)
     source_now, receiver_now = source_field[0], receiver_field[0]
     images = []
     for z in range(DEPTHS):
-        angles = depth_step * omega * slow[z]
+        angles = depth_step * omega * slow[store_pos[z]]
         lens_cos, lens_sin = jnp.cos(angles), jnp.sin(angles)
         source_now = plain_step(source_now, mult_real, -mult_imag)
         receiver_now = plain_step(receiver_now, mult_real, mult_imag)

time: 523 us -> 496 us (0.948)
  starting transfers between devices: 92.9 us -> 82.5 us
    ppermute x79 -> x76, starting transfers between devices: 92.8 us -> 82.4 us  [swap(): return lax.ppermute(array, axis, [(d, d ^ mask) for d in range(size)])]
    pallas_call x4, Pallas kernels: 92.5 us -> 83 us  [middle(): pl.pallas_call(functools.partial(middle_kernel, sign, tuple((size for siz...]
    ppermute x79 -> x76, waiting for transfers between devices: 216 us -> 212 us  [swap(): return lax.ppermute(array, axis, [(d, d ^ mask) for d in range(size)])]
  transfers between devices with their start and end apart: 81 -> 79, of which waited for: 33 -> 32; matrix products, arithmetic and copies ran while one was open for 3% -> 3% of each run, Pallas kernels for 31% -> 31%
where the time goes in v3:
time: 496 us
  waiting for transfers between devices  213 us (43%)
  Pallas kernels  169 us (34%)
  starting transfers between devices  82.5 us (17%)
  between operations  15.2 us (3%)
  other arithmetic  12.9 us (3%)
    ppermute x76, waiting for transfers between devices, swap(): return lax.ppermute(array, axis, [(d, d ^ mask) for d in range(size)])  212 us
    pallas_call x4, Pallas kernels, middle(): pl.pallas_call(functools.partial(middle_kernel, sign, tuple((size for siz...  83 us
    ppermute x76, starting transfers between devices, swap(): return lax.ppermute(array, axis, [(d, d ^ mask) for d in range(size)])  82.4 us
    pallas_call x8, Pallas kernels, space(): pl.pallas_call(functools.partial(space_kernel, sign, onward, keep, image,...  67.2 us
    pallas_call x2, Pallas kernels, forward_last(): pl.pallas_call(forward_last_kernel, grid=(rows // chunk,), in_specs=[smem...  12.8 us
    mul x1, other arithmetic, multiplier(): damping * jnp.sin(depth_step * travel)  10.8 us
  transfers between devices with their start and end apart: 79, of which 32 were waited for; matrix products, arithmetic and copies ran while one was open for 3% of the time, Pallas kernels for 31%

profile of v3, /device:TPU:0, one launch (start us, length us, event | category | flops | bytes accessed | tf_op | source)
XLA Modules:
  0.0 495.8 jit_solution(12523203928044675281)
XLA Ops:
  7.9 6.4 %forward_last.2 = (f32[2,2,256,128]{3,2,1,0:T(8,128)}, f32[2,2,256,128]{3,2,1,0:T(8,128)}, f32[2,2,256,128]{3,2,1,0:T(8,128)}, f32[2,2,256,128]{3,2,1,0:T(8,128)...) custom-call(s32[1]{0:T(128)} %bitcast.1.me_ref.refs_1_, ...), custom_call_target="tpu_custom_call" | custom-call | flops 1000 | bytes 1000 | tf_op jit(solution)/shard_map/forward_last/pallas_call | solution.py:224
  21.9 9.1 %collective-permute-done.6.rest_7_ = f32[2,2,256,128]{3,2,1,0:T(8,128)S(1)} collective-permute-done((f32[2,2,256,128]{3,2,1,0:T(8,128)}, f32[2,2,256,128]{3,2,1,0:T(8,128)S(1)}, u32[]{:S(2)}, u32[]{:S(2)}) %collective-permute-start.6) | collective-permute-done | bytes 524320 | tf_op jit(solution)/shard_map/ppermute | solution.py:161
  33.2 6.4 %forward_last.3 = (f32[2,2,256,128]{3,2,1,0:T(8,128)}, f32[2,2,256,128]{3,2,1,0:T(8,128)}, f32[2,2,256,128]{3,2,1,0:T(8,128)}, f32[2,2,256,128]{3,2,1,0:T(8,128)...) custom-call(s32[1]{0:T(128)} %bitcast.1.me_ref.refs_1_, ...), custom_call_target="tpu_custom_call" | custom-call | flops 1000 | bytes 1000 | tf_op jit(solution)/shard_map/forward_last/pallas_call | solution.py:224
  44.0 9.5 %collective-permute-done.2.rest_3_ = f32[2,2,256,128]{3,2,1,0:T(8,128)S(1)} collective-permute-done((f32[2,2,256,128]{3,2,1,0:T(8,128)}, f32[2,2,256,128]{3,2,1,0:T(8,128)S(1)}, u32[]{:S(2)}, u32[]{:S(2)}) %collective-permute-start.2) | collective-permute-done | bytes 524320 | tf_op jit(solution)/shard_map/ppermute | solution.py:161
  53.8 11.4 %collective-permute-done.5.rest_6_ = f32[2,2,256,128]{3,2,1,0:T(8,128)} collective-permute-done((f32[2,2,256,128]{3,2,1,0:T(8,128)}, f32[2,2,256,128]{3,2,1,0:T(8,128)}, u32[]{:S(2)}, u32[]{:S(2)}) %collective-permute-start.5) | collective-permute-done | bytes 524320 | tf_op jit(solution)/shard_map/ppermute | solution.py:161
  70.1 5.9 %collective-permute-done.13.rest_7_ = f32[2,2,256,128]{3,2,1,0:T(8,128)S(1)} collective-permute-done((f32[2,2,256,128]{3,2,1,0:T(8,128)}, f32[2,2,256,128]{3,2,1,0:T(8,128)S(1)}, u32[]{:S(2)}, u32[]{:S(2)}) %collective-permute-start.13) | collective-permute-done | bytes 524320 | tf_op jit(solution)/shard_map/ppermute | solution.py:161
  77.2 10.8 %sine_multiply_fusion = (f32[16,128,256]{2,1,0:T(8,128)}, f32[16,128,256]{2,1,0:T(8,128)}) fusion(s32[256]{0:T(256)S(1)} %get-tuple-element.378, s32[256]{0:T(256)S(1)} %get-tuple-element.381, pred[256]{0:T(512)(128)(4,1)S(1)} %get-tuple-element.379, s32[256]{0:T(256)S(1)} %get-tuple-element.377, s32[256]{0:T(256)S(1)} %get-tuple-element.382, ...), kind=kLoop, calls=%fused_computation.10 | loop fusion | flops 14680064 | bytes 4199432 | tf_op jit(solution)/shard_map/mul | solution.py:569
  88.0 20.6 %middle.4 = (f32[2,2,256,128]{3,2,1,0:T(8,128)}, f32[2,2,256,128]{3,2,1,0:T(8,128)}, f32[2,2,256,128]{3,2,1,0:T(8,128)}, f32[2,2,256,128]{3,2,1,0:T(8,128)}, f32...) custom-call(s32[1]{0:T(128)} %bitcast.1.me_ref.refs_1_, ...), custom_call_target="tpu_custom_call" | custom-call | flops 1000 | bytes 1000 | tf_op jit(solution)/shard_map/middle/pallas_call | solution.py:346
  115.0 20.5 %middle.5 = (f32[2,2,256,128]{3,2,1,0:T(8,128)}, f32[2,2,256,128]{3,2,1,0:T(8,128)}, f32[2,2,256,128]{3,2,1,0:T(8,128)}, f32[2,2,256,128]{3,2,1,0:T(8,128)}, f32...) custom-call(s32[1]{0:T(128)} %bitcast.1.me_ref.refs_1_, ...), custom_call_target="tpu_custom_call" | custom-call | flops 1000 | bytes 1000 | tf_op jit(solution)/shard_map/middle/pallas_call | solution.py:346
  136.7 10.8 %collective-permute-done.22.refs_11_ = f32[2,2,256,128]{3,2,1,0:T(8,128)S(1)} collective-permute-done((f32[2,2,256,128]{3,2,1,0:T(8,128)}, f32[2,2,256,128]{3,2,1,0:T(8,128)S(1)}, u32[]{:S(2)}, u32[]{:S(2)}) %collective-permute-start.22) | collective-permute-done | bytes 524320 | tf_op jit(solution)/shard_map/ppermute | solution.py:161
  148.9 10.1 %collective-permute-done.20.refs_10_ = f32[2,2,256,128]{3,2,1,0:T(8,128)S(1)} collective-permute-done((f32[2,2,256,128]{3,2,1,0:T(8,128)}, f32[2,2,256,128]{3,2,1,0:T(8,128)S(1)}, u32[]{:S(2)}, u32[]{:S(2)}) %collective-permute-start.20) | collective-permute-done | bytes 524320 | tf_op jit(solution)/shard_map/ppermute | solution.py:161
  163.5 6.5 %collective-permute-done.27.refs_13_ = f32[2,2,256,128]{3,2,1,0:T(8,128)} collective-permute-done((f32[2,2,256,128]{3,2,1,0:T(8,128)}, f32[2,2,256,128]{3,2,1,0:T(8,128)}, u32[]{:S(2)}, u32[]{:S(2)}) %collective-permute-start.27) | collective-permute-done | bytes 524320 | tf_op jit(solution)/shard_map/ppermute | solution.py:161
  170.3 11.4 %collective-permute-done.25.refs_12_ = f32[2,2,256,128]{3,2,1,0:T(8,128)} collective-permute-done((f32[2,2,256,128]{3,2,1,0:T(8,128)}, f32[2,2,256,128]{3,2,1,0:T(8,128)}, u32[]{:S(2)}, u32[]{:S(2)}) %collective-permute-start.25) | collective-permute-done | bytes 524320 | tf_op jit(solution)/shard_map/ppermute | solution.py:161
  181.8 14.8 %space.8 = (f32[2,256,2048]{2,1,0:T(8,128)}, f32[2,2,256,128]{3,2,1,0:T(8,128)}, f32[2,2,256,128]{3,2,1,0:T(8,128)}, f32[2,2,256,128]{3,2,1,0:T(8,128)}, f32[2,2...) custom-call(s32[4]{0:T(128)} %refs_0_.15, ...), custom_call_target="tpu_custom_call" | custom-call | flops 1000 | bytes 1000 | tf_op jit(solution)/shard_map/space/pallas_call | solution.py:489
  198.2 5.9 %collective-permute-done.21.refs_10_ = f32[2,2,256,128]{3,2,1,0:T(8,128)} collective-permute-done((f32[2,2,256,128]{3,2,1,0:T(8,128)}, f32[2,2,256,128]{3,2,1,0:T(8,128)}, u32[]{:S(2)}, u32[]{:S(2)}) %collective-permute-start.21) | collective-permute-done | bytes 524320 | tf_op jit(solution)/shard_map/ppermute | solution.py:161
  208.6 15.1 %space.9 = (f32[2,2,256,128]{3,2,1,0:T(8,128)}, f32[2,2,256,128]{3,2,1,0:T(8,128)}, f32[2,2,256,128]{3,2,1,0:T(8,128)}, f32[2,2,256,128]{3,2,1,0:T(8,128)}, f32[...) custom-call(s32[4]{0:T(128)} %refs_0_.15, ...), custom_call_target="tpu_custom_call" | custom-call | flops 1000 | bytes 1000 | tf_op jit(solution)/shard_map/space/pallas_call | solution.py:489
  226.6 10.9 %collective-permute-done.36.rest_5_ = f32[2,2,256,128]{3,2,1,0:T(8,128)S(1)} collective-permute-done((f32[2,2,256,128]{3,2,1,0:T(8,128)}, f32[2,2,256,128]{3,2,1,0:T(8,128)S(1)}, u32[]{:S(2)}, u32[]{:S(2)}) %collective-permute-start.36) | collective-permute-done | bytes 524320 | tf_op jit(solution)/shard_map/ppermute | solution.py:161
  238.9 10.1 %collective-permute-done.34.rest_4_ = f32[2,2,256,128]{3,2,1,0:T(8,128)S(1)} collective-permute-done((f32[2,2,256,128]{3,2,1,0:T(8,128)}, f32[2,2,256,128]{3,2,1,0:T(8,128)S(1)}, u32[]{:S(2)}, u32[]{:S(2)}) %collective-permute-start.34) | collective-permute-done | bytes 524320 | tf_op jit(solution)/shard_map/ppermute | solution.py:161
  253.6 6.3 %collective-permute-done.41.rest_7_ = f32[2,2,256,128]{3,2,1,0:T(8,128)S(1)} collective-permute-done((f32[2,2,256,128]{3,2,1,0:T(8,128)}, f32[2,2,256,128]{3,2,1,0:T(8,128)S(1)}, u32[]{:S(2)}, u32[]{:S(2)}) %collective-permute-start.41) | collective-permute-done | bytes 524320 | tf_op jit(solution)/shard_map/ppermute | solution.py:161
  260.2 11.4 %collective-permute-done.39.rest_6_ = f32[2,2,256,128]{3,2,1,0:T(8,128)S(1)} collective-permute-done((f32[2,2,256,128]{3,2,1,0:T(8,128)}, f32[2,2,256,128]{3,2,1,0:T(8,128)S(1)}, u32[]{:S(2)}, u32[]{:S(2)}) %collective-permute-start.39) | collective-permute-done | bytes 524320 | tf_op jit(solution)/shard_map/ppermute | solution.py:161
  271.6 20.8 %middle.6 = (f32[1,2,2,128,128]{4,3,2,1,0:T(8,128)}, f32[1,2,2,128,128]{4,3,2,1,0:T(8,128)}, f32[1,2,2,128,128]{4,3,2,1,0:T(8,128)}, f32[1,2,2,128,128]{4,3,2,1,...) custom-call(s32[1]{0:T(128)} %bitcast.1.me_ref.refs_1_, ...), custom_call_target="tpu_custom_call" | custom-call | flops 1000 | bytes 1000 | tf_op jit(solution)/shard_map/middle/pallas_call | solution.py:346
  298.3 21.1 %middle.7 = (f32[1,2,2,128,128]{4,3,2,1,0:T(8,128)}, f32[1,2,2,128,128]{4,3,2,1,0:T(8,128)}, f32[1,2,2,128,128]{4,3,2,1,0:T(8,128)}, f32[1,2,2,128,128]{4,3,2,1,...) custom-call(s32[1]{0:T(128)} %bitcast.1.me_ref.refs_1_, ...), custom_call_target="tpu_custom_call", output_to_operand_aliasing={{8}: (13, {}), {9}: (14, {}), {10}: (15, {}), {11}: (16, {}... | custom-call | flops 1000 | bytes 1000 | tf_op jit(solution)/shard_map/middle/pallas_call | solution.py:346
  334.1 5.8 %collective-permute-done.53.refs_12_ = f32[1,2,2,128,128]{4,3,2,1,0:T(8,128)S(1)} collective-permute-done((f32[1,2,2,128,128]{4,3,2,1,0:T(8,128)}, f32[1,2,2,128,128]{4,3,2,1,0:T(8,128)S(1)}, u32[]{:S(2)}, u32[]{:S(2)}) %collective-permute-start.53) | collective-permute-done | bytes 262176 | tf_op jit(solution)/shard_map/ppermute | solution.py:161
  356.6 5.8 %collective-permute-done.61.refs_12_.refs_13_ = f32[2,2,2,64,128]{4,3,2,1,0:T(8,128)S(1)} collective-permute-done((f32[2,2,2,64,128]{4,3,2,1,0:T(8,128)}, f32[2,2,2,64,128]{4,3,2,1,0:T(8,128)S(1)}, u32[]{:S(2)}, u32[]{:S(2)}) %collective-permute-start.61) | collective-permute-done | bytes 262176 | tf_op jit(solution)/shard_map/ppermute | solution.py:161
  365.7 7.3 %space.10.refs_14_ = f32[2,256,2048]{2,1,0:T(8,128)} custom-call(s32[4]{0:T(128)} %refs_0_.15, s32[1]{0:T(128)} %bitcast.1.me_ref.refs_1_, f32[1]{0:T(128)S(6)} %mul.47.refs_2_.refs_3_, f32[4,256,2048]{2,1,0:T(8,128)} %all-gather.2.cloned.1.call-done.refs_3_.refs_4_, f32[2,16,128]{2,1,0:T(8,128)} %constant.92.clone.refs_4_.refs_5_, ...), custom_call_target="tpu_custom_call" | custom-call | flops 1000 | bytes 1000 | tf_op jit(solution)/shard_map/space/pallas_call | solution.py:489
  373.1 8.6 %space.11 = (f32[2,256,2048]{2,1,0:T(8,128)}, f32[128,2048]{1,0:T(8,128)}) custom-call(s32[4]{0:T(128)} %refs_0_.15, s32[1]{0:T(128)} %bitcast.1.me_ref.refs_1_, f32[1]{0:T(128)S(6)} %mul.47.refs_2_.refs_3_, f32[4,256,2048]{2,1,0:T(8,128)} %all-gather.2.cloned.1.call-done.refs_3_.refs_4_, f32[2,16,128]{2,1,0:T(8,128)} %constant.92.clone.refs_4_.refs_5_, ...), custom_call_target="tpu_custom_call" | custom-call | flops 1000 | bytes 1000 | tf_op jit(solution)/shard_map/space/pallas_call | solution.py:489
  387.7 5.8 %space.13 = (f32[2,256,2048]{2,1,0:T(8,128)}, f32[32,2048]{1,0:T(8,128)}, f32[32,2048]{1,0:T(8,128)}) custom-call(s32[4]{0:T(128)} %refs_0_.15, s32[1]{0:T(128)} %bitcast.1.me_ref.refs_1_, s32[1]{0:T(128)} %bitcast.bit_ref.refs_2_, f32[1]{0:T(128)S(6)} %mul.47.refs_2_.refs_3_, ...), custom_call_target="tpu_custom_call", output_to_operand_aliasing={{0}: (16, {})} | custom-call | flops 1000 | bytes 1000 | tf_op jit(solution)/shard_map/space/pallas_call | solution.py:489
  427.6 5.6 %space.15 = (f32[2,256,2048]{2,1,0:T(8,128)}, f32[32,2048]{1,0:T(8,128)}, f32[32,2048]{1,0:T(8,128)}) custom-call(s32[4]{0:T(128)} %refs_0_.15, s32[1]{0:T(128)} %bitcast.1.me_ref.refs_1_, s32[1]{0:T(128)} %bitcast.bit_ref.refs_2_, f32[1]{0:T(128)S(6)} %mul.47.refs_2_.refs_3_, ...), custom_call_target="tpu_custom_call", output_to_operand_aliasing={{0}: (16, {})} | custom-call | flops 1000 | bytes 1000 | tf_op jit(solution)/shard_map/space/pallas_call | solution.py:489
  436.3 16.2 %collective-permute-done.73 = f32[32,2048]{1,0:T(8,128)S(1)} collective-permute-done((f32[32,2048]{1,0:T(8,128)}, f32[32,2048]{1,0:T(8,128)S(1)}, u32[]{:S(2)}, u32[]{:S(2)}) %collective-permute-start.73) | collective-permute-done | bytes 262176 | tf_op jit(solution)/shard_map/ppermute | solution.py:161
  453.6 9.7 %collective-permute-start.65 = (f32[32,2048]{1,0:T(8,128)S(1)}, f32[32,2048]{1,0:T(8,128)S(1)}, u32[]{:S(2)}, u32[]{:S(2)}) collective-permute-start(f32[32,2048]{1,0:T(8,128)S(1)} %add.49.refs_1_), channel_id=1, source_target_pairs={{0,8},{8,0},{16,24},{24,16},{1,9},{9,1},{17,25},{25,17},{2,10},{10... | collective-permute-start | bytes 786440 | tf_op jit(solution)/shard_map/ppermute | solution.py:161
  463.4 14.5 %collective-permute-done.74 = f32[32,2048]{1,0:T(8,128)S(1)} collective-permute-done((f32[32,2048]{1,0:T(8,128)S(1)}, f32[32,2048]{1,0:T(8,128)S(1)}, u32[]{:S(2)}, u32[]{:S(2)}) %collective-permute-start.74) | collective-permute-done | bytes 262176 | tf_op jit(solution)/shard_map/ppermute | solution.py:161
  478.4 7.2 %collective-permute-done.75.refs_4_ = f32[32,2048]{1,0:T(8,128)S(1)} collective-permute-done((f32[32,2048]{1,0:T(8,128)S(1)}, f32[32,2048]{1,0:T(8,128)S(1)}, u32[]{:S(2)}, u32[]{:S(2)}) %collective-permute-start.75) | collective-permute-done | bytes 262176 | tf_op jit(solution)/shard_map/ppermute | solution.py:161
  (276 shorter events, 138.2 us)
Async XLA Ops:
  7.2 174.6 %all-gather.2.cloned.1.call-start = ((), (), s32[]{:S(2)}) async-start(), calls=%async_computation | async-start | bytes 10485760 | tf_op jit(solution)/shard_map/all_gather | solution.py:591
  7.9 354.7 %all-reduce.3.cloned.1.call-start = ((), (), s32[]{:S(2)}) async-start(), calls=%async_computation.1 | async-start | bytes 4194304 | tf_op jit(solution)/shard_map/psum | solution.py:604
  18.9 34.6 %collective-permute-start.2 = (f32[2,2,256,128]{3,2,1,0:T(8,128)}, f32[2,2,256,128]{3,2,1,0:T(8,128)S(1)}, u32[]{:S(2)}, u32[]{:S(2)}) collective-permute-start(f32[2,2,256,128]{3,2,1,0:T(8,128)} %get-tuple-element.192), channel_id=1, source_target_pairs={{0,3},{1,2},{2,1},{3,0},{4,7},{5,6},{6,5},{7,4},{8,11},{9,10},{10,... | collective-permute-start | bytes 1572872 | tf_op jit(solution)/shard_map/ppermute | solution.py:161
  19.8 33.7 %collective-permute-start.3 = (f32[2,2,256,128]{3,2,1,0:T(8,128)}, f32[2,2,256,128]{3,2,1,0:T(8,128)S(1)}, u32[]{:S(2)}, u32[]{:S(2)}) collective-permute-start(f32[2,2,256,128]{3,2,1,0:T(8,128)} %get-tuple-element.193), channel_id=1, source_target_pairs={{0,4},{1,5},{2,6},{3,7},{4,0},{5,1},{6,2},{7,3},{8,12},{9,13},{10,... | collective-permute-start | bytes 1572872 | tf_op jit(solution)/shard_map/ppermute | solution.py:161
  20.3 33.5 %collective-permute-start.4 = (f32[2,2,256,128]{3,2,1,0:T(8,128)}, f32[2,2,256,128]{3,2,1,0:T(8,128)}, u32[]{:S(2)}, u32[]{:S(2)}) collective-permute-start(f32[2,2,256,128]{3,2,1,0:T(8,128)} %get-tuple-element.194), channel_id=1, source_target_pairs={{0,5},{1,4},{2,7},{3,6},{4,1},{5,0},{6,3},{7,2},{8,13},{9,12},{10,... | collective-permute-start | bytes 1572872 | tf_op jit(solution)/shard_map/ppermute | solution.py:161
  31.0 34.2 %collective-permute-start.5 = (f32[2,2,256,128]{3,2,1,0:T(8,128)}, f32[2,2,256,128]{3,2,1,0:T(8,128)}, u32[]{:S(2)}, u32[]{:S(2)}) collective-permute-start(f32[2,2,256,128]{3,2,1,0:T(8,128)} %get-tuple-element.195), channel_id=1, source_target_pairs={{0,6},{1,7},{2,4},{3,5},{4,2},{5,3},{6,0},{7,1},{8,14},{9,15},{10,... | collective-permute-start | bytes 1572872 | tf_op jit(solution)/shard_map/ppermute | solution.py:161
  43.1 32.9 %collective-permute-start.13 = (f32[2,2,256,128]{3,2,1,0:T(8,128)}, f32[2,2,256,128]{3,2,1,0:T(8,128)S(1)}, u32[]{:S(2)}, u32[]{:S(2)}) collective-permute-start(f32[2,2,256,128]{3,2,1,0:T(8,128)} %get-tuple-element.216), channel_id=1, source_target_pairs={{0,7},{1,6},{2,5},{3,4},{4,3},{5,2},{6,1},{7,0},{8,15},{9,14},{10,... | collective-permute-start | bytes 1572872 | tf_op jit(solution)/shard_map/ppermute | solution.py:161
  65.2 43.5 %collective-permute-start.12 = (f32[2,2,256,128]{3,2,1,0:T(8,128)}, f32[2,2,256,128]{3,2,1,0:T(8,128)S(1)}, u32[]{:S(2)}, u32[]{:S(2)}) collective-permute-start(f32[2,2,256,128]{3,2,1,0:T(8,128)} %get-tuple-element.214), channel_id=1, source_target_pairs={{0,6},{1,7},{2,4},{3,5},{4,2},{5,3},{6,0},{7,1},{8,14},{9,15},{10,... | collective-permute-start | bytes 1572872 | tf_op jit(solution)/shard_map/ppermute | solution.py:161
  68.1 41.7 %collective-permute-start.11 = (f32[2,2,256,128]{3,2,1,0:T(8,128)}, f32[2,2,256,128]{3,2,1,0:T(8,128)S(1)}, u32[]{:S(2)}, u32[]{:S(2)}) collective-permute-start(f32[2,2,256,128]{3,2,1,0:T(8,128)} %get-tuple-element.212), channel_id=1, source_target_pairs={{0,5},{1,4},{2,7},{3,6},{4,1},{5,0},{6,3},{7,2},{8,13},{9,12},{10,... | collective-permute-start | bytes 1572872 | tf_op jit(solution)/shard_map/ppermute | solution.py:161
  68.1 42.9 %collective-permute-start.10 = (f32[2,2,256,128]{3,2,1,0:T(8,128)}, f32[2,2,256,128]{3,2,1,0:T(8,128)S(1)}, u32[]{:S(2)}, u32[]{:S(2)}) collective-permute-start(f32[2,2,256,128]{3,2,1,0:T(8,128)} %get-tuple-element.210), channel_id=1, source_target_pairs={{0,4},{1,5},{2,6},{3,7},{4,0},{5,1},{6,2},{7,3},{8,12},{9,13},{10,... | collective-permute-start | bytes 1572872 | tf_op jit(solution)/shard_map/ppermute | solution.py:161
  68.6 43.8 %collective-permute-start.9 = (f32[2,2,256,128]{3,2,1,0:T(8,128)}, f32[2,2,256,128]{3,2,1,0:T(8,128)}, u32[]{:S(2)}, u32[]{:S(2)}) collective-permute-start(f32[2,2,256,128]{3,2,1,0:T(8,128)} %get-tuple-element.208), channel_id=1, source_target_pairs={{0,3},{1,2},{2,1},{3,0},{4,7},{5,6},{6,5},{7,4},{8,11},{9,10},{10,... | collective-permute-start | bytes 1572872 | tf_op jit(solution)/shard_map/ppermute | solution.py:161
  76.0 37.7 %collective-permute-start.8 = (f32[2,2,256,128]{3,2,1,0:T(8,128)}, f32[2,2,256,128]{3,2,1,0:T(8,128)}, u32[]{:S(2)}, u32[]{:S(2)}) collective-permute-start(f32[2,2,256,128]{3,2,1,0:T(8,128)} %get-tuple-element.206), channel_id=1, source_target_pairs={{0,2},{1,3},{2,0},{3,1},{4,6},{5,7},{6,4},{7,5},{8,10},{9,11},{10,... | collective-permute-start | bytes 1572872 | tf_op jit(solution)/shard_map/ppermute | solution.py:161
  112.4 35.1 %collective-permute-start.22 = (f32[2,2,256,128]{3,2,1,0:T(8,128)}, f32[2,2,256,128]{3,2,1,0:T(8,128)S(1)}, u32[]{:S(2)}, u32[]{:S(2)}) collective-permute-start(f32[2,2,256,128]{3,2,1,0:T(8,128)} %get-tuple-element.236), channel_id=1, source_target_pairs={{0,5},{1,4},{2,7},{3,6},{4,1},{5,0},{6,3},{7,2},{8,13},{9,12},{10,... | collective-permute-start | bytes 1572872 | tf_op jit(solution)/shard_map/ppermute | solution.py:161
  113.7 45.3 %collective-permute-start.20 = (f32[2,2,256,128]{3,2,1,0:T(8,128)}, f32[2,2,256,128]{3,2,1,0:T(8,128)S(1)}, u32[]{:S(2)}, u32[]{:S(2)}) collective-permute-start(f32[2,2,256,128]{3,2,1,0:T(8,128)} %get-tuple-element.232), channel_id=1, source_target_pairs={{0,4},{1,5},{2,6},{3,7},{4,0},{5,1},{6,2},{7,3},{8,12},{9,13},{10,... | collective-permute-start | bytes 1572872 | tf_op jit(solution)/shard_map/ppermute | solution.py:161
  114.2 46.3 %collective-permute-start.18 = (f32[2,2,256,128]{3,2,1,0:T(8,128)}, f32[2,2,256,128]{3,2,1,0:T(8,128)S(1)}, u32[]{:S(2)}, u32[]{:S(2)}) collective-permute-start(f32[2,2,256,128]{3,2,1,0:T(8,128)} %get-tuple-element.228), channel_id=1, source_target_pairs={{0,3},{1,2},{2,1},{3,0},{4,7},{5,6},{6,5},{7,4},{8,11},{9,10},{10,... | collective-permute-start | bytes 1572872 | tf_op jit(solution)/shard_map/ppermute | solution.py:161
  160.5 36.0 %collective-permute-start.23 = (f32[2,2,256,128]{3,2,1,0:T(8,128)}, f32[2,2,256,128]{3,2,1,0:T(8,128)}, u32[]{:S(2)}, u32[]{:S(2)}) collective-permute-start(f32[2,2,256,128]{3,2,1,0:T(8,128)} %get-tuple-element.237), channel_id=1, source_target_pairs={{0,5},{1,4},{2,7},{3,6},{4,1},{5,0},{6,3},{7,2},{8,13},{9,12},{10,... | collective-permute-start | bytes 1572872 | tf_op jit(solution)/shard_map/ppermute | solution.py:161
  160.6 43.5 %collective-permute-start.21 = (f32[2,2,256,128]{3,2,1,0:T(8,128)}, f32[2,2,256,128]{3,2,1,0:T(8,128)}, u32[]{:S(2)}, u32[]{:S(2)}) collective-permute-start(f32[2,2,256,128]{3,2,1,0:T(8,128)} %get-tuple-element.233), channel_id=1, source_target_pairs={{0,4},{1,5},{2,6},{3,7},{4,0},{5,1},{6,2},{7,3},{8,12},{9,13},{10,... | collective-permute-start | bytes 1572872 | tf_op jit(solution)/shard_map/ppermute | solution.py:161
  162.1 43.6 %collective-permute-start.19 = (f32[2,2,256,128]{3,2,1,0:T(8,128)}, f32[2,2,256,128]{3,2,1,0:T(8,128)}, u32[]{:S(2)}, u32[]{:S(2)}) collective-permute-start(f32[2,2,256,128]{3,2,1,0:T(8,128)} %get-tuple-element.229), channel_id=1, source_target_pairs={{0,3},{1,2},{2,1},{3,0},{4,7},{5,6},{6,5},{7,4},{8,11},{9,10},{10,... | collective-permute-start | bytes 1572872 | tf_op jit(solution)/shard_map/ppermute | solution.py:161
  170.0 35.6 %collective-permute-start.17 = (f32[2,2,256,128]{3,2,1,0:T(8,128)}, f32[2,2,256,128]{3,2,1,0:T(8,128)}, u32[]{:S(2)}, u32[]{:S(2)}) collective-permute-start(f32[2,2,256,128]{3,2,1,0:T(8,128)} %get-tuple-element.225), channel_id=1, source_target_pairs={{0,2},{1,3},{2,0},{3,1},{4,6},{5,7},{6,4},{7,5},{8,10},{9,11},{10,... | collective-permute-start | bytes 1572872 | tf_op jit(solution)/shard_map/ppermute | solution.py:161
  196.6 27.1 %collective-permute-start.40 = (f32[2,2,256,128]{3,2,1,0:T(8,128)}, f32[2,2,256,128]{3,2,1,0:T(8,128)S(1)}, u32[]{:S(2)}, u32[]{:S(2)}) collective-permute-start(f32[2,2,256,128]{3,2,1,0:T(8,128)} %get-tuple-element.275), channel_id=1, source_target_pairs={{0,7},{1,6},{2,5},{3,4},{4,3},{5,2},{6,1},{7,0},{8,15},{9,14},{10,... | collective-permute-start | bytes 1572872 | tf_op jit(solution)/shard_map/ppermute | solution.py:161
  205.6 31.9 %collective-permute-start.36 = (f32[2,2,256,128]{3,2,1,0:T(8,128)}, f32[2,2,256,128]{3,2,1,0:T(8,128)S(1)}, u32[]{:S(2)}, u32[]{:S(2)}) collective-permute-start(f32[2,2,256,128]{3,2,1,0:T(8,128)} %get-tuple-element.267), channel_id=1, source_target_pairs={{0,5},{1,4},{2,7},{3,6},{4,1},{5,0},{6,3},{7,2},{8,13},{9,12},{10,... | collective-permute-start | bytes 1572872 | tf_op jit(solution)/shard_map/ppermute | solution.py:161
  205.6 43.3 %collective-permute-start.34 = (f32[2,2,256,128]{3,2,1,0:T(8,128)}, f32[2,2,256,128]{3,2,1,0:T(8,128)S(1)}, u32[]{:S(2)}, u32[]{:S(2)}) collective-permute-start(f32[2,2,256,128]{3,2,1,0:T(8,128)} %get-tuple-element.263), channel_id=1, source_target_pairs={{0,4},{1,5},{2,6},{3,7},{4,0},{5,1},{6,2},{7,3},{8,12},{9,13},{10,... | collective-permute-start | bytes 1572872 | tf_op jit(solution)/shard_map/ppermute | solution.py:161
  207.1 43.5 %collective-permute-start.32 = (f32[2,2,256,128]{3,2,1,0:T(8,128)}, f32[2,2,256,128]{3,2,1,0:T(8,128)}, u32[]{:S(2)}, u32[]{:S(2)}) collective-permute-start(f32[2,2,256,128]{3,2,1,0:T(8,128)} %get-tuple-element.259), channel_id=1, source_target_pairs={{0,3},{1,2},{2,1},{3,0},{4,7},{5,6},{6,5},{7,4},{8,11},{9,10},{10,... | collective-permute-start | bytes 1572872 | tf_op jit(solution)/shard_map/ppermute | solution.py:161
  250.5 227.9 %all-reduce.5.cloned.1.call-start = ((), (), s32[]{:S(2)}) async-start(), calls=%async_computation.2 | async-start | bytes 2097152 | tf_op jit(solution)/shard_map/psum | solution.py:642
  250.6 41.8 %collective-permute-start.37 = (f32[2,2,256,128]{3,2,1,0:T(8,128)}, f32[2,2,256,128]{3,2,1,0:T(8,128)S(1)}, u32[]{:S(2)}, u32[]{:S(2)}) collective-permute-start(f32[2,2,256,128]{3,2,1,0:T(8,128)} %get-tuple-element.268), channel_id=1, source_target_pairs={{0,5},{1,4},{2,7},{3,6},{4,1},{5,0},{6,3},{7,2},{8,13},{9,12},{10,... | collective-permute-start | bytes 1572872 | tf_op jit(solution)/shard_map/ppermute | solution.py:161
  250.7 43.4 %collective-permute-start.35 = (f32[2,2,256,128]{3,2,1,0:T(8,128)}, f32[2,2,256,128]{3,2,1,0:T(8,128)}, u32[]{:S(2)}, u32[]{:S(2)}) collective-permute-start(f32[2,2,256,128]{3,2,1,0:T(8,128)} %get-tuple-element.264), channel_id=1, source_target_pairs={{0,4},{1,5},{2,6},{3,7},{4,0},{5,1},{6,2},{7,3},{8,12},{9,13},{10,... | collective-permute-start | bytes 1572872 | tf_op jit(solution)/shard_map/ppermute | solution.py:161
  252.1 43.4 %collective-permute-start.33 = (f32[2,2,256,128]{3,2,1,0:T(8,128)}, f32[2,2,256,128]{3,2,1,0:T(8,128)}, u32[]{:S(2)}, u32[]{:S(2)}) collective-permute-start(f32[2,2,256,128]{3,2,1,0:T(8,128)} %get-tuple-element.260), channel_id=1, source_target_pairs={{0,3},{1,2},{2,1},{3,0},{4,7},{5,6},{6,5},{7,4},{8,11},{9,10},{10,... | collective-permute-start | bytes 1572872 | tf_op jit(solution)/shard_map/ppermute | solution.py:161
  259.9 36.5 %collective-permute-start.31 = (f32[2,2,256,128]{3,2,1,0:T(8,128)}, f32[2,2,256,128]{3,2,1,0:T(8,128)}, u32[]{:S(2)}, u32[]{:S(2)}) collective-permute-start(f32[2,2,256,128]{3,2,1,0:T(8,128)} %get-tuple-element.256), channel_id=1, source_target_pairs={{0,2},{1,3},{2,0},{3,1},{4,6},{5,7},{6,4},{7,5},{8,10},{9,11},{10,... | collective-permute-start | bytes 1572872 | tf_op jit(solution)/shard_map/ppermute | solution.py:161
  292.4 27.0 %collective-permute-start.54 = (f32[1,2,2,128,128]{4,3,2,1,0:T(8,128)}, f32[1,2,2,128,128]{4,3,2,1,0:T(8,128)S(1)}, u32[]{:S(2)}, u32[]{:S(2)}) collective-permute-start(f32[1,2,2,128,128]{4,3,2,1,0:T(8,128)} %get-tuple-element.324), channel_id=1, source_target_pairs={{0,7},{1,6},{2,5},{3,4},{4,3},{5,2},{6,1},{7,0},{8,15},{9,14},{10,... | collective-permute-start | bytes 786440 | tf_op jit(solution)/shard_map/ppermute | solution.py:161
  350.5 31.2 %collective-permute-start.60 = (f32[2,2,2,64,128]{4,3,2,1,0:T(8,128)}, f32[2,2,2,64,128]{4,3,2,1,0:T(8,128)S(1)}, u32[]{:S(2)}, u32[]{:S(2)}) collective-permute-start(f32[2,2,2,64,128]{4,3,2,1,0:T(8,128)} %get-tuple-element.342), channel_id=1, source_target_pairs={{0,5},{1,4},{2,7},{3,6},{4,1},{5,0},{6,3},{7,2},{8,13},{9,12},{10,... | collective-permute-start | bytes 786440 | tf_op jit(solution)/shard_map/ppermute | solution.py:161
  351.3 30.3 %collective-permute-start.59 = (f32[2,2,2,64,128]{4,3,2,1,0:T(8,128)}, f32[2,2,2,64,128]{4,3,2,1,0:T(8,128)S(1)}, u32[]{:S(2)}, u32[]{:S(2)}) collective-permute-start(f32[2,2,2,64,128]{4,3,2,1,0:T(8,128)} %get-tuple-element.340), channel_id=1, source_target_pairs={{0,4},{1,5},{2,6},{3,7},{4,0},{5,1},{6,2},{7,3},{8,12},{9,13},{10,... | collective-permute-start | bytes 786440 | tf_op jit(solution)/shard_map/ppermute | solution.py:161
  352.0 29.7 %collective-permute-start.58 = (f32[2,2,2,64,128]{4,3,2,1,0:T(8,128)}, f32[2,2,2,64,128]{4,3,2,1,0:T(8,128)S(1)}, u32[]{:S(2)}, u32[]{:S(2)}) collective-permute-start(f32[2,2,2,64,128]{4,3,2,1,0:T(8,128)} %get-tuple-element.338), channel_id=1, source_target_pairs={{0,3},{1,2},{2,1},{3,0},{4,7},{5,6},{6,5},{7,4},{8,11},{9,10},{10,... | collective-permute-start | bytes 786440 | tf_op jit(solution)/shard_map/ppermute | solution.py:161
  (108 other events, 2083.7 us)
Sparse Core Ops, SparseCore 0:
  9.6 152.3 all-gather.1
  250.6 86.7 all-reduce.2
  410.3 68.0 all-reduce.4

commit v4 on v3

--- a/solution.py
+++ b/solution.py
@@ -436,13 +436,14 @@
         to_last_wavenumbers(me, held, table_ref, outs)
 
 
-def space(me, blocks, scale, slow, store_pos, z, sign, onward, other=None, keep=True, start=0, into=None, bit=None, chunk=128):
+def space(me, blocks, scale, slow, store_pos, z, sign, onward, other=None, keep=True, start=0, into=None, bit=None, chunk=128, part=None, skip=0):
     _, rows, cols = slow.shape
     if isinstance(blocks, tuple):
         blocks, place = blocks
-        part = blocks[0].shape[3]
+        part = part or blocks[0].shape[3]
         chunk = min(chunk, part)
-        specs = [pl.BlockSpec((1, 2, 2, chunk, lanes), lambda i, *_: (place, 0, 0, i, 0))] * shards
+        over = skip // chunk
+        specs = [pl.BlockSpec((1, 2, 2, chunk, lanes), lambda i, *_: (place, 0, 0, over + i, 0))] * shards
     else:
         part = blocks[0].shape[2]
         specs = block_specs(chunk)
@@ -605,7 +606,7 @@
 
     moved_source = exchange(spec_source, back_receiver)
     moved_receiver = exchange(spec_receiver, moved_source)
-    sizes = (rows // 2, rows // 4, rows // 4)
+    sizes = (rows // 2, rows // 2)
     mid_source = middle(
         behind(spec_receiver[0]), moved_source, mult, -1,
         tuple((size, min(n, 1) + 1, 0) for n, size in enumerate(sizes)),
@@ -617,38 +618,49 @@
     )
     late = [after(block, mid_receiver[0][0]) for block in mid_source[0][1:3]]
     first_source = exchange([mid_source[0][0], *late, *mid_source[0][3:]], moved_receiver)
-    source_now = receiver_now = None
-    sums = []
-    marks = []
-    start = 0
-    seen = first_source
-    for n, size in enumerate(sizes):
-        blocks = mid_receiver[n]
-        if n == 2:
-            late = [after(block, mark) for block, mark in zip(blocks[1:3], marks[2:0:-1])]
-            blocks = [blocks[0], *late, *[after(block, marks[0]) for block in blocks[3:]]]
-        moved = exchange(blocks, seen)
-        seen = moved
-        back_source, back_receiver = ((moved, 0), (moved, 1)) if n else ((first_source, 0), (moved, 0))
+    moved = exchange(mid_receiver[0], first_source)
+
+    def finish(tie, back_source, back_receiver, start, source_now, receiver_now, part, skip):
         source_now, _, _ = space(
-            behind(mid_receiver[-1][0], image) if n == 0 else me, back_source, scale, slow, store_pos, 1, -1, False, start=start, into=source_now
+            tie, back_source, scale, slow, store_pos, 1, -1, False, start=start, into=source_now, part=part, skip=skip
         )
         receiver_now, _, term = space(
-            me, back_receiver, scale, slow, store_pos, 1, 1, False, other=source_now, start=start, into=receiver_now,
-            bit=bit if n else None,
+            me, back_receiver, scale, slow, store_pos, 1, 1, False, other=source_now, start=start,
+            into=receiver_now, bit=bit, part=part, skip=skip,
         )
-        start += size
-        if n == 0:
-            sums.append(lax.psum(after(term, image), "freq"))
-            marks.append(term)
-            continue
+        return source_now, receiver_now, term
+
+    def near_sum(term, *marks):
         mine, theirs = term
-        marks.append(theirs)
-        mine = mine + swap(theirs, "freq", 1)
-        marks.append(mine)
-        mine = mine + swap(mine, "freq", 2)
-        sums.append((mine, swap(mine, "freq", 1)))
-    return put(image, 1, bit, sums), source_now[None], receiver_now[None]
+        return mine + swap(after(theirs, *marks) if marks else theirs, "freq", 1)
+
+    def far_sum(value, *marks):
+        value = after(value, *marks) if marks else value
+        return value + swap(value, "freq", 2)
+
+    half, quarter = rows // 2, rows // 4
+    source_now, receiver_now, term = finish(
+        behind(image), (first_source, 0), (moved, 0), 0, None, None, half, 0
+    )
+    blocks = mid_receiver[1]
+    blocks = [blocks[0], *[after(block, term[0]) for block in blocks[1:3]], *blocks[3:]]
+    moved = exchange(blocks, moved)
+    pair = ((moved, 0), (moved, 1))
+    near = [near_sum(term)]
+    far = [far_sum(near[0])]
+    source_now, receiver_now, term = finish(
+        behind(near[0]), *pair, half, source_now, receiver_now, quarter, 0
+    )
+    back = [swap(far[0], "freq", 1)]
+    near.append(near_sum(term))
+    source_now, receiver_now, term = finish(
+        behind(near[0]), *pair, half + quarter, source_now, receiver_now, quarter, quarter
+    )
+    far.append(far_sum(near[1]))
+    near.append(near_sum(term, far[0], near[1]))
+    far.append(far_sum(near[2], back[0]))
+    back += [swap(value, "freq", 1) for value in far[1:]]
+    return put(image, 1, bit, list(zip(far, back))), source_now[None], receiver_now[None]
 
 
 def plain_step(field, mult_real, mult_imag):

time: 496 us -> 481 us (0.970)
  waiting for transfers between devices: 213 us -> 204 us
  starting transfers between devices: 82.5 us -> 74.4 us
    ppermute x76 -> x72, waiting for transfers between devices: 212 us -> 204 us  [swap(): return lax.ppermute(array, axis, [(d, d ^ mask) for d in range(size)])]
    ppermute x76 -> x72, starting transfers between devices: 82.4 us -> 74.3 us  [swap(): return lax.ppermute(array, axis, [(d, d ^ mask) for d in range(size)])]
  transfers between devices with their start and end apart: 79 -> 74, of which waited for: 32 -> 28; matrix products, arithmetic and copies ran while one was open for 3% -> 3% of each run, Pallas kernels for 31% -> 35%
where the time goes in v4:
time: 481 us; the launch traced here: 480 us
  waiting for transfers between devices  204 us (42%)
  Pallas kernels  169 us (35%)
  starting transfers between devices  74.4 us (15%)
  between operations  15.4 us (3%)
  other arithmetic  15.1 us (3%)
    ppermute x72, waiting for transfers between devices, swap(): return lax.ppermute(array, axis, [(d, d ^ mask) for d in range(size)])  204 us
    pallas_call x4, Pallas kernels, middle(): pl.pallas_call(functools.partial(middle_kernel, sign, tuple((size for siz...  83.2 us
    ppermute x72, starting transfers between devices, swap(): return lax.ppermute(array, axis, [(d, d ^ mask) for d in range(size)])  74.3 us
    pallas_call x8, Pallas kernels, space(): pl.pallas_call(functools.partial(space_kernel, sign, onward, keep, image,...  67 us
    pallas_call x2, Pallas kernels, forward_last(): pl.pallas_call(forward_last_kernel, grid=(rows // chunk,), in_specs=[smem...  12.8 us
    mul x1, other arithmetic, multiplier(): damping * jnp.sin(depth_step * travel)  10.8 us
  transfers between devices with their start and end apart: 74, of which 28 were waited for; matrix products, arithmetic and copies ran while one was open for 3% of the time, Pallas kernels for 35%

profile of v4, /device:TPU:0, one launch (start us, length us, event | category | flops | bytes accessed | tf_op | source)
XLA Modules:
  0.0 480.3 jit_solution(2930695748344169709)
XLA Ops:
  7.9 6.4 %forward_last.2 = (f32[2,2,256,128]{3,2,1,0:T(8,128)}, f32[2,2,256,128]{3,2,1,0:T(8,128)}, f32[2,2,256,128]{3,2,1,0:T(8,128)}, f32[2,2,256,128]{3,2,1,0:T(8,128)...) custom-call(s32[1]{0:T(128)} %bitcast.1.me_ref.refs_1_, ...), custom_call_target="tpu_custom_call" | custom-call | flops 1000 | bytes 1000 | tf_op jit(solution)/shard_map/forward_last/pallas_call | solution.py:224
  21.9 9.1 %collective-permute-done.6.rest_7_ = f32[2,2,256,128]{3,2,1,0:T(8,128)S(1)} collective-permute-done((f32[2,2,256,128]{3,2,1,0:T(8,128)}, f32[2,2,256,128]{3,2,1,0:T(8,128)S(1)}, u32[]{:S(2)}, u32[]{:S(2)}) %collective-permute-start.6) | collective-permute-done | bytes 524320 | tf_op jit(solution)/shard_map/ppermute | solution.py:161
  33.2 6.4 %forward_last.3 = (f32[2,2,256,128]{3,2,1,0:T(8,128)}, f32[2,2,256,128]{3,2,1,0:T(8,128)}, f32[2,2,256,128]{3,2,1,0:T(8,128)}, f32[2,2,256,128]{3,2,1,0:T(8,128)...) custom-call(s32[1]{0:T(128)} %bitcast.1.me_ref.refs_1_, ...), custom_call_target="tpu_custom_call" | custom-call | flops 1000 | bytes 1000 | tf_op jit(solution)/shard_map/forward_last/pallas_call | solution.py:224
  44.0 9.5 %collective-permute-done.2.rest_3_ = f32[2,2,256,128]{3,2,1,0:T(8,128)S(1)} collective-permute-done((f32[2,2,256,128]{3,2,1,0:T(8,128)}, f32[2,2,256,128]{3,2,1,0:T(8,128)S(1)}, u32[]{:S(2)}, u32[]{:S(2)}) %collective-permute-start.2) | collective-permute-done | bytes 524320 | tf_op jit(solution)/shard_map/ppermute | solution.py:161
  53.8 11.4 %collective-permute-done.5.rest_6_ = f32[2,2,256,128]{3,2,1,0:T(8,128)} collective-permute-done((f32[2,2,256,128]{3,2,1,0:T(8,128)}, f32[2,2,256,128]{3,2,1,0:T(8,128)}, u32[]{:S(2)}, u32[]{:S(2)}) %collective-permute-start.5) | collective-permute-done | bytes 524320 | tf_op jit(solution)/shard_map/ppermute | solution.py:161
  70.1 5.9 %collective-permute-done.13.rest_7_ = f32[2,2,256,128]{3,2,1,0:T(8,128)S(1)} collective-permute-done((f32[2,2,256,128]{3,2,1,0:T(8,128)}, f32[2,2,256,128]{3,2,1,0:T(8,128)S(1)}, u32[]{:S(2)}, u32[]{:S(2)}) %collective-permute-start.13) | collective-permute-done | bytes 524320 | tf_op jit(solution)/shard_map/ppermute | solution.py:161
  77.2 10.8 %sine_multiply_fusion = (f32[16,128,256]{2,1,0:T(8,128)}, f32[16,128,256]{2,1,0:T(8,128)}) fusion(s32[256]{0:T(256)S(1)} %get-tuple-element.328, s32[256]{0:T(256)S(1)} %get-tuple-element.331, pred[256]{0:T(512)(128)(4,1)S(1)} %get-tuple-element.329, s32[256]{0:T(256)S(1)} %get-tuple-element.327, s32[256]{0:T(256)S(1)} %get-tuple-element.332, ...), kind=kLoop, calls=%fused_computation.10 | loop fusion | flops 14680064 | bytes 4199432 | tf_op jit(solution)/shard_map/mul | solution.py:570
  88.0 20.6 %middle.4 = (f32[2,2,256,128]{3,2,1,0:T(8,128)}, f32[2,2,256,128]{3,2,1,0:T(8,128)}, f32[2,2,256,128]{3,2,1,0:T(8,128)}, f32[2,2,256,128]{3,2,1,0:T(8,128)}, f32...) custom-call(s32[1]{0:T(128)} %bitcast.1.me_ref.refs_1_, ...), custom_call_target="tpu_custom_call" | custom-call | flops 1000 | bytes 1000 | tf_op jit(solution)/shard_map/middle/pallas_call | solution.py:346
  114.4 10.5 %collective-permute-done.26.refs_13_ = f32[2,2,256,128]{3,2,1,0:T(8,128)S(1)} collective-permute-done((f32[2,2,256,128]{3,2,1,0:T(8,128)}, f32[2,2,256,128]{3,2,1,0:T(8,128)S(1)}, u32[]{:S(2)}, u32[]{:S(2)}) %collective-permute-start.26) | collective-permute-done | bytes 524320 | tf_op jit(solution)/shard_map/ppermute | solution.py:161
  125.2 11.4 %collective-permute-done.24.refs_12_ = f32[2,2,256,128]{3,2,1,0:T(8,128)S(1)} collective-permute-done((f32[2,2,256,128]{3,2,1,0:T(8,128)}, f32[2,2,256,128]{3,2,1,0:T(8,128)S(1)}, u32[]{:S(2)}, u32[]{:S(2)}) %collective-permute-start.24) | collective-permute-done | bytes 524320 | tf_op jit(solution)/shard_map/ppermute | solution.py:161
  136.6 20.7 %middle.5 = (f32[2,2,256,128]{3,2,1,0:T(8,128)}, f32[2,2,256,128]{3,2,1,0:T(8,128)}, f32[2,2,256,128]{3,2,1,0:T(8,128)}, f32[2,2,256,128]{3,2,1,0:T(8,128)}, f32...) custom-call(s32[1]{0:T(128)} %bitcast.1.me_ref.refs_1_, ...), custom_call_target="tpu_custom_call" | custom-call | flops 1000 | bytes 1000 | tf_op jit(solution)/shard_map/middle/pallas_call | solution.py:346
  163.2 9.2 %collective-permute-done.27.refs_13_ = f32[2,2,256,128]{3,2,1,0:T(8,128)S(1)} collective-permute-done((f32[2,2,256,128]{3,2,1,0:T(8,128)}, f32[2,2,256,128]{3,2,1,0:T(8,128)S(1)}, u32[]{:S(2)}, u32[]{:S(2)}) %collective-permute-start.27) | collective-permute-done | bytes 524320 | tf_op jit(solution)/shard_map/ppermute | solution.py:161
  172.9 11.5 %collective-permute-done.25.refs_12_ = f32[2,2,256,128]{3,2,1,0:T(8,128)S(1)} collective-permute-done((f32[2,2,256,128]{3,2,1,0:T(8,128)}, f32[2,2,256,128]{3,2,1,0:T(8,128)S(1)}, u32[]{:S(2)}, u32[]{:S(2)}) %collective-permute-start.25) | collective-permute-done | bytes 524320 | tf_op jit(solution)/shard_map/ppermute | solution.py:161
  184.5 14.8 %space.8 = (f32[2,256,2048]{2,1,0:T(8,128)}, f32[2,2,256,128]{3,2,1,0:T(8,128)}, f32[2,2,256,128]{3,2,1,0:T(8,128)}, f32[2,2,256,128]{3,2,1,0:T(8,128)}, f32[2,2...) custom-call(s32[4]{0:T(128)} %refs_0_.15, ...), custom_call_target="tpu_custom_call" | custom-call | flops 1000 | bytes 1000 | tf_op jit(solution)/shard_map/space/pallas_call | solution.py:490
  200.9 5.9 %collective-permute-done.21.refs_10_ = f32[2,2,256,128]{3,2,1,0:T(8,128)S(1)} collective-permute-done((f32[2,2,256,128]{3,2,1,0:T(8,128)}, f32[2,2,256,128]{3,2,1,0:T(8,128)S(1)}, u32[]{:S(2)}, u32[]{:S(2)}) %collective-permute-start.21) | collective-permute-done | bytes 524320 | tf_op jit(solution)/shard_map/ppermute | solution.py:161
  209.8 15.1 %space.9 = (f32[2,2,256,128]{3,2,1,0:T(8,128)}, f32[2,2,256,128]{3,2,1,0:T(8,128)}, f32[2,2,256,128]{3,2,1,0:T(8,128)}, f32[2,2,256,128]{3,2,1,0:T(8,128)}, f32[...) custom-call(s32[4]{0:T(128)} %refs_0_.15, ...), custom_call_target="tpu_custom_call" | custom-call | flops 1000 | bytes 1000 | tf_op jit(solution)/shard_map/space/pallas_call | solution.py:490
  229.4 10.7 %collective-permute-done.36.rest_5_ = f32[2,2,256,128]{3,2,1,0:T(8,128)S(1)} collective-permute-done((f32[2,2,256,128]{3,2,1,0:T(8,128)}, f32[2,2,256,128]{3,2,1,0:T(8,128)S(1)}, u32[]{:S(2)}, u32[]{:S(2)}) %collective-permute-start.36) | collective-permute-done | bytes 524320 | tf_op jit(solution)/shard_map/ppermute | solution.py:161
  241.5 10.3 %collective-permute-done.34.rest_4_ = f32[2,2,256,128]{3,2,1,0:T(8,128)S(1)} collective-permute-done((f32[2,2,256,128]{3,2,1,0:T(8,128)}, f32[2,2,256,128]{3,2,1,0:T(8,128)S(1)}, u32[]{:S(2)}, u32[]{:S(2)}) %collective-permute-start.34) | collective-permute-done | bytes 524320 | tf_op jit(solution)/shard_map/ppermute | solution.py:161
  256.3 6.1 %collective-permute-done.41.rest_7_ = f32[2,2,256,128]{3,2,1,0:T(8,128)S(1)} collective-permute-done((f32[2,2,256,128]{3,2,1,0:T(8,128)}, f32[2,2,256,128]{3,2,1,0:T(8,128)S(1)}, u32[]{:S(2)}, u32[]{:S(2)}) %collective-permute-start.41) | collective-permute-done | bytes 524320 | tf_op jit(solution)/shard_map/ppermute | solution.py:161
  263.2 11.2 %collective-permute-done.39.rest_6_ = f32[2,2,256,128]{3,2,1,0:T(8,128)S(1)} collective-permute-done((f32[2,2,256,128]{3,2,1,0:T(8,128)}, f32[2,2,256,128]{3,2,1,0:T(8,128)S(1)}, u32[]{:S(2)}, u32[]{:S(2)}) %collective-permute-start.39) | collective-permute-done | bytes 524320 | tf_op jit(solution)/shard_map/ppermute | solution.py:161
  274.5 21.3 %middle.6 = (f32[1,2,2,128,128]{4,3,2,1,0:T(8,128)}, f32[1,2,2,128,128]{4,3,2,1,0:T(8,128)}, f32[1,2,2,128,128]{4,3,2,1,0:T(8,128)}, f32[1,2,2,128,128]{4,3,2,1,...) custom-call(s32[1]{0:T(128)} %bitcast.1.me_ref.refs_1_, ...), custom_call_target="tpu_custom_call" | custom-call | flops 1000 | bytes 1000 | tf_op jit(solution)/shard_map/middle/pallas_call | solution.py:346
  301.1 20.7 %middle.7 = (f32[1,2,2,128,128]{4,3,2,1,0:T(8,128)}, f32[1,2,2,128,128]{4,3,2,1,0:T(8,128)}, f32[1,2,2,128,128]{4,3,2,1,0:T(8,128)}, f32[1,2,2,128,128]{4,3,2,1,...) custom-call(s32[1]{0:T(128)} %bitcast.1.me_ref.refs_1_, ...), custom_call_target="tpu_custom_call", output_to_operand_aliasing={{8}: (13, {}), {9}: (14, {}), {10}: (15, {}), {11}: (16, {}... | custom-call | flops 1000 | bytes 1000 | tf_op jit(solution)/shard_map/middle/pallas_call | solution.py:346
  337.4 6.0 %collective-permute-done.53.refs_13_ = f32[1,2,2,128,128]{4,3,2,1,0:T(8,128)S(1)} collective-permute-done((f32[1,2,2,128,128]{4,3,2,1,0:T(8,128)}, f32[1,2,2,128,128]{4,3,2,1,0:T(8,128)S(1)}, u32[]{:S(2)}, u32[]{:S(2)}) %collective-permute-start.53) | collective-permute-done | bytes 262176 | tf_op jit(solution)/shard_map/ppermute | solution.py:161
  346.6 7.5 %space.10.refs_15_.refs_14_ = f32[2,256,2048]{2,1,0:T(8,128)} custom-call(s32[4]{0:T(128)} %refs_0_.15, s32[1]{0:T(128)} %bitcast.1.me_ref.refs_1_, f32[1]{0:T(128)S(6)} %mul.47.refs_2_.refs_3_, f32[4,256,2048]{2,1,0:T(8,128)} %all-gather.2.cloned.1.call-done.refs_3_.refs_4_, f32[2,16,128]{2,1,0:T(8,128)} %constant.92.clone.refs_4_.refs_5_, ...), custom_call_target="tpu_custom_call" | custom-call | flops 1000 | bytes 1000 | tf_op jit(solution)/shard_map/space/pallas_call | solution.py:490
  357.1 8.6 %space.11 = (f32[2,256,2048]{2,1,0:T(8,128)}, f32[64,2048]{1,0:T(8,128)}, f32[64,2048]{1,0:T(8,128)}) custom-call(s32[4]{0:T(128)} %refs_0_.15, s32[1]{0:T(128)} %bitcast.1.me_ref.refs_1_, s32[1]{0:T(128)} %bitcast.bit_ref.refs_2_, f32[1]{0:T(128)S(6)} %mul.47.refs_2_.refs_3_, f32[4,256,2048]{2,1,0:T(8,128)} %all-gather.2.cloned.1.call-done.refs_3_.refs_4_, ...), custom_call_target="tpu_custom_call" | custom-call | flops 1000 | bytes 1000 | tf_op jit(solution)/shard_map/space/pallas_call | solution.py:490
  370.4 10.7 %collective-permute-done.64.refs_12_.refs_13_ = f32[2,2,2,128,128]{4,3,2,1,0:T(8,128)S(1)} collective-permute-done((f32[2,2,2,128,128]{4,3,2,1,0:T(8,128)S(1)}, f32[2,2,2,128,128]{4,3,2,1,0:T(8,128)S(1)}, u32[]{:S(2)}, u32[]{:S(2)}) %collective-permute-start.64) | collective-permute-done | bytes 524320 | tf_op jit(solution)/shard_map/ppermute | solution.py:161
  384.2 7.6 %collective-permute-done.63.refs_11_.refs_12_ = f32[2,2,2,128,128]{4,3,2,1,0:T(8,128)S(1)} collective-permute-done((f32[2,2,2,128,128]{4,3,2,1,0:T(8,128)}, f32[2,2,2,128,128]{4,3,2,1,0:T(8,128)S(1)}, u32[]{:S(2)}, u32[]{:S(2)}) %collective-permute-start.63) | collective-permute-done | bytes 524320 | tf_op jit(solution)/shard_map/ppermute | solution.py:161
  394.0 9.0 %collective-permute-done.62.refs_10_.refs_11_ = f32[2,2,2,128,128]{4,3,2,1,0:T(8,128)S(1)} collective-permute-done((f32[2,2,2,128,128]{4,3,2,1,0:T(8,128)}, f32[2,2,2,128,128]{4,3,2,1,0:T(8,128)S(1)}, u32[]{:S(2)}, u32[]{:S(2)}) %collective-permute-start.62) | collective-permute-done | bytes 524320 | tf_op jit(solution)/shard_map/ppermute | solution.py:161
  424.6 5.7 %space.15 = (f32[2,256,2048]{2,1,0:T(8,128)}, f32[32,2048]{1,0:T(8,128)}, f32[32,2048]{1,0:T(8,128)}) custom-call(s32[4]{0:T(128)} %refs_0_.15, s32[1]{0:T(128)} %bitcast.1.me_ref.refs_1_, s32[1]{0:T(128)} %bitcast.bit_ref.refs_2_, f32[1]{0:T(128)S(6)} %mul.47.refs_2_.refs_3_, ...), custom_call_target="tpu_custom_call", output_to_operand_aliasing={{0}: (16, {})} | custom-call | flops 1000 | bytes 1000 | tf_op jit(solution)/shard_map/space/pallas_call | solution.py:490
  433.9 12.2 %collective-permute-done.69 = f32[32,2048]{1,0:T(8,128)S(1)} collective-permute-done((f32[32,2048]{1,0:T(8,128)}, f32[32,2048]{1,0:T(8,128)S(1)}, u32[]{:S(2)}, u32[]{:S(2)}) %collective-permute-start.69) | collective-permute-done | bytes 262176 | tf_op jit(solution)/shard_map/ppermute | solution.py:161
  450.6 10.9 %collective-permute-done.70 = f32[32,2048]{1,0:T(8,128)S(1)} collective-permute-done((f32[32,2048]{1,0:T(8,128)S(1)}, f32[32,2048]{1,0:T(8,128)S(1)}, u32[]{:S(2)}, u32[]{:S(2)}) %collective-permute-start.70) | collective-permute-done | bytes 262176 | tf_op jit(solution)/shard_map/ppermute | solution.py:161
  461.8 8.0 %collective-permute-done.71.refs_5_ = f32[32,2048]{1,0:T(8,128)S(1)} collective-permute-done((f32[32,2048]{1,0:T(8,128)S(1)}, f32[32,2048]{1,0:T(8,128)S(1)}, u32[]{:S(2)}, u32[]{:S(2)}) %collective-permute-start.71) | collective-permute-done | bytes 262176 | tf_op jit(solution)/shard_map/ppermute | solution.py:161
  (257 shorter events, 119.5 us)
Async XLA Ops:
  7.2 177.3 %all-gather.2.cloned.1.call-start = ((), (), s32[]{:S(2)}) async-start(), calls=%async_computation | async-start | bytes 10485760 | tf_op jit(solution)/shard_map/all_gather | solution.py:592
  7.9 335.5 %all-reduce.2.cloned.1.call-start = ((), (), s32[]{:S(2)}) async-start(), calls=%async_computation.1 | async-start | bytes 4194304 | tf_op jit(solution)/shard_map/psum | solution.py:605
  18.9 34.6 %collective-permute-start.2 = (f32[2,2,256,128]{3,2,1,0:T(8,128)}, f32[2,2,256,128]{3,2,1,0:T(8,128)S(1)}, u32[]{:S(2)}, u32[]{:S(2)}) collective-permute-start(f32[2,2,256,128]{3,2,1,0:T(8,128)} %get-tuple-element.167), channel_id=1, source_target_pairs={{0,3},{1,2},{2,1},{3,0},{4,7},{5,6},{6,5},{7,4},{8,11},{9,10},{10,... | collective-permute-start | bytes 1572872 | tf_op jit(solution)/shard_map/ppermute | solution.py:161
  19.8 33.7 %collective-permute-start.3 = (f32[2,2,256,128]{3,2,1,0:T(8,128)}, f32[2,2,256,128]{3,2,1,0:T(8,128)S(1)}, u32[]{:S(2)}, u32[]{:S(2)}) collective-permute-start(f32[2,2,256,128]{3,2,1,0:T(8,128)} %get-tuple-element.168), channel_id=1, source_target_pairs={{0,4},{1,5},{2,6},{3,7},{4,0},{5,1},{6,2},{7,3},{8,12},{9,13},{10,... | collective-permute-start | bytes 1572872 | tf_op jit(solution)/shard_map/ppermute | solution.py:161
  20.3 33.5 %collective-permute-start.4 = (f32[2,2,256,128]{3,2,1,0:T(8,128)}, f32[2,2,256,128]{3,2,1,0:T(8,128)}, u32[]{:S(2)}, u32[]{:S(2)}) collective-permute-start(f32[2,2,256,128]{3,2,1,0:T(8,128)} %get-tuple-element.169), channel_id=1, source_target_pairs={{0,5},{1,4},{2,7},{3,6},{4,1},{5,0},{6,3},{7,2},{8,13},{9,12},{10,... | collective-permute-start | bytes 1572872 | tf_op jit(solution)/shard_map/ppermute | solution.py:161
  31.0 34.2 %collective-permute-start.5 = (f32[2,2,256,128]{3,2,1,0:T(8,128)}, f32[2,2,256,128]{3,2,1,0:T(8,128)}, u32[]{:S(2)}, u32[]{:S(2)}) collective-permute-start(f32[2,2,256,128]{3,2,1,0:T(8,128)} %get-tuple-element.170), channel_id=1, source_target_pairs={{0,6},{1,7},{2,4},{3,5},{4,2},{5,3},{6,0},{7,1},{8,14},{9,15},{10,... | collective-permute-start | bytes 1572872 | tf_op jit(solution)/shard_map/ppermute | solution.py:161
  43.1 32.9 %collective-permute-start.13 = (f32[2,2,256,128]{3,2,1,0:T(8,128)}, f32[2,2,256,128]{3,2,1,0:T(8,128)S(1)}, u32[]{:S(2)}, u32[]{:S(2)}) collective-permute-start(f32[2,2,256,128]{3,2,1,0:T(8,128)} %get-tuple-element.191), channel_id=1, source_target_pairs={{0,7},{1,6},{2,5},{3,4},{4,3},{5,2},{6,1},{7,0},{8,15},{9,14},{10,... | collective-permute-start | bytes 1572872 | tf_op jit(solution)/shard_map/ppermute | solution.py:161
  65.2 43.4 %collective-permute-start.12 = (f32[2,2,256,128]{3,2,1,0:T(8,128)}, f32[2,2,256,128]{3,2,1,0:T(8,128)S(1)}, u32[]{:S(2)}, u32[]{:S(2)}) collective-permute-start(f32[2,2,256,128]{3,2,1,0:T(8,128)} %get-tuple-element.189), channel_id=1, source_target_pairs={{0,6},{1,7},{2,4},{3,5},{4,2},{5,3},{6,0},{7,1},{8,14},{9,15},{10,... | collective-permute-start | bytes 1572872 | tf_op jit(solution)/shard_map/ppermute | solution.py:161
  68.1 41.6 %collective-permute-start.11 = (f32[2,2,256,128]{3,2,1,0:T(8,128)}, f32[2,2,256,128]{3,2,1,0:T(8,128)S(1)}, u32[]{:S(2)}, u32[]{:S(2)}) collective-permute-start(f32[2,2,256,128]{3,2,1,0:T(8,128)} %get-tuple-element.187), channel_id=1, source_target_pairs={{0,5},{1,4},{2,7},{3,6},{4,1},{5,0},{6,3},{7,2},{8,13},{9,12},{10,... | collective-permute-start | bytes 1572872 | tf_op jit(solution)/shard_map/ppermute | solution.py:161
  68.1 42.8 %collective-permute-start.10 = (f32[2,2,256,128]{3,2,1,0:T(8,128)}, f32[2,2,256,128]{3,2,1,0:T(8,128)S(1)}, u32[]{:S(2)}, u32[]{:S(2)}) collective-permute-start(f32[2,2,256,128]{3,2,1,0:T(8,128)} %get-tuple-element.185), channel_id=1, source_target_pairs={{0,4},{1,5},{2,6},{3,7},{4,0},{5,1},{6,2},{7,3},{8,12},{9,13},{10,... | collective-permute-start | bytes 1572872 | tf_op jit(solution)/shard_map/ppermute | solution.py:161
  68.6 43.7 %collective-permute-start.9 = (f32[2,2,256,128]{3,2,1,0:T(8,128)}, f32[2,2,256,128]{3,2,1,0:T(8,128)}, u32[]{:S(2)}, u32[]{:S(2)}) collective-permute-start(f32[2,2,256,128]{3,2,1,0:T(8,128)} %get-tuple-element.183), channel_id=1, source_target_pairs={{0,3},{1,2},{2,1},{3,0},{4,7},{5,6},{6,5},{7,4},{8,11},{9,10},{10,... | collective-permute-start | bytes 1572872 | tf_op jit(solution)/shard_map/ppermute | solution.py:161
  76.0 37.6 %collective-permute-start.8 = (f32[2,2,256,128]{3,2,1,0:T(8,128)}, f32[2,2,256,128]{3,2,1,0:T(8,128)}, u32[]{:S(2)}, u32[]{:S(2)}) collective-permute-start(f32[2,2,256,128]{3,2,1,0:T(8,128)} %get-tuple-element.181), channel_id=1, source_target_pairs={{0,2},{1,3},{2,0},{3,1},{4,6},{5,7},{6,4},{7,5},{8,10},{9,11},{10,... | collective-permute-start | bytes 1572872 | tf_op jit(solution)/shard_map/ppermute | solution.py:161
  112.4 44.9 %collective-permute-start.22 = (f32[2,2,256,128]{3,2,1,0:T(8,128)}, f32[2,2,256,128]{3,2,1,0:T(8,128)S(1)}, u32[]{:S(2)}, u32[]{:S(2)}) collective-permute-start(f32[2,2,256,128]{3,2,1,0:T(8,128)} %get-tuple-element.211), channel_id=1, source_target_pairs={{0,5},{1,4},{2,7},{3,6},{4,1},{5,0},{6,3},{7,2},{8,13},{9,12},{10,... | collective-permute-start | bytes 1572872 | tf_op jit(solution)/shard_map/ppermute | solution.py:161
  113.6 45.3 %collective-permute-start.20 = (f32[2,2,256,128]{3,2,1,0:T(8,128)}, f32[2,2,256,128]{3,2,1,0:T(8,128)S(1)}, u32[]{:S(2)}, u32[]{:S(2)}) collective-permute-start(f32[2,2,256,128]{3,2,1,0:T(8,128)} %get-tuple-element.207), channel_id=1, source_target_pairs={{0,4},{1,5},{2,6},{3,7},{4,0},{5,1},{6,2},{7,3},{8,12},{9,13},{10,... | collective-permute-start | bytes 1572872 | tf_op jit(solution)/shard_map/ppermute | solution.py:161
  114.1 46.2 %collective-permute-start.18 = (f32[2,2,256,128]{3,2,1,0:T(8,128)}, f32[2,2,256,128]{3,2,1,0:T(8,128)}, u32[]{:S(2)}, u32[]{:S(2)}) collective-permute-start(f32[2,2,256,128]{3,2,1,0:T(8,128)} %get-tuple-element.203), channel_id=1, source_target_pairs={{0,3},{1,2},{2,1},{3,0},{4,7},{5,6},{6,5},{7,4},{8,11},{9,10},{10,... | collective-permute-start | bytes 1572872 | tf_op jit(solution)/shard_map/ppermute | solution.py:161
  124.8 36.4 %collective-permute-start.16 = (f32[2,2,256,128]{3,2,1,0:T(8,128)}, f32[2,2,256,128]{3,2,1,0:T(8,128)}, u32[]{:S(2)}, u32[]{:S(2)}) collective-permute-start(f32[2,2,256,128]{3,2,1,0:T(8,128)} %get-tuple-element.199), channel_id=1, source_target_pairs={{0,2},{1,3},{2,0},{3,1},{4,6},{5,7},{6,4},{7,5},{8,10},{9,11},{10,... | collective-permute-start | bytes 1572872 | tf_op jit(solution)/shard_map/ppermute | solution.py:161
  160.3 39.0 %collective-permute-start.23 = (f32[2,2,256,128]{3,2,1,0:T(8,128)}, f32[2,2,256,128]{3,2,1,0:T(8,128)S(1)}, u32[]{:S(2)}, u32[]{:S(2)}) collective-permute-start(f32[2,2,256,128]{3,2,1,0:T(8,128)} %get-tuple-element.212), channel_id=1, source_target_pairs={{0,5},{1,4},{2,7},{3,6},{4,1},{5,0},{6,3},{7,2},{8,13},{9,12},{10,... | collective-permute-start | bytes 1572872 | tf_op jit(solution)/shard_map/ppermute | solution.py:161
  161.3 45.6 %collective-permute-start.21 = (f32[2,2,256,128]{3,2,1,0:T(8,128)}, f32[2,2,256,128]{3,2,1,0:T(8,128)S(1)}, u32[]{:S(2)}, u32[]{:S(2)}) collective-permute-start(f32[2,2,256,128]{3,2,1,0:T(8,128)} %get-tuple-element.208), channel_id=1, source_target_pairs={{0,4},{1,5},{2,6},{3,7},{4,0},{5,1},{6,2},{7,3},{8,12},{9,13},{10,... | collective-permute-start | bytes 1572872 | tf_op jit(solution)/shard_map/ppermute | solution.py:161
  161.8 46.5 %collective-permute-start.19 = (f32[2,2,256,128]{3,2,1,0:T(8,128)}, f32[2,2,256,128]{3,2,1,0:T(8,128)}, u32[]{:S(2)}, u32[]{:S(2)}) collective-permute-start(f32[2,2,256,128]{3,2,1,0:T(8,128)} %get-tuple-element.204), channel_id=1, source_target_pairs={{0,3},{1,2},{2,1},{3,0},{4,7},{5,6},{6,5},{7,4},{8,11},{9,10},{10,... | collective-permute-start | bytes 1572872 | tf_op jit(solution)/shard_map/ppermute | solution.py:161
  172.4 36.0 %collective-permute-start.17 = (f32[2,2,256,128]{3,2,1,0:T(8,128)}, f32[2,2,256,128]{3,2,1,0:T(8,128)}, u32[]{:S(2)}, u32[]{:S(2)}) collective-permute-start(f32[2,2,256,128]{3,2,1,0:T(8,128)} %get-tuple-element.200), channel_id=1, source_target_pairs={{0,2},{1,3},{2,0},{3,1},{4,6},{5,7},{6,4},{7,5},{8,10},{9,11},{10,... | collective-permute-start | bytes 1572872 | tf_op jit(solution)/shard_map/ppermute | solution.py:161
  199.3 27.2 %collective-permute-start.40 = (f32[2,2,256,128]{3,2,1,0:T(8,128)}, f32[2,2,256,128]{3,2,1,0:T(8,128)S(1)}, u32[]{:S(2)}, u32[]{:S(2)}) collective-permute-start(f32[2,2,256,128]{3,2,1,0:T(8,128)} %get-tuple-element.250), channel_id=1, source_target_pairs={{0,7},{1,6},{2,5},{3,4},{4,3},{5,2},{6,1},{7,0},{8,15},{9,14},{10,... | collective-permute-start | bytes 1572872 | tf_op jit(solution)/shard_map/ppermute | solution.py:161
  208.3 31.8 %collective-permute-start.36 = (f32[2,2,256,128]{3,2,1,0:T(8,128)}, f32[2,2,256,128]{3,2,1,0:T(8,128)S(1)}, u32[]{:S(2)}, u32[]{:S(2)}) collective-permute-start(f32[2,2,256,128]{3,2,1,0:T(8,128)} %get-tuple-element.242), channel_id=1, source_target_pairs={{0,5},{1,4},{2,7},{3,6},{4,1},{5,0},{6,3},{7,2},{8,13},{9,12},{10,... | collective-permute-start | bytes 1572872 | tf_op jit(solution)/shard_map/ppermute | solution.py:161
  208.4 43.4 %collective-permute-start.34 = (f32[2,2,256,128]{3,2,1,0:T(8,128)}, f32[2,2,256,128]{3,2,1,0:T(8,128)S(1)}, u32[]{:S(2)}, u32[]{:S(2)}) collective-permute-start(f32[2,2,256,128]{3,2,1,0:T(8,128)} %get-tuple-element.238), channel_id=1, source_target_pairs={{0,4},{1,5},{2,6},{3,7},{4,0},{5,1},{6,2},{7,3},{8,12},{9,13},{10,... | collective-permute-start | bytes 1572872 | tf_op jit(solution)/shard_map/ppermute | solution.py:161
  225.0 28.4 %collective-permute-start.32 = (f32[2,2,256,128]{3,2,1,0:T(8,128)}, f32[2,2,256,128]{3,2,1,0:T(8,128)S(1)}, u32[]{:S(2)}, u32[]{:S(2)}) collective-permute-start(f32[2,2,256,128]{3,2,1,0:T(8,128)} %get-tuple-element.234), channel_id=1, source_target_pairs={{0,3},{1,2},{2,1},{3,0},{4,7},{5,6},{6,5},{7,4},{8,11},{9,10},{10,... | collective-permute-start | bytes 1572872 | tf_op jit(solution)/shard_map/ppermute | solution.py:161
  253.3 42.4 %collective-permute-start.37 = (f32[2,2,256,128]{3,2,1,0:T(8,128)}, f32[2,2,256,128]{3,2,1,0:T(8,128)S(1)}, u32[]{:S(2)}, u32[]{:S(2)}) collective-permute-start(f32[2,2,256,128]{3,2,1,0:T(8,128)} %get-tuple-element.243), channel_id=1, source_target_pairs={{0,5},{1,4},{2,7},{3,6},{4,1},{5,0},{6,3},{7,2},{8,13},{9,12},{10,... | collective-permute-start | bytes 1572872 | tf_op jit(solution)/shard_map/ppermute | solution.py:161
  253.4 44.3 %collective-permute-start.35 = (f32[2,2,256,128]{3,2,1,0:T(8,128)}, f32[2,2,256,128]{3,2,1,0:T(8,128)}, u32[]{:S(2)}, u32[]{:S(2)}) collective-permute-start(f32[2,2,256,128]{3,2,1,0:T(8,128)} %get-tuple-element.239), channel_id=1, source_target_pairs={{0,4},{1,5},{2,6},{3,7},{4,0},{5,1},{6,2},{7,3},{8,12},{9,13},{10,... | collective-permute-start | bytes 1572872 | tf_op jit(solution)/shard_map/ppermute | solution.py:161
  254.9 43.8 %collective-permute-start.33 = (f32[2,2,256,128]{3,2,1,0:T(8,128)}, f32[2,2,256,128]{3,2,1,0:T(8,128)}, u32[]{:S(2)}, u32[]{:S(2)}) collective-permute-start(f32[2,2,256,128]{3,2,1,0:T(8,128)} %get-tuple-element.235), channel_id=1, source_target_pairs={{0,3},{1,2},{2,1},{3,0},{4,7},{5,6},{6,5},{7,4},{8,11},{9,10},{10,... | collective-permute-start | bytes 1572872 | tf_op jit(solution)/shard_map/ppermute | solution.py:161
  262.3 37.5 %collective-permute-start.31 = (f32[2,2,256,128]{3,2,1,0:T(8,128)}, f32[2,2,256,128]{3,2,1,0:T(8,128)}, u32[]{:S(2)}, u32[]{:S(2)}) collective-permute-start(f32[2,2,256,128]{3,2,1,0:T(8,128)} %get-tuple-element.231), channel_id=1, source_target_pairs={{0,2},{1,3},{2,0},{3,1},{4,6},{5,7},{6,4},{7,5},{8,10},{9,11},{10,... | collective-permute-start | bytes 1572872 | tf_op jit(solution)/shard_map/ppermute | solution.py:161
  326.3 27.8 %collective-permute-start.51 = (f32[1,2,2,128,128]{4,3,2,1,0:T(8,128)}, f32[1,2,2,128,128]{4,3,2,1,0:T(8,128)S(1)}, u32[]{:S(2)}, u32[]{:S(2)}) collective-permute-start(f32[1,2,2,128,128]{4,3,2,1,0:T(8,128)} %get-tuple-element.284), channel_id=1, source_target_pairs={{0,5},{1,4},{2,7},{3,6},{4,1},{5,0},{6,3},{7,2},{8,13},{9,12},{10,... | collective-permute-start | bytes 786440 | tf_op jit(solution)/shard_map/ppermute | solution.py:161
  367.0 35.9 %collective-permute-start.62 = (f32[2,2,2,128,128]{4,3,2,1,0:T(8,128)}, f32[2,2,2,128,128]{4,3,2,1,0:T(8,128)S(1)}, u32[]{:S(2)}, u32[]{:S(2)}) collective-permute-start(f32[2,2,2,128,128]{4,3,2,1,0:T(8,128)} %get-tuple-element.308), channel_id=1, source_target_pairs={{0,4},{1,5},{2,6},{3,7},{4,0},{5,1},{6,2},{7,3},{8,12},{9,13},{10,... | collective-permute-start | bytes 1572872 | tf_op jit(solution)/shard_map/ppermute | solution.py:161
  368.7 34.2 %collective-permute-start.61 = (f32[2,2,2,128,128]{4,3,2,1,0:T(8,128)}, f32[2,2,2,128,128]{4,3,2,1,0:T(8,128)S(1)}, u32[]{:S(2)}, u32[]{:S(2)}) collective-permute-start(f32[2,2,2,128,128]{4,3,2,1,0:T(8,128)} %get-tuple-element.306), channel_id=1, source_target_pairs={{0,3},{1,2},{2,1},{3,0},{4,7},{5,6},{6,5},{7,4},{8,11},{9,10},{10,... | collective-permute-start | bytes 1572872 | tf_op jit(solution)/shard_map/ppermute | solution.py:161
  419.4 27.7 %collective-permute-start.58 = (f32[64,2048]{1,0:T(8,128)S(1)}, f32[64,2048]{1,0:T(8,128)S(1)}, u32[]{:S(2)}, u32[]{:S(2)}) collective-permute-start(f32[64,2048]{1,0:T(8,128)S(1)} %add.53.refs_0_), channel_id=1, source_target_pairs={{0,8},{8,0},{16,24},{24,16},{1,9},{9,1},{17,25},{25,17},{2,10},{10... | collective-permute-start | bytes 1572872 | tf_op jit(solution)/shard_map/ppermute | solution.py:161
  (98 other events, 1853.6 us)
Sparse Core Ops, SparseCore 0:
  9.6 152.3 all-gather.1
  225.1 86.8 all-reduce.1

commit v5 on v4

--- a/solution.py
+++ b/solution.py
@@ -390,11 +390,16 @@
         (held,) = refs
     rows = held.shape[1]
 
-    for k in range(shards):
-        block = ins[k][0] if len(ins[k].shape) == 5 else ins[k][...]
-        wide = [jnp.concatenate([block[j, 0], block[j, 1]], axis=1) for j in range(2)]
+    group = max(1, lanes // rows)
+    for first in range(0, shards, group):
+        wide = []
+        for k in range(first, first + group):
+            block = ins[k][0] if len(ins[k].shape) == 5 else ins[k][...]
+            wide += [jnp.concatenate([block[j, 0], block[j, 1]], axis=1) for j in range(2)]
         done = times_right(jnp.concatenate(wide, axis=0), itable_ref)
-        held[pl.ds((me ^ k) * 2, 2)] = done.reshape(2, rows, 2 * lanes)
+        for n in range(group):
+            part = done[2 * n * rows:2 * (n + 1) * rows]
+            held[pl.ds((me ^ (first + n)) * 2, 2)] = part.reshape(2, rows, 2 * lanes)
 
     def one(t, carry):
         at = pl.ds(pl.multiple_of(t * sub, sub), sub)

time: 481 us -> 481 us (level)
  no operation moved by 1% of the time
where the time goes in v5:
time: 481 us; the launch traced here: 480 us
  waiting for transfers between devices  204 us (42%)
  Pallas kernels  169 us (35%)
  starting transfers between devices  74.5 us (15%)
  between operations  15.4 us (3%)
  other arithmetic  15.1 us (3%)
    ppermute x72, waiting for transfers between devices, swap(): return lax.ppermute(array, axis, [(d, d ^ mask) for d in range(size)])  203 us
    pallas_call x4, Pallas kernels, middle(): pl.pallas_call(functools.partial(middle_kernel, sign, tuple((size for siz...  83.2 us
    ppermute x72, starting transfers between devices, swap(): return lax.ppermute(array, axis, [(d, d ^ mask) for d in range(size)])  74.4 us
    pallas_call x8, Pallas kernels, space(): pl.pallas_call(functools.partial(space_kernel, sign, onward, keep, image,...  67 us
    pallas_call x2, Pallas kernels, forward_last(): pl.pallas_call(forward_last_kernel, grid=(rows // chunk,), in_specs=[smem...  12.8 us
    mul x1, other arithmetic, multiplier(): damping * jnp.sin(depth_step * travel)  10.8 us
  transfers between devices with their start and end apart: 74, of which 28 were waited for; matrix products, arithmetic and copies ran while one was open for 3% of the time, Pallas kernels for 35%

profile of v5, /device:TPU:0, one launch (start us, length us, event | category | flops | bytes accessed | tf_op | source)
XLA Modules:
  0.0 480.4 jit_solution(6076268138729470283)
XLA Ops:
  7.9 6.4 %forward_last.2 = (f32[2,2,256,128]{3,2,1,0:T(8,128)}, f32[2,2,256,128]{3,2,1,0:T(8,128)}, f32[2,2,256,128]{3,2,1,0:T(8,128)}, f32[2,2,256,128]{3,2,1,0:T(8,128)...) custom-call(s32[1]{0:T(128)} %bitcast.1.me_ref.refs_1_, ...), custom_call_target="tpu_custom_call" | custom-call | flops 1000 | bytes 1000 | tf_op jit(solution)/shard_map/forward_last/pallas_call | solution.py:224
  21.9 9.1 %collective-permute-done.6.rest_7_ = f32[2,2,256,128]{3,2,1,0:T(8,128)S(1)} collective-permute-done((f32[2,2,256,128]{3,2,1,0:T(8,128)}, f32[2,2,256,128]{3,2,1,0:T(8,128)S(1)}, u32[]{:S(2)}, u32[]{:S(2)}) %collective-permute-start.6) | collective-permute-done | bytes 524320 | tf_op jit(solution)/shard_map/ppermute | solution.py:161
  33.2 6.4 %forward_last.3 = (f32[2,2,256,128]{3,2,1,0:T(8,128)}, f32[2,2,256,128]{3,2,1,0:T(8,128)}, f32[2,2,256,128]{3,2,1,0:T(8,128)}, f32[2,2,256,128]{3,2,1,0:T(8,128)...) custom-call(s32[1]{0:T(128)} %bitcast.1.me_ref.refs_1_, ...), custom_call_target="tpu_custom_call" | custom-call | flops 1000 | bytes 1000 | tf_op jit(solution)/shard_map/forward_last/pallas_call | solution.py:224
  44.0 9.5 %collective-permute-done.2.rest_3_ = f32[2,2,256,128]{3,2,1,0:T(8,128)S(1)} collective-permute-done((f32[2,2,256,128]{3,2,1,0:T(8,128)}, f32[2,2,256,128]{3,2,1,0:T(8,128)S(1)}, u32[]{:S(2)}, u32[]{:S(2)}) %collective-permute-start.2) | collective-permute-done | bytes 524320 | tf_op jit(solution)/shard_map/ppermute | solution.py:161
  53.8 11.4 %collective-permute-done.5.rest_6_ = f32[2,2,256,128]{3,2,1,0:T(8,128)} collective-permute-done((f32[2,2,256,128]{3,2,1,0:T(8,128)}, f32[2,2,256,128]{3,2,1,0:T(8,128)}, u32[]{:S(2)}, u32[]{:S(2)}) %collective-permute-start.5) | collective-permute-done | bytes 524320 | tf_op jit(solution)/shard_map/ppermute | solution.py:161
  70.1 5.9 %collective-permute-done.13.rest_7_ = f32[2,2,256,128]{3,2,1,0:T(8,128)S(1)} collective-permute-done((f32[2,2,256,128]{3,2,1,0:T(8,128)}, f32[2,2,256,128]{3,2,1,0:T(8,128)S(1)}, u32[]{:S(2)}, u32[]{:S(2)}) %collective-permute-start.13) | collective-permute-done | bytes 524320 | tf_op jit(solution)/shard_map/ppermute | solution.py:161
  77.2 10.8 %sine_multiply_fusion = (f32[16,128,256]{2,1,0:T(8,128)}, f32[16,128,256]{2,1,0:T(8,128)}) fusion(s32[256]{0:T(256)S(1)} %get-tuple-element.328, s32[256]{0:T(256)S(1)} %get-tuple-element.331, pred[256]{0:T(512)(128)(4,1)S(1)} %get-tuple-element.329, s32[256]{0:T(256)S(1)} %get-tuple-element.327, s32[256]{0:T(256)S(1)} %get-tuple-element.332, ...), kind=kLoop, calls=%fused_computation.10 | loop fusion | flops 14680064 | bytes 4199432 | tf_op jit(solution)/shard_map/mul | solution.py:575
  88.0 20.6 %middle.4 = (f32[2,2,256,128]{3,2,1,0:T(8,128)}, f32[2,2,256,128]{3,2,1,0:T(8,128)}, f32[2,2,256,128]{3,2,1,0:T(8,128)}, f32[2,2,256,128]{3,2,1,0:T(8,128)}, f32...) custom-call(s32[1]{0:T(128)} %bitcast.1.me_ref.refs_1_, ...), custom_call_target="tpu_custom_call" | custom-call | flops 1000 | bytes 1000 | tf_op jit(solution)/shard_map/middle/pallas_call | solution.py:346
  114.4 10.5 %collective-permute-done.26.refs_13_ = f32[2,2,256,128]{3,2,1,0:T(8,128)S(1)} collective-permute-done((f32[2,2,256,128]{3,2,1,0:T(8,128)}, f32[2,2,256,128]{3,2,1,0:T(8,128)S(1)}, u32[]{:S(2)}, u32[]{:S(2)}) %collective-permute-start.26) | collective-permute-done | bytes 524320 | tf_op jit(solution)/shard_map/ppermute | solution.py:161
  125.2 11.4 %collective-permute-done.24.refs_12_ = f32[2,2,256,128]{3,2,1,0:T(8,128)S(1)} collective-permute-done((f32[2,2,256,128]{3,2,1,0:T(8,128)}, f32[2,2,256,128]{3,2,1,0:T(8,128)S(1)}, u32[]{:S(2)}, u32[]{:S(2)}) %collective-permute-start.24) | collective-permute-done | bytes 524320 | tf_op jit(solution)/shard_map/ppermute | solution.py:161
  136.6 20.7 %middle.5 = (f32[2,2,256,128]{3,2,1,0:T(8,128)}, f32[2,2,256,128]{3,2,1,0:T(8,128)}, f32[2,2,256,128]{3,2,1,0:T(8,128)}, f32[2,2,256,128]{3,2,1,0:T(8,128)}, f32...) custom-call(s32[1]{0:T(128)} %bitcast.1.me_ref.refs_1_, ...), custom_call_target="tpu_custom_call" | custom-call | flops 1000 | bytes 1000 | tf_op jit(solution)/shard_map/middle/pallas_call | solution.py:346
  163.2 9.2 %collective-permute-done.27.refs_13_ = f32[2,2,256,128]{3,2,1,0:T(8,128)S(1)} collective-permute-done((f32[2,2,256,128]{3,2,1,0:T(8,128)}, f32[2,2,256,128]{3,2,1,0:T(8,128)S(1)}, u32[]{:S(2)}, u32[]{:S(2)}) %collective-permute-start.27) | collective-permute-done | bytes 524320 | tf_op jit(solution)/shard_map/ppermute | solution.py:161
  172.9 11.5 %collective-permute-done.25.refs_12_ = f32[2,2,256,128]{3,2,1,0:T(8,128)S(1)} collective-permute-done((f32[2,2,256,128]{3,2,1,0:T(8,128)}, f32[2,2,256,128]{3,2,1,0:T(8,128)S(1)}, u32[]{:S(2)}, u32[]{:S(2)}) %collective-permute-start.25) | collective-permute-done | bytes 524320 | tf_op jit(solution)/shard_map/ppermute | solution.py:161
  184.5 14.8 %space.8 = (f32[2,256,2048]{2,1,0:T(8,128)}, f32[2,2,256,128]{3,2,1,0:T(8,128)}, f32[2,2,256,128]{3,2,1,0:T(8,128)}, f32[2,2,256,128]{3,2,1,0:T(8,128)}, f32[2,2...) custom-call(s32[4]{0:T(128)} %refs_0_.15, ...), custom_call_target="tpu_custom_call" | custom-call | flops 1000 | bytes 1000 | tf_op jit(solution)/shard_map/space/pallas_call | solution.py:495
  200.9 5.9 %collective-permute-done.21.refs_10_ = f32[2,2,256,128]{3,2,1,0:T(8,128)S(1)} collective-permute-done((f32[2,2,256,128]{3,2,1,0:T(8,128)}, f32[2,2,256,128]{3,2,1,0:T(8,128)S(1)}, u32[]{:S(2)}, u32[]{:S(2)}) %collective-permute-start.21) | collective-permute-done | bytes 524320 | tf_op jit(solution)/shard_map/ppermute | solution.py:161
  209.8 15.1 %space.9 = (f32[2,2,256,128]{3,2,1,0:T(8,128)}, f32[2,2,256,128]{3,2,1,0:T(8,128)}, f32[2,2,256,128]{3,2,1,0:T(8,128)}, f32[2,2,256,128]{3,2,1,0:T(8,128)}, f32[...) custom-call(s32[4]{0:T(128)} %refs_0_.15, ...), custom_call_target="tpu_custom_call" | custom-call | flops 1000 | bytes 1000 | tf_op jit(solution)/shard_map/space/pallas_call | solution.py:495
  229.4 10.7 %collective-permute-done.36.rest_5_ = f32[2,2,256,128]{3,2,1,0:T(8,128)S(1)} collective-permute-done((f32[2,2,256,128]{3,2,1,0:T(8,128)}, f32[2,2,256,128]{3,2,1,0:T(8,128)S(1)}, u32[]{:S(2)}, u32[]{:S(2)}) %collective-permute-start.36) | collective-permute-done | bytes 524320 | tf_op jit(solution)/shard_map/ppermute | solution.py:161
  241.5 10.3 %collective-permute-done.34.rest_4_ = f32[2,2,256,128]{3,2,1,0:T(8,128)S(1)} collective-permute-done((f32[2,2,256,128]{3,2,1,0:T(8,128)}, f32[2,2,256,128]{3,2,1,0:T(8,128)S(1)}, u32[]{:S(2)}, u32[]{:S(2)}) %collective-permute-start.34) | collective-permute-done | bytes 524320 | tf_op jit(solution)/shard_map/ppermute | solution.py:161
  256.3 6.1 %collective-permute-done.41.rest_7_ = f32[2,2,256,128]{3,2,1,0:T(8,128)S(1)} collective-permute-done((f32[2,2,256,128]{3,2,1,0:T(8,128)}, f32[2,2,256,128]{3,2,1,0:T(8,128)S(1)}, u32[]{:S(2)}, u32[]{:S(2)}) %collective-permute-start.41) | collective-permute-done | bytes 524320 | tf_op jit(solution)/shard_map/ppermute | solution.py:161
  263.2 11.2 %collective-permute-done.39.rest_6_ = f32[2,2,256,128]{3,2,1,0:T(8,128)S(1)} collective-permute-done((f32[2,2,256,128]{3,2,1,0:T(8,128)}, f32[2,2,256,128]{3,2,1,0:T(8,128)S(1)}, u32[]{:S(2)}, u32[]{:S(2)}) %collective-permute-start.39) | collective-permute-done | bytes 524320 | tf_op jit(solution)/shard_map/ppermute | solution.py:161
  274.5 21.3 %middle.6 = (f32[1,2,2,128,128]{4,3,2,1,0:T(8,128)}, f32[1,2,2,128,128]{4,3,2,1,0:T(8,128)}, f32[1,2,2,128,128]{4,3,2,1,0:T(8,128)}, f32[1,2,2,128,128]{4,3,2,1,...) custom-call(s32[1]{0:T(128)} %bitcast.1.me_ref.refs_1_, ...), custom_call_target="tpu_custom_call" | custom-call | flops 1000 | bytes 1000 | tf_op jit(solution)/shard_map/middle/pallas_call | solution.py:346
  301.1 20.7 %middle.7 = (f32[1,2,2,128,128]{4,3,2,1,0:T(8,128)}, f32[1,2,2,128,128]{4,3,2,1,0:T(8,128)}, f32[1,2,2,128,128]{4,3,2,1,0:T(8,128)}, f32[1,2,2,128,128]{4,3,2,1,...) custom-call(s32[1]{0:T(128)} %bitcast.1.me_ref.refs_1_, ...), custom_call_target="tpu_custom_call", output_to_operand_aliasing={{8}: (13, {}), {9}: (14, {}), {10}: (15, {}), {11}: (16, {}... | custom-call | flops 1000 | bytes 1000 | tf_op jit(solution)/shard_map/middle/pallas_call | solution.py:346
  337.4 6.0 %collective-permute-done.53.refs_13_ = f32[1,2,2,128,128]{4,3,2,1,0:T(8,128)S(1)} collective-permute-done((f32[1,2,2,128,128]{4,3,2,1,0:T(8,128)}, f32[1,2,2,128,128]{4,3,2,1,0:T(8,128)S(1)}, u32[]{:S(2)}, u32[]{:S(2)}) %collective-permute-start.53) | collective-permute-done | bytes 262176 | tf_op jit(solution)/shard_map/ppermute | solution.py:161
  346.6 7.5 %space.10.refs_15_.refs_14_ = f32[2,256,2048]{2,1,0:T(8,128)} custom-call(s32[4]{0:T(128)} %refs_0_.15, s32[1]{0:T(128)} %bitcast.1.me_ref.refs_1_, f32[1]{0:T(128)S(6)} %mul.47.refs_2_.refs_3_, f32[4,256,2048]{2,1,0:T(8,128)} %all-gather.2.cloned.1.call-done.refs_3_.refs_4_, f32[2,16,128]{2,1,0:T(8,128)} %constant.92.clone.refs_4_.refs_5_, ...), custom_call_target="tpu_custom_call" | custom-call | flops 1000 | bytes 1000 | tf_op jit(solution)/shard_map/space/pallas_call | solution.py:495
  357.1 8.6 %space.11 = (f32[2,256,2048]{2,1,0:T(8,128)}, f32[64,2048]{1,0:T(8,128)}, f32[64,2048]{1,0:T(8,128)}) custom-call(s32[4]{0:T(128)} %refs_0_.15, s32[1]{0:T(128)} %bitcast.1.me_ref.refs_1_, s32[1]{0:T(128)} %bitcast.bit_ref.refs_2_, f32[1]{0:T(128)S(6)} %mul.47.refs_2_.refs_3_, f32[4,256,2048]{2,1,0:T(8,128)} %all-gather.2.cloned.1.call-done.refs_3_.refs_4_, ...), custom_call_target="tpu_custom_call" | custom-call | flops 1000 | bytes 1000 | tf_op jit(solution)/shard_map/space/pallas_call | solution.py:495
  370.4 10.7 %collective-permute-done.64.refs_12_.refs_13_ = f32[2,2,2,128,128]{4,3,2,1,0:T(8,128)S(1)} collective-permute-done((f32[2,2,2,128,128]{4,3,2,1,0:T(8,128)S(1)}, f32[2,2,2,128,128]{4,3,2,1,0:T(8,128)S(1)}, u32[]{:S(2)}, u32[]{:S(2)}) %collective-permute-start.64) | collective-permute-done | bytes 524320 | tf_op jit(solution)/shard_map/ppermute | solution.py:161
  384.2 7.6 %collective-permute-done.63.refs_11_.refs_12_ = f32[2,2,2,128,128]{4,3,2,1,0:T(8,128)S(1)} collective-permute-done((f32[2,2,2,128,128]{4,3,2,1,0:T(8,128)}, f32[2,2,2,128,128]{4,3,2,1,0:T(8,128)S(1)}, u32[]{:S(2)}, u32[]{:S(2)}) %collective-permute-start.63) | collective-permute-done | bytes 524320 | tf_op jit(solution)/shard_map/ppermute | solution.py:161
  394.0 9.0 %collective-permute-done.62.refs_10_.refs_11_ = f32[2,2,2,128,128]{4,3,2,1,0:T(8,128)S(1)} collective-permute-done((f32[2,2,2,128,128]{4,3,2,1,0:T(8,128)}, f32[2,2,2,128,128]{4,3,2,1,0:T(8,128)S(1)}, u32[]{:S(2)}, u32[]{:S(2)}) %collective-permute-start.62) | collective-permute-done | bytes 524320 | tf_op jit(solution)/shard_map/ppermute | solution.py:161
  424.6 5.7 %space.15 = (f32[2,256,2048]{2,1,0:T(8,128)}, f32[32,2048]{1,0:T(8,128)}, f32[32,2048]{1,0:T(8,128)}) custom-call(s32[4]{0:T(128)} %refs_0_.15, s32[1]{0:T(128)} %bitcast.1.me_ref.refs_1_, s32[1]{0:T(128)} %bitcast.bit_ref.refs_2_, f32[1]{0:T(128)S(6)} %mul.47.refs_2_.refs_3_, ...), custom_call_target="tpu_custom_call", output_to_operand_aliasing={{0}: (16, {})} | custom-call | flops 1000 | bytes 1000 | tf_op jit(solution)/shard_map/space/pallas_call | solution.py:495
  433.9 12.2 %collective-permute-done.69 = f32[32,2048]{1,0:T(8,128)S(1)} collective-permute-done((f32[32,2048]{1,0:T(8,128)}, f32[32,2048]{1,0:T(8,128)S(1)}, u32[]{:S(2)}, u32[]{:S(2)}) %collective-permute-start.69) | collective-permute-done | bytes 262176 | tf_op jit(solution)/shard_map/ppermute | solution.py:161
  450.7 10.9 %collective-permute-done.70 = f32[32,2048]{1,0:T(8,128)S(1)} collective-permute-done((f32[32,2048]{1,0:T(8,128)S(1)}, f32[32,2048]{1,0:T(8,128)S(1)}, u32[]{:S(2)}, u32[]{:S(2)}) %collective-permute-start.70) | collective-permute-done | bytes 262176 | tf_op jit(solution)/shard_map/ppermute | solution.py:161
  461.8 8.0 %collective-permute-done.71.refs_5_ = f32[32,2048]{1,0:T(8,128)S(1)} collective-permute-done((f32[32,2048]{1,0:T(8,128)S(1)}, f32[32,2048]{1,0:T(8,128)S(1)}, u32[]{:S(2)}, u32[]{:S(2)}) %collective-permute-start.71) | collective-permute-done | bytes 262176 | tf_op jit(solution)/shard_map/ppermute | solution.py:161
  (257 shorter events, 119.6 us)
Async XLA Ops:
  7.2 177.3 %all-gather.2.cloned.1.call-start = ((), (), s32[]{:S(2)}) async-start(), calls=%async_computation | async-start | bytes 10485760 | tf_op jit(solution)/shard_map/all_gather | solution.py:597
  7.9 335.5 %all-reduce.2.cloned.1.call-start = ((), (), s32[]{:S(2)}) async-start(), calls=%async_computation.1 | async-start | bytes 4194304 | tf_op jit(solution)/shard_map/psum | solution.py:610
  18.9 34.6 %collective-permute-start.2 = (f32[2,2,256,128]{3,2,1,0:T(8,128)}, f32[2,2,256,128]{3,2,1,0:T(8,128)S(1)}, u32[]{:S(2)}, u32[]{:S(2)}) collective-permute-start(f32[2,2,256,128]{3,2,1,0:T(8,128)} %get-tuple-element.167), channel_id=1, source_target_pairs={{0,3},{1,2},{2,1},{3,0},{4,7},{5,6},{6,5},{7,4},{8,11},{9,10},{10,... | collective-permute-start | bytes 1572872 | tf_op jit(solution)/shard_map/ppermute | solution.py:161
  19.8 33.7 %collective-permute-start.3 = (f32[2,2,256,128]{3,2,1,0:T(8,128)}, f32[2,2,256,128]{3,2,1,0:T(8,128)S(1)}, u32[]{:S(2)}, u32[]{:S(2)}) collective-permute-start(f32[2,2,256,128]{3,2,1,0:T(8,128)} %get-tuple-element.168), channel_id=1, source_target_pairs={{0,4},{1,5},{2,6},{3,7},{4,0},{5,1},{6,2},{7,3},{8,12},{9,13},{10,... | collective-permute-start | bytes 1572872 | tf_op jit(solution)/shard_map/ppermute | solution.py:161
  20.3 33.5 %collective-permute-start.4 = (f32[2,2,256,128]{3,2,1,0:T(8,128)}, f32[2,2,256,128]{3,2,1,0:T(8,128)}, u32[]{:S(2)}, u32[]{:S(2)}) collective-permute-start(f32[2,2,256,128]{3,2,1,0:T(8,128)} %get-tuple-element.169), channel_id=1, source_target_pairs={{0,5},{1,4},{2,7},{3,6},{4,1},{5,0},{6,3},{7,2},{8,13},{9,12},{10,... | collective-permute-start | bytes 1572872 | tf_op jit(solution)/shard_map/ppermute | solution.py:161
  31.0 34.2 %collective-permute-start.5 = (f32[2,2,256,128]{3,2,1,0:T(8,128)}, f32[2,2,256,128]{3,2,1,0:T(8,128)}, u32[]{:S(2)}, u32[]{:S(2)}) collective-permute-start(f32[2,2,256,128]{3,2,1,0:T(8,128)} %get-tuple-element.170), channel_id=1, source_target_pairs={{0,6},{1,7},{2,4},{3,5},{4,2},{5,3},{6,0},{7,1},{8,14},{9,15},{10,... | collective-permute-start | bytes 1572872 | tf_op jit(solution)/shard_map/ppermute | solution.py:161
  43.1 32.9 %collective-permute-start.13 = (f32[2,2,256,128]{3,2,1,0:T(8,128)}, f32[2,2,256,128]{3,2,1,0:T(8,128)S(1)}, u32[]{:S(2)}, u32[]{:S(2)}) collective-permute-start(f32[2,2,256,128]{3,2,1,0:T(8,128)} %get-tuple-element.191), channel_id=1, source_target_pairs={{0,7},{1,6},{2,5},{3,4},{4,3},{5,2},{6,1},{7,0},{8,15},{9,14},{10,... | collective-permute-start | bytes 1572872 | tf_op jit(solution)/shard_map/ppermute | solution.py:161
  65.2 43.4 %collective-permute-start.12 = (f32[2,2,256,128]{3,2,1,0:T(8,128)}, f32[2,2,256,128]{3,2,1,0:T(8,128)S(1)}, u32[]{:S(2)}, u32[]{:S(2)}) collective-permute-start(f32[2,2,256,128]{3,2,1,0:T(8,128)} %get-tuple-element.189), channel_id=1, source_target_pairs={{0,6},{1,7},{2,4},{3,5},{4,2},{5,3},{6,0},{7,1},{8,14},{9,15},{10,... | collective-permute-start | bytes 1572872 | tf_op jit(solution)/shard_map/ppermute | solution.py:161
  68.1 41.6 %collective-permute-start.11 = (f32[2,2,256,128]{3,2,1,0:T(8,128)}, f32[2,2,256,128]{3,2,1,0:T(8,128)S(1)}, u32[]{:S(2)}, u32[]{:S(2)}) collective-permute-start(f32[2,2,256,128]{3,2,1,0:T(8,128)} %get-tuple-element.187), channel_id=1, source_target_pairs={{0,5},{1,4},{2,7},{3,6},{4,1},{5,0},{6,3},{7,2},{8,13},{9,12},{10,... | collective-permute-start | bytes 1572872 | tf_op jit(solution)/shard_map/ppermute | solution.py:161
  68.1 42.8 %collective-permute-start.10 = (f32[2,2,256,128]{3,2,1,0:T(8,128)}, f32[2,2,256,128]{3,2,1,0:T(8,128)S(1)}, u32[]{:S(2)}, u32[]{:S(2)}) collective-permute-start(f32[2,2,256,128]{3,2,1,0:T(8,128)} %get-tuple-element.185), channel_id=1, source_target_pairs={{0,4},{1,5},{2,6},{3,7},{4,0},{5,1},{6,2},{7,3},{8,12},{9,13},{10,... | collective-permute-start | bytes 1572872 | tf_op jit(solution)/shard_map/ppermute | solution.py:161
  68.6 43.7 %collective-permute-start.9 = (f32[2,2,256,128]{3,2,1,0:T(8,128)}, f32[2,2,256,128]{3,2,1,0:T(8,128)}, u32[]{:S(2)}, u32[]{:S(2)}) collective-permute-start(f32[2,2,256,128]{3,2,1,0:T(8,128)} %get-tuple-element.183), channel_id=1, source_target_pairs={{0,3},{1,2},{2,1},{3,0},{4,7},{5,6},{6,5},{7,4},{8,11},{9,10},{10,... | collective-permute-start | bytes 1572872 | tf_op jit(solution)/shard_map/ppermute | solution.py:161
  76.0 37.6 %collective-permute-start.8 = (f32[2,2,256,128]{3,2,1,0:T(8,128)}, f32[2,2,256,128]{3,2,1,0:T(8,128)}, u32[]{:S(2)}, u32[]{:S(2)}) collective-permute-start(f32[2,2,256,128]{3,2,1,0:T(8,128)} %get-tuple-element.181), channel_id=1, source_target_pairs={{0,2},{1,3},{2,0},{3,1},{4,6},{5,7},{6,4},{7,5},{8,10},{9,11},{10,... | collective-permute-start | bytes 1572872 | tf_op jit(solution)/shard_map/ppermute | solution.py:161
  112.4 44.9 %collective-permute-start.22 = (f32[2,2,256,128]{3,2,1,0:T(8,128)}, f32[2,2,256,128]{3,2,1,0:T(8,128)S(1)}, u32[]{:S(2)}, u32[]{:S(2)}) collective-permute-start(f32[2,2,256,128]{3,2,1,0:T(8,128)} %get-tuple-element.211), channel_id=1, source_target_pairs={{0,5},{1,4},{2,7},{3,6},{4,1},{5,0},{6,3},{7,2},{8,13},{9,12},{10,... | collective-permute-start | bytes 1572872 | tf_op jit(solution)/shard_map/ppermute | solution.py:161
  113.6 45.3 %collective-permute-start.20 = (f32[2,2,256,128]{3,2,1,0:T(8,128)}, f32[2,2,256,128]{3,2,1,0:T(8,128)S(1)}, u32[]{:S(2)}, u32[]{:S(2)}) collective-permute-start(f32[2,2,256,128]{3,2,1,0:T(8,128)} %get-tuple-element.207), channel_id=1, source_target_pairs={{0,4},{1,5},{2,6},{3,7},{4,0},{5,1},{6,2},{7,3},{8,12},{9,13},{10,... | collective-permute-start | bytes 1572872 | tf_op jit(solution)/shard_map/ppermute | solution.py:161
  114.1 46.2 %collective-permute-start.18 = (f32[2,2,256,128]{3,2,1,0:T(8,128)}, f32[2,2,256,128]{3,2,1,0:T(8,128)}, u32[]{:S(2)}, u32[]{:S(2)}) collective-permute-start(f32[2,2,256,128]{3,2,1,0:T(8,128)} %get-tuple-element.203), channel_id=1, source_target_pairs={{0,3},{1,2},{2,1},{3,0},{4,7},{5,6},{6,5},{7,4},{8,11},{9,10},{10,... | collective-permute-start | bytes 1572872 | tf_op jit(solution)/shard_map/ppermute | solution.py:161
  124.8 36.4 %collective-permute-start.16 = (f32[2,2,256,128]{3,2,1,0:T(8,128)}, f32[2,2,256,128]{3,2,1,0:T(8,128)}, u32[]{:S(2)}, u32[]{:S(2)}) collective-permute-start(f32[2,2,256,128]{3,2,1,0:T(8,128)} %get-tuple-element.199), channel_id=1, source_target_pairs={{0,2},{1,3},{2,0},{3,1},{4,6},{5,7},{6,4},{7,5},{8,10},{9,11},{10,... | collective-permute-start | bytes 1572872 | tf_op jit(solution)/shard_map/ppermute | solution.py:161
  160.3 39.0 %collective-permute-start.23 = (f32[2,2,256,128]{3,2,1,0:T(8,128)}, f32[2,2,256,128]{3,2,1,0:T(8,128)S(1)}, u32[]{:S(2)}, u32[]{:S(2)}) collective-permute-start(f32[2,2,256,128]{3,2,1,0:T(8,128)} %get-tuple-element.212), channel_id=1, source_target_pairs={{0,5},{1,4},{2,7},{3,6},{4,1},{5,0},{6,3},{7,2},{8,13},{9,12},{10,... | collective-permute-start | bytes 1572872 | tf_op jit(solution)/shard_map/ppermute | solution.py:161
  161.3 45.6 %collective-permute-start.21 = (f32[2,2,256,128]{3,2,1,0:T(8,128)}, f32[2,2,256,128]{3,2,1,0:T(8,128)S(1)}, u32[]{:S(2)}, u32[]{:S(2)}) collective-permute-start(f32[2,2,256,128]{3,2,1,0:T(8,128)} %get-tuple-element.208), channel_id=1, source_target_pairs={{0,4},{1,5},{2,6},{3,7},{4,0},{5,1},{6,2},{7,3},{8,12},{9,13},{10,... | collective-permute-start | bytes 1572872 | tf_op jit(solution)/shard_map/ppermute | solution.py:161
  161.8 46.5 %collective-permute-start.19 = (f32[2,2,256,128]{3,2,1,0:T(8,128)}, f32[2,2,256,128]{3,2,1,0:T(8,128)}, u32[]{:S(2)}, u32[]{:S(2)}) collective-permute-start(f32[2,2,256,128]{3,2,1,0:T(8,128)} %get-tuple-element.204), channel_id=1, source_target_pairs={{0,3},{1,2},{2,1},{3,0},{4,7},{5,6},{6,5},{7,4},{8,11},{9,10},{10,... | collective-permute-start | bytes 1572872 | tf_op jit(solution)/shard_map/ppermute | solution.py:161
  172.4 36.0 %collective-permute-start.17 = (f32[2,2,256,128]{3,2,1,0:T(8,128)}, f32[2,2,256,128]{3,2,1,0:T(8,128)}, u32[]{:S(2)}, u32[]{:S(2)}) collective-permute-start(f32[2,2,256,128]{3,2,1,0:T(8,128)} %get-tuple-element.200), channel_id=1, source_target_pairs={{0,2},{1,3},{2,0},{3,1},{4,6},{5,7},{6,4},{7,5},{8,10},{9,11},{10,... | collective-permute-start | bytes 1572872 | tf_op jit(solution)/shard_map/ppermute | solution.py:161
  199.3 27.2 %collective-permute-start.40 = (f32[2,2,256,128]{3,2,1,0:T(8,128)}, f32[2,2,256,128]{3,2,1,0:T(8,128)S(1)}, u32[]{:S(2)}, u32[]{:S(2)}) collective-permute-start(f32[2,2,256,128]{3,2,1,0:T(8,128)} %get-tuple-element.250), channel_id=1, source_target_pairs={{0,7},{1,6},{2,5},{3,4},{4,3},{5,2},{6,1},{7,0},{8,15},{9,14},{10,... | collective-permute-start | bytes 1572872 | tf_op jit(solution)/shard_map/ppermute | solution.py:161
  208.3 31.8 %collective-permute-start.36 = (f32[2,2,256,128]{3,2,1,0:T(8,128)}, f32[2,2,256,128]{3,2,1,0:T(8,128)S(1)}, u32[]{:S(2)}, u32[]{:S(2)}) collective-permute-start(f32[2,2,256,128]{3,2,1,0:T(8,128)} %get-tuple-element.242), channel_id=1, source_target_pairs={{0,5},{1,4},{2,7},{3,6},{4,1},{5,0},{6,3},{7,2},{8,13},{9,12},{10,... | collective-permute-start | bytes 1572872 | tf_op jit(solution)/shard_map/ppermute | solution.py:161
  208.4 43.4 %collective-permute-start.34 = (f32[2,2,256,128]{3,2,1,0:T(8,128)}, f32[2,2,256,128]{3,2,1,0:T(8,128)S(1)}, u32[]{:S(2)}, u32[]{:S(2)}) collective-permute-start(f32[2,2,256,128]{3,2,1,0:T(8,128)} %get-tuple-element.238), channel_id=1, source_target_pairs={{0,4},{1,5},{2,6},{3,7},{4,0},{5,1},{6,2},{7,3},{8,12},{9,13},{10,... | collective-permute-start | bytes 1572872 | tf_op jit(solution)/shard_map/ppermute | solution.py:161
  225.0 28.4 %collective-permute-start.32 = (f32[2,2,256,128]{3,2,1,0:T(8,128)}, f32[2,2,256,128]{3,2,1,0:T(8,128)S(1)}, u32[]{:S(2)}, u32[]{:S(2)}) collective-permute-start(f32[2,2,256,128]{3,2,1,0:T(8,128)} %get-tuple-element.234), channel_id=1, source_target_pairs={{0,3},{1,2},{2,1},{3,0},{4,7},{5,6},{6,5},{7,4},{8,11},{9,10},{10,... | collective-permute-start | bytes 1572872 | tf_op jit(solution)/shard_map/ppermute | solution.py:161
  253.3 42.4 %collective-permute-start.37 = (f32[2,2,256,128]{3,2,1,0:T(8,128)}, f32[2,2,256,128]{3,2,1,0:T(8,128)S(1)}, u32[]{:S(2)}, u32[]{:S(2)}) collective-permute-start(f32[2,2,256,128]{3,2,1,0:T(8,128)} %get-tuple-element.243), channel_id=1, source_target_pairs={{0,5},{1,4},{2,7},{3,6},{4,1},{5,0},{6,3},{7,2},{8,13},{9,12},{10,... | collective-permute-start | bytes 1572872 | tf_op jit(solution)/shard_map/ppermute | solution.py:161
  253.4 44.3 %collective-permute-start.35 = (f32[2,2,256,128]{3,2,1,0:T(8,128)}, f32[2,2,256,128]{3,2,1,0:T(8,128)}, u32[]{:S(2)}, u32[]{:S(2)}) collective-permute-start(f32[2,2,256,128]{3,2,1,0:T(8,128)} %get-tuple-element.239), channel_id=1, source_target_pairs={{0,4},{1,5},{2,6},{3,7},{4,0},{5,1},{6,2},{7,3},{8,12},{9,13},{10,... | collective-permute-start | bytes 1572872 | tf_op jit(solution)/shard_map/ppermute | solution.py:161
  254.9 43.8 %collective-permute-start.33 = (f32[2,2,256,128]{3,2,1,0:T(8,128)}, f32[2,2,256,128]{3,2,1,0:T(8,128)}, u32[]{:S(2)}, u32[]{:S(2)}) collective-permute-start(f32[2,2,256,128]{3,2,1,0:T(8,128)} %get-tuple-element.235), channel_id=1, source_target_pairs={{0,3},{1,2},{2,1},{3,0},{4,7},{5,6},{6,5},{7,4},{8,11},{9,10},{10,... | collective-permute-start | bytes 1572872 | tf_op jit(solution)/shard_map/ppermute | solution.py:161
  262.3 37.5 %collective-permute-start.31 = (f32[2,2,256,128]{3,2,1,0:T(8,128)}, f32[2,2,256,128]{3,2,1,0:T(8,128)}, u32[]{:S(2)}, u32[]{:S(2)}) collective-permute-start(f32[2,2,256,128]{3,2,1,0:T(8,128)} %get-tuple-element.231), channel_id=1, source_target_pairs={{0,2},{1,3},{2,0},{3,1},{4,6},{5,7},{6,4},{7,5},{8,10},{9,11},{10,... | collective-permute-start | bytes 1572872 | tf_op jit(solution)/shard_map/ppermute | solution.py:161
  326.3 27.8 %collective-permute-start.51 = (f32[1,2,2,128,128]{4,3,2,1,0:T(8,128)}, f32[1,2,2,128,128]{4,3,2,1,0:T(8,128)S(1)}, u32[]{:S(2)}, u32[]{:S(2)}) collective-permute-start(f32[1,2,2,128,128]{4,3,2,1,0:T(8,128)} %get-tuple-element.284), channel_id=1, source_target_pairs={{0,5},{1,4},{2,7},{3,6},{4,1},{5,0},{6,3},{7,2},{8,13},{9,12},{10,... | collective-permute-start | bytes 786440 | tf_op jit(solution)/shard_map/ppermute | solution.py:161
  367.0 35.9 %collective-permute-start.62 = (f32[2,2,2,128,128]{4,3,2,1,0:T(8,128)}, f32[2,2,2,128,128]{4,3,2,1,0:T(8,128)S(1)}, u32[]{:S(2)}, u32[]{:S(2)}) collective-permute-start(f32[2,2,2,128,128]{4,3,2,1,0:T(8,128)} %get-tuple-element.308), channel_id=1, source_target_pairs={{0,4},{1,5},{2,6},{3,7},{4,0},{5,1},{6,2},{7,3},{8,12},{9,13},{10,... | collective-permute-start | bytes 1572872 | tf_op jit(solution)/shard_map/ppermute | solution.py:161
  368.7 34.2 %collective-permute-start.61 = (f32[2,2,2,128,128]{4,3,2,1,0:T(8,128)}, f32[2,2,2,128,128]{4,3,2,1,0:T(8,128)S(1)}, u32[]{:S(2)}, u32[]{:S(2)}) collective-permute-start(f32[2,2,2,128,128]{4,3,2,1,0:T(8,128)} %get-tuple-element.306), channel_id=1, source_target_pairs={{0,3},{1,2},{2,1},{3,0},{4,7},{5,6},{6,5},{7,4},{8,11},{9,10},{10,... | collective-permute-start | bytes 1572872 | tf_op jit(solution)/shard_map/ppermute | solution.py:161
  419.4 27.7 %collective-permute-start.58 = (f32[64,2048]{1,0:T(8,128)S(1)}, f32[64,2048]{1,0:T(8,128)S(1)}, u32[]{:S(2)}, u32[]{:S(2)}) collective-permute-start(f32[64,2048]{1,0:T(8,128)S(1)} %add.53.refs_0_), channel_id=1, source_target_pairs={{0,8},{8,0},{16,24},{24,16},{1,9},{9,1},{17,25},{25,17},{2,10},{10... | collective-permute-start | bytes 1572872 | tf_op jit(solution)/shard_map/ppermute | solution.py:161
  (98 other events, 1853.7 us)
Sparse Core Ops, SparseCore 0:
  9.6 152.3 all-gather.1
  225.1 86.8 all-reduce.1
